TPU v7x, 256 devices: a whole 4x4x8 slice. The times are simulated.
256 devices in a mesh: dp: 16 (over y, x), expert: 16 (over z, core).
Axes of the slice: x: 4, y: 4, z: 8, core: 2. Of those that a mesh axis runs over, the one named last changes fastest.
Arguments:
- tokens: bfloat16 [512, 256, 1280], P(('dp', 'expert')), may hold values from -6 to 6, as said below
- router: float32 [1280, 128], replicated
- w_gate: bfloat16 [128, 2560, 1280], P('expert', 'dp'), may hold values from -0.15625 to 0.15625
- w_up: bfloat16 [128, 2560, 1280], P('expert', 'dp'), may hold values from -0.15625 to 0.15625
- w_down: bfloat16 [128, 2560, 1280], P('expert', 'dp'), may hold values from -0.125 to 0.125
Outputs:
- mixed: bfloat16 [512, 256, 1280], P(('dp', 'expert'))
Inputs may be any that keep to these rules, and one draw needn't show every extreme that they name: `tokens`: token activations lie in this range.
All inputs are finite; a program needn't handle non-finite values.
Results may differ from a plain program's by a relative error of at most 0.03.
Values may be sent and summed in bfloat16 or wider, within the bound.
No kernel may reach another device: no remote copies, remote signals or barrier semaphores. Data moves between devices by JAX's collectives and lax.ppermute only.
A program may use at most 128 MiB of HBM per device.

v0:
```python
import jax
import jax.numpy as jnp
from jax import lax
from jax.sharding import PartitionSpec as P


def run_experts(rows, w_gate, w_up, w_down):
    gate = jnp.einsum("ehd,red->ehr", w_gate, rows, preferred_element_type=jnp.float32)
    up = jnp.einsum("ehd,red->ehr", w_up, rows, preferred_element_type=jnp.float32)
    act = (jax.nn.silu(gate) * up).astype(jnp.bfloat16)
    return jnp.einsum("ehr,ehd->red", act, w_down, preferred_element_type=jnp.float32)


def body(tokens, router, w_gate, w_up, w_down):
    logits = jnp.einsum(
        "imd,de->ime", tokens.astype(jnp.float32), router, precision=lax.Precision.HIGHEST
    )
    dispatch = jax.nn.softmax(logits, axis=1).astype(jnp.bfloat16)
    combine = jax.nn.softmax(logits, axis=2).astype(jnp.bfloat16)
    slots = jnp.einsum("ime,imd->ied", dispatch, tokens, preferred_element_type=jnp.float32).astype(
        jnp.bfloat16
    )
    owned = lax.all_to_all(slots, "expert", split_axis=1, concat_axis=0, tiled=True)
    partial_value = run_experts(
        lax.all_gather(owned, "dp", axis=0, tiled=True), w_gate, w_up, w_down
    )
    summed = lax.psum_scatter(
        partial_value.astype(jnp.bfloat16), "dp", scatter_dimension=0, tiled=True
    )
    expert_out = lax.all_to_all(summed, "expert", split_axis=0, concat_axis=1, tiled=True)
    mixed = jnp.einsum("ime,ied->imd", combine, expert_out, preferred_element_type=jnp.float32)
    return mixed.astype(jnp.bfloat16)


def solution(mesh):
    return jax.shard_map(
        body,
        mesh=mesh,
        in_specs=(
            P(("dp", "expert"), None, None),
            P(),
            P("expert", "dp", None),
            P("expert", "dp", None),
            P("expert", "dp", None),
        ),
        out_specs=P(("dp", "expert"), None, None),
        check_vma=False,
    )
```

profile of v0, /device:TPU:1, one launch (start us, length us, event | category | flops | bytes accessed | tf_op | source)
XLA Modules:
  0.0 287.3 jit_solution(12354241569821474360)
XLA Ops:
  6.5 0.0 copy-start
  6.5 0.0 all-gather.2.cloned.1.call-start
  6.5 2.8 fusion.13
  9.4 0.1 fusion.21
  9.5 2.6 convolution_convert_fusion.2
  12.1 1.8 copy.10
  13.8 30.0 %all_to_all.36 = bf16[2,128,1280]{2,0,1:T(2,128)(2,1)S(1)} all-to-all(bf16[2,128,1280]{2,0,1:T(2,128)(2,1)S(1)} %copy.10), channel_id=1, replica_groups=mesh['dp'=16,'expert'=16] {'expert'}, dimensions={1} | all-to-all | bytes 1310720 | tf_op jit(solution)/shard_map/all_to_all | solution.py:23
  43.8 1.3 copy.20
  45.2 2.7 all_to_all.29
  47.9 0.0 all-gather.2.cloned.1.call-update
  47.9 0.0 reduce-scatter.2.cloned.1.call-start
  48.0 82.1 %all-gather.2.cloned.1.call-done = bf16[512,8,1280]{2,0,1:T(8,128)(2,1)} async-done(((bf16[32,8,1280]{2,0,1:T(8,128)(2,1)}), bf16[512,8,1280]{2,0,1:T(8,128)(2,1)}) %all-gather.2.cloned.1.call-update) | async-done | bytes 10485776 | tf_op jit(solution)/shard_map/all_gather | solution.py:25
  130.1 10.0 %fusion.23 = f32[8,512,160]{1,2,0:T(8,128)} fusion(bf16[512,8,1280]{2,0,1:T(8,128)(2,1)} %all-gather.2.cloned.1.call-done, bf16[8,160,1280]{2,1,0:T(8,128)(2,1)} %param.7), kind=kOutput, calls=%fused_computation.32 | convolution fusion | flops 1677721600 | bytes 16384000 | tf_op jit(solution)/shard_map/ehd,red->ehr/dot_general | solution.py:8
  140.1 0.0 copy-done
  140.1 12.0 %fusion.2 = bf16[512,8,1280]{2,0,1:T(8,128)(2,1)} fusion(bf16[8,160,1280]{2,1,0:T(8,128)(2,1)S(1)} %copy-done, f32[8,512,160]{1,2,0:T(8,128)} %fusion.23, bf16[512,8,1280]{2,0,1:T(8,128)(2,1)} %all-gather.2.cloned.1.call-done, bf16[8,160,1280]{2,1,0:T(8,128)(2,1)} %param.8), kind=kOutput, calls=%fused_computation.3 | convolution fusion | flops 3364618240 | bytes 30146560 | tf_op jit(solution)/shard_map/ehr,ehd->red/dot_general | solution.py:11
  152.1 0.0 reduce-scatter.2.cloned.1.call-update
  152.2 93.9 %reduce-scatter.2.cloned.1.call-done = bf16[32,8,1280]{2,0,1:T(8,128)(2,1)} async-done(((bf16[512,8,1280]{2,0,1:T(8,128)(2,1)}), bf16[32,8,1280]{2,0,1:T(8,128)(2,1)}) %reduce-scatter.2.cloned.1.call-update) | async-done | bytes 655376 | tf_op jit(solution)/shard_map/reduce_scatter | solution.py:27
  246.1 2.3 copy.12
  248.4 8.6 %all-to-all-start.1 = ((bf16[32,8,1280]{2,1,0:T(8,128)(2,1)}), bf16[32,8,1280]{2,1,0:T(8,128)(2,1)}, u32[]{:S(2)}, u32[]{:S(2)}) async-start(bf16[32,8,1280]{2,1,0:T(8,128)(2,1)} %copy.12), calls=%async_computation.2 | async-start | bytes 1310720 | tf_op jit(solution)/shard_map/all_to_all | solution.py:30
  257.0 0.2 fusion.22
  257.2 19.9 %all-to-all-done.1 = bf16[32,8,1280]{2,1,0:T(8,128)(2,1)} async-done(((bf16[32,8,1280]{2,1,0:T(8,128)(2,1)}), bf16[32,8,1280]{2,1,0:T(8,128)(2,1)}, u32[]{:S(2)}, u32[]{:S(2)}) %all-to-all-start.1) | async-done | bytes 655392 | tf_op jit(solution)/shard_map/all_to_all | solution.py:30
  277.1 3.4 %convolution_convert_fusion.1 = bf16[2,256,1280]{2,1,0:T(8,128)(2,1)} fusion(bf16[16,2,8,1280]{3,2,1,0:T(8,128)(2,1)} %bitcast.6, f32[2,256]{1,0:T(2,128)S(1)} %fusion.22, f32[2,256,128]{2,1,0:T(8,128)S(1)} %fusion.13), kind=kOutput, calls=%fused_computation.4 | convolution fusion | flops 168624768 | bytes 2230272 | tf_op jit(solution)/shard_map/ime,ied->imd/dot_general | solution.py:31
Async XLA Ops:
  6.5 133.6 %copy-start = (bf16[8,160,1280]{2,1,0:T(8,128)(2,1)S(1)}, bf16[8,160,1280]{2,1,0:T(8,128)(2,1)}, u32[]{:S(2)}) copy-start(bf16[8,160,1280]{2,1,0:T(8,128)(2,1)} %param.9) | copy-start | bytes 9830404
  6.5 123.6 %all-gather.2.cloned.1.call-start = ((), (), s32[]{:S(2)}) async-start(), calls=%async_computation.3 | async-start | bytes 11141120 | tf_op jit(solution)/shard_map/all_gather | solution.py:25
  47.9 198.1 %reduce-scatter.2.cloned.1.call-start = ((), (), s32[]{:S(2)}) async-start(), calls=%async_computation.4 | async-start | bytes 11141120 | tf_op jit(solution)/shard_map/reduce_scatter | solution.py:27
  248.4 28.7 %all-to-all-start.1 = ((bf16[32,8,1280]{2,1,0:T(8,128)(2,1)}), bf16[32,8,1280]{2,1,0:T(8,128)(2,1)}, u32[]{:S(2)}, u32[]{:S(2)}) async-start(bf16[32,8,1280]{2,1,0:T(8,128)(2,1)} %copy.12), calls=%async_computation.2 | async-start | bytes 1310720 | tf_op jit(solution)/shard_map/all_to_all | solution.py:30
Sparse Core Ops, SparseCore 0:
  48.1 82.0 all-gather.1
  152.3 93.7 reduce-scatter.1
where the time goes:
time: 288 us; the launch traced here: 287 us
  waiting for transfers between devices  196 us (68%)
  matrix products  30.8 us (11%)
  blocking collectives  30 us (10%)
  between operations  13.4 us (5%)
  starting transfers between devices  8.64 us (3%)
  local copies, waits for them, and re-layouts  8.11 us (3%)
    reduce_scatter x1, waiting for transfers between devices, body(): lax.psum_scatter(partial_value.astype(jnp.bfloat16), 'dp', scatter_dimens...  93.9 us
    all_gather x1, waiting for transfers between devices, body(): lax.all_gather(owned, 'dp', axis=0, tiled=True)  82.1 us
    all_to_all x1, blocking collectives, body(): lax.all_to_all(slots, 'expert', split_axis=1, concat_axis=0, tiled=True)  30 us
    all_to_all x1, waiting for transfers between devices, body(): lax.all_to_all(summed, 'expert', split_axis=0, concat_axis=1, tiled=True)  19.9 us
    dot_general x1, matrix products, run_experts(): jnp.einsum('ehr,ehd->red', act, w_down, preferred_element_type=jnp.float32)  12 us
    dot_general x1, matrix products, run_experts(): jnp.einsum('ehd,red->ehr', w_gate, rows, preferred_element_type=jnp.float32)  9.98 us
    all_to_all x1, starting transfers between devices, body(): lax.all_to_all(summed, 'expert', split_axis=0, concat_axis=1, tiled=True)  8.6 us
  transfers between devices with their start and end apart: 3, of which 3 were waited for; matrix products, arithmetic and copies ran while one was open for 0% of the time, Pallas kernels for 0%

commit v1 on v0

v1 whole, which is shorter than its diff:
```python
import functools

import jax
import jax.numpy as jnp
from jax import lax
from jax.experimental import pallas as pl
from jax.experimental.pallas import tpu as pltpu
from jax.sharding import PartitionSpec as P

D = 1280
EXPERTS = 128
TOK = 256
HS = 160
NDEV = 256
AXES = ("dp", "expert")
F32 = jnp.float32
BF16 = jnp.bfloat16


def place():
    dp = lax.axis_index("dp")
    core = lax.axis_index("expert") & 1
    y, x = dp >> 2, dp & 3
    p = jnp.where(core == 0, x, y)
    q = jnp.where(core == 0, y, x)
    return p, q


def shift_pairs(along_p, by):
    pairs = []
    for y in range(4):
        for x in range(4):
            for e in range(16):
                move_x = (e % 2 == 0) == along_p
                ny, nx = (y, (x + by) % 4) if move_x else ((y + by) % 4, x)
                pairs.append(((y * 4 + x) * 16 + e, (ny * 4 + nx) * 16 + e))
    return pairs


def shift(value, along_p, by):
    return lax.ppermute(value, AXES, shift_pairs(along_p, by))


def row_select(image):
    shape = (EXPERTS, NDEV)
    row = lax.broadcasted_iota(jnp.int32, shape, 1)
    e = lax.broadcasted_iota(jnp.int32, shape, 0)
    y, x, z, core = row >> 6, (row >> 4) & 3, (row >> 1) & 7, row & 1
    p = jnp.where(core == 0, x, y)
    q = jnp.where(core == 0, y, x)
    chosen = z * 16 + core * 8 + p * 2 + (q & 1)
    return jnp.where((chosen == e) & ((q >> 1) == image), 1.0, 0.0).astype(BF16)


def front_kernel(tok_ref, router_ref, rows_ref, comb_ref):
    r = router_ref[...]
    r0 = r.astype(BF16)
    rest = r - r0.astype(F32)
    r1 = rest.astype(BF16)
    r2 = (rest - r1.astype(F32)).astype(BF16)
    rows = jnp.zeros((NDEV, D), F32)
    for i in range(2):
        tok = tok_ref[i]
        logits = (
            jnp.dot(tok, r2, preferred_element_type=F32)
            + jnp.dot(tok, r1, preferred_element_type=F32)
            + jnp.dot(tok, r0, preferred_element_type=F32)
        )
        select = row_select(i)
        ex = jnp.exp(logits - jnp.max(logits, axis=0, keepdims=True))
        disp = (ex / jnp.sum(ex, axis=0, keepdims=True)).astype(BF16)
        ec = jnp.exp(logits - jnp.max(logits, axis=1, keepdims=True))
        comb = (ec / jnp.sum(ec, axis=1, keepdims=True)).astype(BF16)
        disp_rows = jnp.dot(disp, select, preferred_element_type=F32)
        comb_ref[i] = jnp.dot(comb, select, preferred_element_type=F32).astype(BF16)
        rows = rows + jnp.dot(
            jnp.transpose(disp_rows).astype(BF16), tok, preferred_element_type=F32
        )
    rows_ref[...] = rows.astype(BF16)


def front(tokens, router):
    return pl.pallas_call(
        front_kernel,
        out_shape=(
            jax.ShapeDtypeStruct((NDEV, D), BF16),
            jax.ShapeDtypeStruct((2, TOK, NDEV), BF16),
        ),
        in_specs=[pl.BlockSpec(memory_space=pltpu.VMEM)] * 2,
        out_specs=(pl.BlockSpec(memory_space=pltpu.VMEM),) * 2,
        compiler_params=pltpu.CompilerParams(vmem_limit_bytes=40 * 2**20),
        cost_estimate=pl.CostEstimate(flops=900_000_000, bytes_accessed=3_000_000, transcendentals=131072),
    )(tokens, router)


def experts_kernel(
    s0, s2, s1, s3, wg, wu, wd, w1, w2, w3, o0, o2, o1, o3,
    s_buf, gu_buf, wd_buf, o_buf, s_sem, g_sem, u_sem, d_sem, o_sem,
):
    p, q = place()
    odd = q & 1
    slots = (s0, s2, s1, s3)
    outs = (o0, o2, o1, o3)
    moved = (w1, w2, w3)
    copies = []
    for j in range(2):
        pick = odd if j == 0 else 1 - odd
        own = 2 * p + pick
        group = []
        for b in (2 * j, 2 * j + 1):
            group.append(pltpu.make_async_copy(slots[b], s_buf.at[b], s_sem.at[b]))
        for k in range(4):
            if k == 0:
                g, u, d = wg.at[own], wu.at[own], wd.at[own]
            else:
                g, u, d = (moved[k - 1].at[t, pick] for t in range(3))
            lo = pl.ds(k * HS, HS)
            hi = pl.ds(4 * HS + k * HS, HS)
            group.append(pltpu.make_async_copy(g, gu_buf.at[j, lo], g_sem.at[j, k]))
            group.append(pltpu.make_async_copy(u, gu_buf.at[j, hi], u_sem.at[j, k]))
            group.append(pltpu.make_async_copy(d, wd_buf.at[j, lo], d_sem.at[j, k]))
        for c in group:
            c.start()
        copies.append(group)
    out_copies = []
    for j in range(2):
        for c in copies[j]:
            c.wait()

        def block(b, carry, j=j):
            gu = lax.dot_general(
                s_buf[b], gu_buf[j], (((1,), (1,)), ((), ())), preferred_element_type=F32
            )
            gate, up = gu[:, : 4 * HS], gu[:, 4 * HS :]
            act = (gate / (1.0 + jnp.exp(-gate)) * up).astype(BF16)
            o_buf[b] = jnp.dot(act, wd_buf[j], preferred_element_type=F32).astype(BF16)
            return carry

        lax.fori_loop(2 * j, 2 * j + 2, block, 0)
        for b in (2 * j, 2 * j + 1):
            c = pltpu.make_async_copy(o_buf.at[b], outs[b], o_sem.at[b])
            c.start()
            out_copies.append(c)
    for c in out_copies:
        c.wait()


def experts(s0, s2, s1, s3, wg, wu, wd, w1, w2, w3):
    block = jax.ShapeDtypeStruct((NDEV, D), BF16)
    return pl.pallas_call(
        experts_kernel,
        out_shape=(block,) * 4,
        in_specs=[pl.BlockSpec(memory_space=pl.ANY)] * 10,
        out_specs=(pl.BlockSpec(memory_space=pl.ANY),) * 4,
        scratch_shapes=[
            pltpu.VMEM((4, NDEV, D), BF16),
            pltpu.VMEM((2, 8 * HS, D), BF16),
            pltpu.VMEM((2, 4 * HS, D), BF16),
            pltpu.VMEM((4, NDEV, D), BF16),
            pltpu.SemaphoreType.DMA((4,)),
            pltpu.SemaphoreType.DMA((2, 4)),
            pltpu.SemaphoreType.DMA((2, 4)),
            pltpu.SemaphoreType.DMA((2, 4)),
            pltpu.SemaphoreType.DMA((4,)),
        ],
        compiler_params=pltpu.CompilerParams(vmem_limit_bytes=44 * 2**20),
        cost_estimate=pl.CostEstimate(flops=5_100_000_000, bytes_accessed=15_000_000, transcendentals=1310720),
    )(s0, s2, s1, s3, wg, wu, wd, w1, w2, w3)


def body(tokens, router, w_gate, w_up, w_down):
    p, _ = place()

    def moved(by):
        first = 2 * ((p + by) & 3)
        parts = [lax.dynamic_slice_in_dim(w, first, 2, 0) for w in (w_gate, w_up, w_down)]
        return shift(jnp.stack(parts), True, by)

    w1, w3, w2 = moved(1), moved(3), moved(2)
    rows, comb = front(tokens, router)
    s0 = lax.all_to_all(rows, AXES, split_axis=0, concat_axis=0, tiled=True)
    s1, s3, s2 = (shift(s0, False, by) for by in (1, 3, 2))
    o0, o2, o1, o3 = experts(s0, s2, s1, s3, w_gate, w_up, w_down, w1, w2, w3)
    t1, t3, t2 = shift(o1, False, 3), shift(o3, False, 1), shift(o2, False, 2)
    total = o0.astype(F32) + t1.astype(F32) + t2.astype(F32) + t3.astype(F32)
    out_rows = lax.all_to_all(
        total.astype(BF16), AXES, split_axis=0, concat_axis=0, tiled=True
    )
    mixed = jnp.dot(comb.reshape(2 * TOK, NDEV), out_rows, preferred_element_type=F32)
    return mixed.astype(BF16).reshape(2, TOK, D)


def solution(mesh):
    return jax.shard_map(
        body,
        mesh=mesh,
        in_specs=(
            P(("dp", "expert"), None, None),
            P(),
            P("expert", "dp", None),
            P("expert", "dp", None),
            P("expert", "dp", None),
        ),
        out_specs=P(("dp", "expert"), None, None),
        check_vma=False,
    )
```

time: 288 us -> 178 us (0.62)
  waiting for transfers between devices: 196 us -> 75.6 us
  matrix products: 30.8 us -> 1.57 us
  starting transfers between devices: 8.64 us -> 27.8 us
  Pallas kernels: 0 us -> 13.3 us
  between operations: 13.4 us -> 0.1 us
  other arithmetic: 0.35 us -> 8.18 us
  local copies, waits for them, and re-layouts: 8.11 us -> 15.8 us
  blocking collectives: 30 us -> 35.4 us
    reduce_scatter x1 -> x0, waiting for transfers between devices: 93.9 us -> none  [body(): lax.psum_scatter(partial_value.astype(jnp.bfloat16), 'dp', scatter_dimens...]
    all_gather x1 -> x0, waiting for transfers between devices: 82.1 us -> none  [body(): lax.all_gather(owned, 'dp', axis=0, tiled=True)]
    ppermute x0 -> x9, waiting for transfers between devices: none -> 65.3 us  [shift(): return lax.ppermute(value, AXES, shift_pairs(along_p, by))]
    dot_general x5 -> x1, matrix products: 30.8 us -> 1.57 us  [body(): jnp.dot(comb.reshape(2 * TOK, NDEV), out_rows, preferred_element_type=F32)]
    pallas_call x0 -> x2, Pallas kernels: none -> 13.3 us  [the longest x1 10.9 us: experts(): pl.pallas_call(experts_kernel, out_shape=(block,) * 4, in_specs=[pl.Block...]
    unnamed x2 -> x13, local copies, waits for them, and re-layouts: 0.01 us -> 13 us
    ppermute x0 -> x9, starting transfers between devices: none -> 11.3 us  [shift(): return lax.ppermute(value, AXES, shift_pairs(along_p, by))]
    all_to_all x1, waiting for transfers between devices: 19.9 us -> 10.3 us  [body(): s0 = lax.all_to_all(rows, AXES, split_axis=0, concat_axis=0, tiled=True)]
  transfers between devices with their start and end apart: 3 -> 10, of which waited for: 3 -> 6; matrix products, arithmetic and copies ran while one was open for 0% -> 8% of each run, Pallas kernels for 0% -> 0%
where the time goes in v1:
time: 178 us
  waiting for transfers between devices  75.6 us (42%)
  blocking collectives  35.4 us (20%)
  starting transfers between devices  27.8 us (16%)
  local copies, waits for them, and re-layouts  15.8 us (9%)
  Pallas kernels  13.3 us (7%)
  other arithmetic  8.18 us (5%)
    ppermute x9, waiting for transfers between devices, shift(): return lax.ppermute(value, AXES, shift_pairs(along_p, by))  65.3 us
    all_to_all x1, blocking collectives, body(): lax.all_to_all(total.astype(BF16), AXES, split_axis=0, concat_axis=0, til...  35.4 us
    all_to_all x1, starting transfers between devices, body(): s0 = lax.all_to_all(rows, AXES, split_axis=0, concat_axis=0, tiled=True)  16.5 us
    unnamed x13, local copies, waits for them, and re-layouts  13 us
    ppermute x9, starting transfers between devices, shift(): return lax.ppermute(value, AXES, shift_pairs(along_p, by))  11.3 us
    pallas_call x1, Pallas kernels, experts(): pl.pallas_call(experts_kernel, out_shape=(block,) * 4, in_specs=[pl.Block...  10.9 us
    all_to_all x1, waiting for transfers between devices, body(): s0 = lax.all_to_all(rows, AXES, split_axis=0, concat_axis=0, tiled=True)  10.3 us
    another operation x3, other arithmetic, moved(): return shift(jnp.stack(parts), True, by)  5.16 us
  transfers between devices with their start and end apart: 10, of which 6 were waited for; matrix products, arithmetic and copies ran while one was open for 8% of the time, Pallas kernels for 0%

profile of v1, /device:TPU:1, one launch (start us, length us, event | category | flops | bytes accessed | tf_op | source)
XLA Modules:
  0.0 177.7 jit_solution(8938657144517497612)
XLA Ops:
  0.0 1.3 copy-done
  2.4 2.4 %shard_map.55 = (bf16[256,1280]{1,0:T(8,128)(2,1)S(1)}, bf16[2,256,256]{2,1,0:T(8,128)(2,1)S(1)}) custom-call(bf16[2,256,1280]{2,1,0:T(8,128)(2,1)S(1)} %copy-done, f32[1280,128]{1,0:T(8,128)S(1)} %copy-done.1), custom_call_target="tpu_custom_call" | custom-call | flops 900000000 | bytes 3000000 | tf_op jit(solution)/shard_map/pallas_call | solution.py:83
  5.3 1.7 reduce
  7.0 2.7 %reshape.12 = bf16[256,2,640]{2,1,0:T(2,128)(2,1)} reshape(bf16[256,1280]{1,0:T(8,128)(2,1)} %reduce) | data formatting | bytes 1310720
  9.7 16.5 %all-to-all-start = ((bf16[256,2,640]{2,1,0:T(2,128)(2,1)}), bf16[256,2,640]{2,1,0:T(2,128)(2,1)}, u32[]{:S(2)}, u32[]{:S(2)}) async-start(bf16[256,2,640]{2,1,0:T(2,128)(2,1)} %reshape.12), calls=%async_computation | async-start | bytes 1310720 | tf_op jit(solution)/shard_map/all_to_all | solution.py:181
  26.3 2.0 %dynamic-slice_bitcast_fusion.2 = (bf16[1,2,160,1280]{3,2,1,0:T(8,128)(2,1)S(1)}, bf16[1,2,160,1280]{3,2,1,0:T(8,128)(2,1)S(1)}, bf16[1,2,160,1280]{3,2,1,0:T(8,128)(2,1)S(1)}) fusion(bf16[8,160,1280]{2,1,0:T(8,128)(2,1)} %wg.1, s32[]{:T(128)S(6)} %select_n.22, s32[]{:T(128)S(6)} %select_n.21, s32[]{:T(128)S(6)} %select_n.20), kind=kLoop, calls=%fused_computation.7 | loop fusion | bytes 4915212 | tf_op jit(solution)/shard_map/stack | solution.py:177
  29.3 1.7 pad_maximum_fusion
  31.0 1.4 collective-permute-start.3
  32.4 1.7 pad_maximum_fusion.1
  34.2 2.4 %collective-permute-start.4 = (bf16[3,2,160,1280]{3,2,1,0:T(8,128)(2,1)}, bf16[3,2,160,1280]{3,2,1,0:T(8,128)(2,1)}, u32[]{:S(2)}, u32[]{:S(2)}) collective-permute-start(bf16[3,2,160,1280]{3,2,1,0:T(8,128)(2,1)} %pad_maximum_fusion.1), channel_id=1, source_target_pairs={{0,32},{1,129},{2,34},{3,131},{4,36},{5,133},{6,38},{7,135},{8,40}... | collective-permute-start | bytes 7372808 | tf_op jit(solution)/shard_map/ppermute | solution.py:41
  36.6 1.7 pad_maximum_fusion.2
  39.4 10.3 %all-to-all-done = bf16[256,2,640]{2,1,0:T(2,128)(2,1)} async-done(((bf16[256,2,640]{2,1,0:T(2,128)(2,1)}), bf16[256,2,640]{2,1,0:T(2,128)(2,1)}, u32[]{:S(2)}, u32[]{:S(2)}) %all-to-all-start) | async-done | bytes 655392 | tf_op jit(solution)/shard_map/all_to_all | solution.py:181
  49.7 5.1 %reshape.13 = bf16[256,1,1280]{2,1,0:T(2,128)(2,1)} reshape(bf16[256,2,640]{2,1,0:T(2,128)(2,1)} %all-to-all-done) | data formatting | bytes 1310720
  54.8 1.4 copy.17
  56.5 1.2 collective-permute-start.1
  57.7 23.3 %collective-permute-done.2.s3 = bf16[256,1280]{1,0:T(8,128)(2,1)S(1)} collective-permute-done((bf16[256,1280]{1,0:T(8,128)(2,1)S(1)}, bf16[256,1280]{1,0:T(8,128)(2,1)S(1)}, u32[]{:S(2)}, u32[]{:S(2)}) %collective-permute-start.2) | collective-permute-done | bytes 655392 | tf_op jit(solution)/shard_map/ppermute | solution.py:41
  81.0 1.6 collective-permute-start
  82.6 24.6 %collective-permute-done.1.s1 = bf16[256,1280]{1,0:T(8,128)(2,1)S(1)} collective-permute-done((bf16[256,1280]{1,0:T(8,128)(2,1)S(1)}, bf16[256,1280]{1,0:T(8,128)(2,1)S(1)}, u32[]{:S(2)}, u32[]{:S(2)}) %collective-permute-start.1) | collective-permute-done | bytes 655392 | tf_op jit(solution)/shard_map/ppermute | solution.py:41
  107.4 10.9 %shard_map.56 = (bf16[256,1280]{1,0:T(8,128)(2,1)S(1)}, bf16[256,1280]{1,0:T(8,128)(2,1)S(1)}, bf16[256,1280]{1,0:T(8,128)(2,1)S(1)}, bf16[256,1280]{1,0:T(8,128)(2,1)S(1)}) custom-call(bf16[256,1280]{1,0:T(8,128)(2,1)S(1)} %bitcast.33, bf16[256,1280]{1,0:T(8,128)(2,1)S(1)} %collective-permute-done.s2, bf16[256,1280]{1,0:T(8,128)(2,1)S(1)} %collective-permute-done.1.s1, ...), custom_call_target="tpu_custom_call" | custom-call | flops 5100000256 | bytes 15000000 | tf_op jit(solution)/shard_map/pallas_call | solution.py:150
  118.3 2.1 %collective-permute-start.6 = (bf16[256,1280]{1,0:T(8,128)(2,1)S(1)}, bf16[256,1280]{1,0:T(8,128)(2,1)S(1)}, u32[]{:S(2)}, u32[]{:S(2)}) collective-permute-start(bf16[256,1280]{1,0:T(8,128)(2,1)S(1)} %get-tuple-element.14), channel_id=1, source_target_pairs={{0,192},{1,49},{2,194},{3,51},{4,196},{5,53},{6,198},{7,55},{8,200... | collective-permute-start | bytes 1966088 | tf_op jit(solution)/shard_map/ppermute | solution.py:41
  121.4 13.5 %collective-permute-done.6 = bf16[256,1280]{1,0:T(8,128)(2,1)S(1)} collective-permute-done((bf16[256,1280]{1,0:T(8,128)(2,1)S(1)}, bf16[256,1280]{1,0:T(8,128)(2,1)S(1)}, u32[]{:S(2)}, u32[]{:S(2)}) %collective-permute-start.6) | collective-permute-done | bytes 655392 | tf_op jit(solution)/shard_map/ppermute | solution.py:41
  135.0 3.7 %collective-permute-done.8 = bf16[256,1280]{1,0:T(8,128)(2,1)S(1)} collective-permute-done((bf16[256,1280]{1,0:T(8,128)(2,1)S(1)}, bf16[256,1280]{1,0:T(8,128)(2,1)S(1)}, u32[]{:S(2)}, u32[]{:S(2)}) %collective-permute-start.8) | collective-permute-done | bytes 655392 | tf_op jit(solution)/shard_map/ppermute | solution.py:41
  140.2 35.4 %all_to_all.23 = bf16[256,2,640]{2,1,0:T(2,128)(2,1)S(1)} all-to-all(bf16[256,2,640]{2,1,0:T(2,128)(2,1)S(1)} %reshape.14), channel_id=1, replica_groups=mesh['dp'=16,'expert'=16] {'dp','expert'}, dimensions={0} | all-to-all | bytes 1310720 | tf_op jit(solution)/shard_map/all_to_all | solution.py:186
  176.1 1.6 convolution_convert_fusion
  (22 shorter events, 7.3 us)
Async XLA Ops:
  0.0 1.3 copy-start
  1.3 1.1 copy-start.1
  7.0 21.3 %copy-start.3 = (bf16[8,160,1280]{2,1,0:T(8,128)(2,1)S(1)}, bf16[8,160,1280]{2,1,0:T(8,128)(2,1)}, u32[]{:S(2)}) copy-start(bf16[8,160,1280]{2,1,0:T(8,128)(2,1)} %wd.1) | copy-start | bytes 9830404
  9.7 40.0 %all-to-all-start = ((bf16[256,2,640]{2,1,0:T(2,128)(2,1)}), bf16[256,2,640]{2,1,0:T(2,128)(2,1)}, u32[]{:S(2)}, u32[]{:S(2)}) async-start(bf16[256,2,640]{2,1,0:T(2,128)(2,1)} %reshape.12), calls=%async_computation | async-start | bytes 1310720 | tf_op jit(solution)/shard_map/all_to_all | solution.py:181
  26.3 2.7 %copy-start.2 = (bf16[8,160,1280]{2,1,0:T(8,128)(2,1)S(1)}, bf16[8,160,1280]{2,1,0:T(8,128)(2,1)}, u32[]{:S(2)}) copy-start(bf16[8,160,1280]{2,1,0:T(8,128)(2,1)} %wu.1) | copy-start | bytes 9830404
  31.0 76.3 %collective-permute-start.3 = (bf16[3,2,160,1280]{3,2,1,0:T(8,128)(2,1)}, bf16[3,2,160,1280]{3,2,1,0:T(8,128)(2,1)S(1)}, u32[]{:S(2)}, u32[]{:S(2)}) collective-permute-start(bf16[3,2,160,1280]{3,2,1,0:T(8,128)(2,1)} %pad_maximum_fusion), channel_id=1, source_target_pairs={{0,16},{1,65},{2,18},{3,67},{4,20},{5,69},{6,22},{7,71},{8,24},{9,... | collective-permute-start | bytes 7372808 | tf_op jit(solution)/shard_map/ppermute | solution.py:41
  34.2 73.1 %collective-permute-start.4 = (bf16[3,2,160,1280]{3,2,1,0:T(8,128)(2,1)}, bf16[3,2,160,1280]{3,2,1,0:T(8,128)(2,1)}, u32[]{:S(2)}, u32[]{:S(2)}) collective-permute-start(bf16[3,2,160,1280]{3,2,1,0:T(8,128)(2,1)} %pad_maximum_fusion.1), channel_id=1, source_target_pairs={{0,32},{1,129},{2,34},{3,131},{4,36},{5,133},{6,38},{7,135},{8,40}... | collective-permute-start | bytes 7372808 | tf_op jit(solution)/shard_map/ppermute | solution.py:41
  38.3 69.1 %collective-permute-start.5 = (bf16[3,2,160,1280]{3,2,1,0:T(8,128)(2,1)}, bf16[3,2,160,1280]{3,2,1,0:T(8,128)(2,1)}, u32[]{:S(2)}, u32[]{:S(2)}) collective-permute-start(bf16[3,2,160,1280]{3,2,1,0:T(8,128)(2,1)} %pad_maximum_fusion.2), channel_id=1, source_target_pairs={{0,48},{1,193},{2,50},{3,195},{4,52},{5,197},{6,54},{7,199},{8,56}... | collective-permute-start | bytes 7372808 | tf_op jit(solution)/shard_map/ppermute | solution.py:41
  56.2 24.8 %collective-permute-start.2 = (bf16[256,1280]{1,0:T(8,128)(2,1)S(1)}, bf16[256,1280]{1,0:T(8,128)(2,1)S(1)}, u32[]{:S(2)}, u32[]{:S(2)}) collective-permute-start(bf16[256,1280]{1,0:T(8,128)(2,1)S(1)} %bitcast.30), channel_id=1, source_target_pairs={{0,192},{1,49},{2,194},{3,51},{4,196},{5,53},{6,198},{7,55},{8,200... | collective-permute-start | bytes 1966088 | tf_op jit(solution)/shard_map/ppermute | solution.py:41
  56.5 50.7 %collective-permute-start.1 = (bf16[256,1280]{1,0:T(8,128)(2,1)S(1)}, bf16[256,1280]{1,0:T(8,128)(2,1)S(1)}, u32[]{:S(2)}, u32[]{:S(2)}) collective-permute-start(bf16[256,1280]{1,0:T(8,128)(2,1)S(1)} %bitcast.31), channel_id=1, source_target_pairs={{0,64},{1,17},{2,66},{3,19},{4,68},{5,21},{6,70},{7,23},{8,72},{9,... | collective-permute-start | bytes 1966088 | tf_op jit(solution)/shard_map/ppermute | solution.py:41
  81.0 26.3 %collective-permute-start = (bf16[256,1280]{1,0:T(8,128)(2,1)S(1)}, bf16[256,1280]{1,0:T(8,128)(2,1)S(1)}, u32[]{:S(2)}, u32[]{:S(2)}) collective-permute-start(bf16[256,1280]{1,0:T(8,128)(2,1)S(1)} %bitcast.32), channel_id=1, source_target_pairs={{0,128},{1,33},{2,130},{3,35},{4,132},{5,37},{6,134},{7,39},{8,136... | collective-permute-start | bytes 1966088 | tf_op jit(solution)/shard_map/ppermute | solution.py:41
  118.3 16.7 %collective-permute-start.6 = (bf16[256,1280]{1,0:T(8,128)(2,1)S(1)}, bf16[256,1280]{1,0:T(8,128)(2,1)S(1)}, u32[]{:S(2)}, u32[]{:S(2)}) collective-permute-start(bf16[256,1280]{1,0:T(8,128)(2,1)S(1)} %get-tuple-element.14), channel_id=1, source_target_pairs={{0,192},{1,49},{2,194},{3,51},{4,196},{5,53},{6,198},{7,55},{8,200... | collective-permute-start | bytes 1966088 | tf_op jit(solution)/shard_map/ppermute | solution.py:41
  120.4 14.6 %collective-permute-start.7 = (bf16[256,1280]{1,0:T(8,128)(2,1)S(1)}, bf16[256,1280]{1,0:T(8,128)(2,1)S(1)}, u32[]{:S(2)}, u32[]{:S(2)}) collective-permute-start(bf16[256,1280]{1,0:T(8,128)(2,1)S(1)} %get-tuple-element.15), channel_id=1, source_target_pairs={{0,128},{1,33},{2,130},{3,35},{4,132},{5,37},{6,134},{7,39},{8,136... | collective-permute-start | bytes 1966088 | tf_op jit(solution)/shard_map/ppermute | solution.py:41
  121.1 17.6 %collective-permute-start.8 = (bf16[256,1280]{1,0:T(8,128)(2,1)S(1)}, bf16[256,1280]{1,0:T(8,128)(2,1)S(1)}, u32[]{:S(2)}, u32[]{:S(2)}) collective-permute-start(bf16[256,1280]{1,0:T(8,128)(2,1)S(1)} %get-tuple-element.16), channel_id=1, source_target_pairs={{0,64},{1,17},{2,66},{3,19},{4,68},{5,21},{6,70},{7,23},{8,72},{9,... | collective-permute-start | bytes 1966088 | tf_op jit(solution)/shard_map/ppermute | solution.py:41

commit v2 on v1

v2 whole, which is shorter than its diff:
```python
import functools

import jax
import jax.numpy as jnp
from jax import lax
from jax.experimental import pallas as pl
from jax.experimental.pallas import tpu as pltpu
from jax.sharding import PartitionSpec as P

D = 1280
EXPERTS = 128
TOK = 256
HS = 160
ROWS = 256
AXES = ("dp", "expert")
F32 = jnp.float32
BF16 = jnp.bfloat16


def place():
    dp = lax.axis_index("dp")
    core = lax.axis_index("expert") & 1
    y, x = dp >> 2, dp & 3
    p = jnp.where(core == 0, x, y)
    q = jnp.where(core == 0, y, x)
    return p, q


def shift_pairs(along_p, by):
    pairs = []
    for y in range(4):
        for x in range(4):
            for e in range(16):
                move_x = (e % 2 == 0) == along_p
                ny, nx = (y, (x + by) % 4) if move_x else ((y + by) % 4, x)
                pairs.append(((y * 4 + x) * 16 + e, (ny * 4 + nx) * 16 + e))
    return pairs


def shift(value, along_p, by):
    return lax.ppermute(value, AXES, shift_pairs(along_p, by))


def row_select(image):
    shape = (EXPERTS, ROWS)
    row = lax.broadcasted_iota(jnp.int32, shape, 1)
    e = lax.broadcasted_iota(jnp.int32, shape, 0)
    y, x, z, core = row >> 6, (row >> 4) & 3, (row >> 1) & 7, row & 1
    p = jnp.where(core == 0, x, y)
    q = jnp.where(core == 0, y, x)
    chosen = z * 16 + core * 8 + p * 2 + (q & 1)
    return jnp.where((chosen == e) & ((q >> 1) == image), 1.0, 0.0).astype(BF16)


def front_kernel(tok_ref, router_ref, rows_ref, comb_ref):
    r = router_ref[...]
    r0 = r.astype(BF16)
    rest = r - r0.astype(F32)
    r1 = rest.astype(BF16)
    r2 = (rest - r1.astype(F32)).astype(BF16)
    rows = jnp.zeros((ROWS, D), F32)
    for i in range(2):
        tok = tok_ref[i]
        logits = (
            jnp.dot(tok, r2, preferred_element_type=F32)
            + jnp.dot(tok, r1, preferred_element_type=F32)
            + jnp.dot(tok, r0, preferred_element_type=F32)
        )
        select = row_select(i)
        ex = jnp.exp(logits - jnp.max(logits, axis=0, keepdims=True))
        disp = (ex / jnp.sum(ex, axis=0, keepdims=True)).astype(BF16)
        ec = jnp.exp(logits - jnp.max(logits, axis=1, keepdims=True))
        comb = (ec / jnp.sum(ec, axis=1, keepdims=True)).astype(BF16)
        disp_rows = jnp.dot(disp, select, preferred_element_type=F32)
        comb_ref[i] = jnp.dot(comb, select, preferred_element_type=F32).astype(BF16)
        rows = rows + jnp.dot(
            jnp.transpose(disp_rows).astype(BF16), tok, preferred_element_type=F32
        )
    rows_ref[...] = rows.astype(BF16)


def front(tokens, router):
    return pl.pallas_call(
        front_kernel,
        out_shape=(
            jax.ShapeDtypeStruct((ROWS, D), BF16),
            jax.ShapeDtypeStruct((2, TOK, ROWS), BF16),
        ),
        in_specs=[pl.BlockSpec(memory_space=pltpu.VMEM)] * 2,
        out_specs=(pl.BlockSpec(memory_space=pltpu.VMEM),) * 2,
        compiler_params=pltpu.CompilerParams(vmem_limit_bytes=20 * 2**20),
        cost_estimate=pl.CostEstimate(flops=900_000_000, bytes_accessed=3_000_000, transcendentals=131072),
    )(tokens, router)


def pack_kernel(plans, *refs):
    weights, outs, (buf, in_sem, out_sem) = refs[:3], refs[3 : 3 + len(plans)], refs[3 + len(plans) :]
    p, _ = place()
    loads, stores = [], []
    slot = 0
    for (by, which), out in zip(plans, outs):
        there = pl.ds(2 * ((p + by) & 3), 2)
        for n, t in enumerate(which):
            loads.append(pltpu.make_async_copy(weights[t].at[there], buf.at[slot], in_sem.at[slot]))
            stores.append(pltpu.make_async_copy(buf.at[slot], out.at[n], out_sem.at[slot]))
            slot += 1
    for c in loads:
        c.start()
    for load, store in zip(loads, stores):
        load.wait()
        store.start()
    for c in stores:
        c.wait()


def pack(weights, plans):
    slots = sum(len(which) for _, which in plans)
    return pl.pallas_call(
        functools.partial(pack_kernel, plans),
        out_shape=tuple(jax.ShapeDtypeStruct((len(which), 2, HS, D), BF16) for _, which in plans),
        in_specs=[pl.BlockSpec(memory_space=pl.ANY)] * 3,
        out_specs=(pl.BlockSpec(memory_space=pl.ANY),) * len(plans),
        scratch_shapes=[
            pltpu.VMEM((slots, 2, HS, D), BF16),
            pltpu.SemaphoreType.DMA((slots,)),
            pltpu.SemaphoreType.DMA((slots,)),
        ],
        compiler_params=pltpu.CompilerParams(vmem_limit_bytes=16 * 2**20),
        cost_estimate=pl.CostEstimate(flops=0, bytes_accessed=slots * 1_640_000, transcendentals=0),
    )(*in_hbm(weights))


def in_hbm(arrays):
    return [pltpu.with_memory_space_constraint(a, pltpu.HBM) for a in arrays]


def collect_kernel(wg, wu, wd, a1, a2, a3, b1, b2, b3, gu1, wd1, gu2, wd2, sems):
    p, q = place()
    copies = []
    for j, (gu_ref, wd_ref) in enumerate(((gu1, wd1), (gu2, wd2))):
        pick = (q & 1) ^ j
        own = 2 * p + pick
        sources = (
            (wg.at[own], wu.at[own], wd.at[own]),
        ) + tuple(
            (a.at[0, pick], a.at[1, pick], b.at[0, pick])
            for a, b in ((a1, b1), (a2, b2), (a3, b3))
        )
        for k, (g, u, d) in enumerate(sources):
            lo = pl.ds(k * HS, HS)
            hi = pl.ds(4 * HS + k * HS, HS)
            copies.append(pltpu.make_async_copy(g, gu_ref.at[lo], sems.at[j, 0, k]))
            copies.append(pltpu.make_async_copy(u, gu_ref.at[hi], sems.at[j, 1, k]))
            copies.append(pltpu.make_async_copy(d, wd_ref.at[lo], sems.at[j, 2, k]))
    for c in copies:
        c.start()
    for c in copies:
        c.wait()


def collect(weights, moved):
    gu = jax.ShapeDtypeStruct((8 * HS, D), BF16)
    down = jax.ShapeDtypeStruct((4 * HS, D), BF16)
    return pl.pallas_call(
        collect_kernel,
        out_shape=(gu, down, gu, down),
        in_specs=[pl.BlockSpec(memory_space=pl.ANY)] * 9,
        out_specs=(pl.BlockSpec(memory_space=pltpu.VMEM),) * 4,
        scratch_shapes=[pltpu.SemaphoreType.DMA((2, 3, 4))],
        compiler_params=pltpu.CompilerParams(vmem_limit_bytes=16 * 2**20),
        cost_estimate=pl.CostEstimate(flops=0, bytes_accessed=10_000_000, transcendentals=0),
    )(*in_hbm(weights), *moved)


def expert_kernel(sa, sb, gu_ref, wd_ref, oa, ob):
    rows = jnp.concatenate([sa[...], sb[...]], axis=0)
    gu = lax.dot_general(rows, gu_ref[...], (((1,), (1,)), ((), ())), preferred_element_type=F32)
    gate, up = gu[:, : 4 * HS], gu[:, 4 * HS :]
    act = (gate / (1.0 + jnp.exp(-gate)) * up).astype(BF16)
    out = jnp.dot(act, wd_ref[...], preferred_element_type=F32).astype(BF16)
    oa[...] = out[:ROWS]
    ob[...] = out[ROWS:]


def expert(sa, sb, gu, down):
    block = jax.ShapeDtypeStruct((ROWS, D), BF16)
    return pl.pallas_call(
        expert_kernel,
        out_shape=(block,) * 2,
        in_specs=[pl.BlockSpec(memory_space=pltpu.VMEM)] * 4,
        out_specs=(pl.BlockSpec(memory_space=pltpu.VMEM),) * 2,
        compiler_params=pltpu.CompilerParams(vmem_limit_bytes=24 * 2**20),
        cost_estimate=pl.CostEstimate(
            flops=2_500_000_000, bytes_accessed=2_000_000, transcendentals=655360
        ),
    )(sa, sb, gu, down)


def body(tokens, router, w_gate, w_up, w_down):
    weights = (w_gate, w_up, w_down)
    ups = pack(weights, tuple((by, (0, 1)) for by in (1, 2, 3)))
    tokens, router, *ups = lax.optimization_barrier((tokens, router, *ups))
    rows, comb = front(tokens, router)
    ups = [shift(w, True, by) for w, by in zip(ups, (1, 2, 3))]
    downs = pack(weights, tuple((by, (2,)) for by in (1, 2, 3)))
    downs = [shift(w, True, by) for w, by in zip(downs, (1, 2, 3))]
    s0 = lax.all_to_all(rows, AXES, split_axis=0, concat_axis=0, tiled=True)
    s0, *ups = lax.optimization_barrier((s0, *ups))
    s2, s1, s3 = (shift(s0, False, by) for by in (2, 1, 3))
    gu1, down1, gu2, down2 = collect(weights, ups + downs)
    o2, o0 = expert(s2, s0, gu1, down1)
    s1, s3, o2 = lax.optimization_barrier((s1, s3, o2))
    o1, o3 = expert(s1, s3, gu2, down2)
    t2, t1, t3 = shift(o2, False, 2), shift(o1, False, 3), shift(o3, False, 1)
    total = o0.astype(F32) + t1.astype(F32) + t2.astype(F32) + t3.astype(F32)
    out_rows = lax.all_to_all(
        total.astype(BF16), AXES, split_axis=0, concat_axis=0, tiled=True
    )
    mixed = jnp.dot(comb.reshape(2 * TOK, ROWS), out_rows, preferred_element_type=F32)
    return mixed.astype(BF16).reshape(2, TOK, D)


def solution(mesh):
    return jax.shard_map(
        body,
        mesh=mesh,
        in_specs=(
            P(("dp", "expert"), None, None),
            P(),
            P("expert", "dp", None),
            P("expert", "dp", None),
            P("expert", "dp", None),
        ),
        out_specs=P(("dp", "expert"), None, None),
        check_vma=False,
    )
```

time: 178 us -> 154 us (0.87)
  waiting for transfers between devices: 75.6 us -> 43.3 us
  Pallas kernels: 13.3 us -> 19.4 us
  blocking collectives: 35.4 us -> 41.3 us
  starting transfers between devices: 27.8 us -> 32.7 us
  local copies, waits for them, and re-layouts: 15.8 us -> 11.1 us
  other arithmetic: 8.18 us -> 4.25 us
    ppermute x9 -> x12, waiting for transfers between devices: 65.3 us -> 27.6 us  [shift(): return lax.ppermute(value, AXES, shift_pairs(along_p, by))]
    ppermute x9 -> x12, starting transfers between devices: 11.3 us -> 18.8 us  [shift(): return lax.ppermute(value, AXES, shift_pairs(along_p, by))]
    pallas_call x2 -> x6, Pallas kernels: 13.3 us -> 19.4 us  [the longest x2 7.02 us: pack(): pl.pallas_call(functools.partial(pack_kernel, plans), out_shape=tuple((ja...]
    all_to_all x1, blocking collectives: 35.4 us -> 41.3 us  [body(): lax.all_to_all(total.astype(BF16), AXES, split_axis=0, concat_axis=0, til...]
    all_to_all x1, waiting for transfers between devices: 10.3 us -> 15.7 us  [body(): s0 = lax.all_to_all(rows, AXES, split_axis=0, concat_axis=0, tiled=True)]
    another operation x3 -> x0, other arithmetic: 5.16 us -> none  [moved(): return shift(jnp.stack(parts), True, by)]
    all_to_all x1, starting transfers between devices: 16.5 us -> 13.9 us  [body(): s0 = lax.all_to_all(rows, AXES, split_axis=0, concat_axis=0, tiled=True)]
    unnamed x13 -> x11, local copies, waits for them, and re-layouts: 13 us -> 10.5 us
  transfers between devices with their start and end apart: 10 -> 13, of which waited for: 6 -> 9; matrix products, arithmetic and copies ran while one was open for 8% -> 8% of each run, Pallas kernels for 0% -> 8%
where the time goes in v2:
time: 154 us
  waiting for transfers between devices  43.3 us (28%)
  blocking collectives  41.3 us (27%)
  starting transfers between devices  32.7 us (21%)
  Pallas kernels  19.4 us (13%)
  local copies, waits for them, and re-layouts  11.1 us (7%)
  other arithmetic  4.25 us (3%)
  matrix products  1.57 us (1%)
    all_to_all x1, blocking collectives, body(): lax.all_to_all(total.astype(BF16), AXES, split_axis=0, concat_axis=0, til...  41.3 us
    ppermute x12, waiting for transfers between devices, shift(): return lax.ppermute(value, AXES, shift_pairs(along_p, by))  27.6 us
    ppermute x12, starting transfers between devices, shift(): return lax.ppermute(value, AXES, shift_pairs(along_p, by))  18.8 us
    all_to_all x1, waiting for transfers between devices, body(): s0 = lax.all_to_all(rows, AXES, split_axis=0, concat_axis=0, tiled=True)  15.7 us
    all_to_all x1, starting transfers between devices, body(): s0 = lax.all_to_all(rows, AXES, split_axis=0, concat_axis=0, tiled=True)  13.9 us
    unnamed x11, local copies, waits for them, and re-layouts  10.5 us
    pallas_call x2, Pallas kernels, pack(): pl.pallas_call(functools.partial(pack_kernel, plans), out_shape=tuple((ja...  7.02 us
    pallas_call x2, Pallas kernels, expert(): pl.pallas_call(expert_kernel, out_shape=(block,) * 2, in_specs=[pl.BlockS...  6.34 us
  transfers between devices with their start and end apart: 13, of which 9 were waited for; matrix products, arithmetic and copies ran while one was open for 8% of the time, Pallas kernels for 8%

profile of v2, /device:TPU:1, one launch (start us, length us, event | category | flops | bytes accessed | tf_op | source)
XLA Modules:
  0.0 153.7 jit_solution(15250420332854483291)
XLA Ops:
  0.0 4.3 %shard_map.55 = (bf16[2,2,160,1280]{3,2,1,0:T(8,128)(2,1)}, bf16[2,2,160,1280]{3,2,1,0:T(8,128)(2,1)}, bf16[2,2,160,1280]{3,2,1,0:T(8,128)(2,1)}) custom-call(bf16[8,160,1280]{2,1,0:T(8,128)(2,1)} %wg.1, bf16[8,160,1280]{2,1,0:T(8,128)(2,1)} %wu.1, bf16[8,160,1280]{2,1,0:T(8,128)(2,1)} %wd.1), custom_call_target="tpu_custom_call" | custom-call | bytes 9840000 | tf_op jit(solution)/shard_map/pallas_call | solution.py:118
  4.3 2.2 %collective-permute-start = (bf16[2,2,160,1280]{3,2,1,0:T(8,128)(2,1)}, bf16[2,2,160,1280]{3,2,1,0:T(8,128)(2,1)S(1)}, u32[]{:S(2)}, u32[]{:S(2)}) collective-permute-start(bf16[2,2,160,1280]{3,2,1,0:T(8,128)(2,1)} %get-tuple-element.40), channel_id=1, source_target_pairs={{0,16},{1,65},{2,18},{3,67},{4,20},{5,69},{6,22},{7,71},{8,24},{9,... | collective-permute-start | bytes 4915208 | tf_op jit(solution)/shard_map/ppermute | solution.py:41
  6.5 2.6 %collective-permute-start.1 = (bf16[2,2,160,1280]{3,2,1,0:T(8,128)(2,1)}, bf16[2,2,160,1280]{3,2,1,0:T(8,128)(2,1)S(1)}, u32[]{:S(2)}, u32[]{:S(2)}) collective-permute-start(bf16[2,2,160,1280]{3,2,1,0:T(8,128)(2,1)} %get-tuple-element.41), channel_id=1, source_target_pairs={{0,32},{1,129},{2,34},{3,131},{4,36},{5,133},{6,38},{7,135},{8,40}... | collective-permute-start | bytes 4915208 | tf_op jit(solution)/shard_map/ppermute | solution.py:41
  10.2 2.4 %shard_map.56 = (bf16[256,1280]{1,0:T(8,128)(2,1)S(1)}, bf16[2,256,256]{2,1,0:T(8,128)(2,1)S(1)}) custom-call(bf16[2,256,1280]{2,1,0:T(8,128)(2,1)S(1)} %copy-done.1, f32[1280,128]{1,0:T(8,128)S(1)} %copy-done.2), custom_call_target="tpu_custom_call" | custom-call | flops 900000000 | bytes 3000000 | tf_op jit(solution)/shard_map/pallas_call | solution.py:83
  14.0 2.8 %reduce = bf16[256,1280]{1,0:T(8,128)(2,1)} reduce(bf16[256,1,1280]{2,0,1:T(8,128)(2,1)} %bitcast.12, bf16[]{:T(256)} %broadcast), dimensions={1}, to_apply=%copy.8.reduce_sub_computation | reduce | bytes 1310722 | tf_op jit(solution)/shard_map/all_to_all | solution.py:207
  16.8 2.5 %reshape.12 = bf16[256,2,640]{2,1,0:T(2,128)(2,1)} reshape(bf16[256,1280]{1,0:T(8,128)(2,1)} %reduce) | data formatting | bytes 1310720
  19.3 13.9 %all-to-all-start = ((bf16[256,2,640]{2,1,0:T(2,128)(2,1)}), bf16[256,2,640]{2,1,0:T(2,128)(2,1)}, u32[]{:S(2)}, u32[]{:S(2)}) async-start(bf16[256,2,640]{2,1,0:T(2,128)(2,1)} %reshape.12), calls=%async_computation | async-start | bytes 1310720 | tf_op jit(solution)/shard_map/all_to_all | solution.py:207
  33.3 2.7 %shard_map.57 = (bf16[1,2,160,1280]{3,2,1,0:T(8,128)(2,1)}, bf16[1,2,160,1280]{3,2,1,0:T(8,128)(2,1)}, bf16[1,2,160,1280]{3,2,1,0:T(8,128)(2,1)}) custom-call(bf16[8,160,1280]{2,1,0:T(8,128)(2,1)} %wg.1, bf16[8,160,1280]{2,1,0:T(8,128)(2,1)} %wu.1, bf16[8,160,1280]{2,1,0:T(8,128)(2,1)} %wd.1), custom_call_target="tpu_custom_call" | custom-call | bytes 4920000 | tf_op jit(solution)/shard_map/pallas_call | solution.py:118
  37.5 2.4 %collective-permute-start.5 = (bf16[1,2,160,1280]{3,2,1,0:T(8,128)(2,1)}, bf16[1,2,160,1280]{3,2,1,0:T(8,128)(2,1)}, u32[]{:S(2)}, u32[]{:S(2)}) collective-permute-start(bf16[1,2,160,1280]{3,2,1,0:T(8,128)(2,1)} %get-tuple-element.48), channel_id=1, source_target_pairs={{0,32},{1,129},{2,34},{3,131},{4,36},{5,133},{6,38},{7,135},{8,40}... | collective-permute-start | bytes 2457608 | tf_op jit(solution)/shard_map/ppermute | solution.py:41
  41.1 15.7 %all-to-all-done = bf16[256,2,640]{2,1,0:T(2,128)(2,1)} async-done(((bf16[256,2,640]{2,1,0:T(2,128)(2,1)}), bf16[256,2,640]{2,1,0:T(2,128)(2,1)}, u32[]{:S(2)}, u32[]{:S(2)}) %all-to-all-start) | async-done | bytes 655392 | tf_op jit(solution)/shard_map/all_to_all | solution.py:207
  56.7 5.1 %reshape.13 = bf16[256,1,1280]{2,1,0:T(2,128)(2,1)} reshape(bf16[256,2,640]{2,1,0:T(2,128)(2,1)} %all-to-all-done) | data formatting | bytes 1310720
  63.2 1.8 %collective-permute-start.3 = (bf16[256,1280]{1,0:T(8,128)(2,1)S(1)}, bf16[256,1280]{1,0:T(8,128)(2,1)S(1)}, u32[]{:S(2)}, u32[]{:S(2)}) collective-permute-start(bf16[256,1280]{1,0:T(8,128)(2,1)S(1)} %bitcast.13), channel_id=1, source_target_pairs={{0,128},{1,33},{2,130},{3,35},{4,132},{5,37},{6,134},{7,39},{8,136... | collective-permute-start | bytes 1966088 | tf_op jit(solution)/shard_map/ppermute | solution.py:41
  65.5 2.2 %collective-permute-start.8 = (bf16[256,1280]{1,0:T(8,128)(2,1)S(1)}, bf16[256,1280]{1,0:T(8,128)(2,1)S(1)}, u32[]{:S(2)}, u32[]{:S(2)}) collective-permute-start(bf16[256,1280]{1,0:T(8,128)(2,1)S(1)} %bitcast.15), channel_id=1, source_target_pairs={{0,192},{1,49},{2,194},{3,51},{4,196},{5,53},{6,198},{7,55},{8,200... | collective-permute-start | bytes 1966088 | tf_op jit(solution)/shard_map/ppermute | solution.py:41
  67.7 4.9 %collective-permute-done.5.b2 = bf16[1,2,160,1280]{3,2,1,0:T(8,128)(2,1)} collective-permute-done((bf16[1,2,160,1280]{3,2,1,0:T(8,128)(2,1)}, bf16[1,2,160,1280]{3,2,1,0:T(8,128)(2,1)}, u32[]{:S(2)}, u32[]{:S(2)}) %collective-permute-start.5) | collective-permute-done | bytes 819232 | tf_op jit(solution)/shard_map/ppermute | solution.py:41
  72.9 3.6 %shard_map.58 = (bf16[1280,1280]{1,0:T(8,128)(2,1)S(1)}, bf16[640,1280]{1,0:T(8,128)(2,1)S(1)}, bf16[1280,1280]{1,0:T(8,128)(2,1)S(1)}, bf16[640,1280]{1,0:T(8,128)(2,1)S(1)}) custom-call(bf16[8,160,1280]{2,1,0:T(8,128)(2,1)} %wg.1, bf16[8,160,1280]{2,1,0:T(8,128)(2,1)} %wu.1, bf16[8,160,1280]{2,1,0:T(8,128)(2,1)} %wd.1, ...), custom_call_target="tpu_custom_call" | custom-call | bytes 10000000 | tf_op jit(solution)/shard_map/pallas_call | solution.py:164
  76.5 1.5 collective-permute-done.3.sa
  78.0 3.2 %shard_map.59 = (bf16[256,1280]{1,0:T(8,128)(2,1)S(1)}, bf16[256,1280]{1,0:T(8,128)(2,1)S(1)}) custom-call(bf16[256,1280]{1,0:T(8,128)(2,1)S(1)} %collective-permute-done.3.sa, bf16[256,1280]{1,0:T(8,128)(2,1)S(1)} %bitcast.16, bf16[1280,1280]{1,0:T(8,128)(2,1)S(1)} %get-tuple-element.50.gu_ref, bf16[640,1280]{1,0:T(8,128)(2,1)S(1)} %get-tuple-element.51.wd_ref), custom_call_target="tpu_custom_call" | custom-call | flops 2500000000 | bytes 2000000 | tf_op jit(solution)/shard_map/pallas_call | solution.py:187
  81.2 4.4 %collective-permute-done.7.sa = bf16[256,1280]{1,0:T(8,128)(2,1)S(1)} collective-permute-done((bf16[256,1280]{1,0:T(8,128)(2,1)S(1)}, bf16[256,1280]{1,0:T(8,128)(2,1)S(1)}, u32[]{:S(2)}, u32[]{:S(2)}) %collective-permute-start.7) | collective-permute-done | bytes 655392 | tf_op jit(solution)/shard_map/ppermute | solution.py:41
  86.9 3.2 %shard_map.60 = (bf16[256,1280]{1,0:T(8,128)(2,1)S(1)}, bf16[256,1280]{1,0:T(8,128)(2,1)S(1)}) custom-call(bf16[256,1280]{1,0:T(8,128)(2,1)S(1)} %collective-permute-done.7.sa, bf16[256,1280]{1,0:T(8,128)(2,1)S(1)} %collective-permute-done.8.sb, bf16[1280,1280]{1,0:T(8,128)(2,1)S(1)} %get-tuple-element.56.gu_ref, bf16[640,1280]{1,0:T(8,128)(2,1)S(1)} %get-tuple-element.57.wd_ref), custom_call_target="tpu_custom_call" | custom-call | flops 2500000000 | bytes 2000000 | tf_op jit(solution)/shard_map/pallas_call | solution.py:187
  90.2 2.7 %collective-permute-start.9 = (bf16[256,1280]{1,0:T(8,128)(2,1)S(1)}, bf16[256,1280]{1,0:T(8,128)(2,1)S(1)}, u32[]{:S(2)}, u32[]{:S(2)}) collective-permute-start(bf16[256,1280]{1,0:T(8,128)(2,1)S(1)} %get-tuple-element.58), channel_id=1, source_target_pairs={{0,192},{1,49},{2,194},{3,51},{4,196},{5,53},{6,198},{7,55},{8,200... | collective-permute-start | bytes 1966088 | tf_op jit(solution)/shard_map/ppermute | solution.py:41
  93.4 7.7 %collective-permute-done.11 = bf16[256,1280]{1,0:T(8,128)(2,1)S(1)} collective-permute-done((bf16[256,1280]{1,0:T(8,128)(2,1)S(1)}, bf16[256,1280]{1,0:T(8,128)(2,1)S(1)}, u32[]{:S(2)}, u32[]{:S(2)}) %collective-permute-start.11) | collective-permute-done | bytes 655392 | tf_op jit(solution)/shard_map/ppermute | solution.py:41
  101.1 6.3 %collective-permute-done.9 = bf16[256,1280]{1,0:T(8,128)(2,1)S(1)} collective-permute-done((bf16[256,1280]{1,0:T(8,128)(2,1)S(1)}, bf16[256,1280]{1,0:T(8,128)(2,1)S(1)}, u32[]{:S(2)}, u32[]{:S(2)}) %collective-permute-start.9) | collective-permute-done | bytes 655392 | tf_op jit(solution)/shard_map/ppermute | solution.py:41
  110.2 41.3 %all_to_all.24 = bf16[256,2,640]{2,1,0:T(2,128)(2,1)S(1)} all-to-all(bf16[256,2,640]{2,1,0:T(2,128)(2,1)S(1)} %reshape.14), channel_id=1, replica_groups=mesh['dp'=16,'expert'=16] {'dp','expert'}, dimensions={0} | all-to-all | bytes 1310720 | tf_op jit(solution)/shard_map/all_to_all | solution.py:216
  152.1 1.6 %convolution_convert_fusion = bf16[512,1280]{1,0:T(8,128)(2,1)} fusion(bf16[512,256]{1,0:T(8,128)(2,1)S(1)} %bitcast.17, bf16[256,1,1280]{2,1,0:T(2,128)(2,1)S(1)} %reshape.15), kind=kOutput, calls=%fused_computation | convolution fusion | flops 336199680 | bytes 2228224 | tf_op jit(solution)/shard_map/dot_general | solution.py:219
  (25 shorter events, 12.4 us)
Async XLA Ops:
  0.0 10.2 %copy-start.1 = (bf16[2,256,1280]{2,1,0:T(8,128)(2,1)S(1)}, bf16[2,256,1280]{2,1,0:T(8,128)(2,1)}, u32[]{:S(2)}) copy-start(bf16[2,256,1280]{2,1,0:T(8,128)(2,1)} %tok_ref) | copy-start | bytes 3932164
  0.0 10.2 %copy-start.2 = (f32[1280,128]{1,0:T(8,128)S(1)}, f32[1280,128]{1,0:T(8,128)}, u32[]{:S(2)}) copy-start(f32[1280,128]{1,0:T(8,128)} %router_ref) | copy-start | bytes 1966084
  4.3 35.6 %collective-permute-start = (bf16[2,2,160,1280]{3,2,1,0:T(8,128)(2,1)}, bf16[2,2,160,1280]{3,2,1,0:T(8,128)(2,1)S(1)}, u32[]{:S(2)}, u32[]{:S(2)}) collective-permute-start(bf16[2,2,160,1280]{3,2,1,0:T(8,128)(2,1)} %get-tuple-element.40), channel_id=1, source_target_pairs={{0,16},{1,65},{2,18},{3,67},{4,20},{5,69},{6,22},{7,71},{8,24},{9,... | collective-permute-start | bytes 4915208 | tf_op jit(solution)/shard_map/ppermute | solution.py:41
  6.5 56.7 %collective-permute-start.1 = (bf16[2,2,160,1280]{3,2,1,0:T(8,128)(2,1)}, bf16[2,2,160,1280]{3,2,1,0:T(8,128)(2,1)S(1)}, u32[]{:S(2)}, u32[]{:S(2)}) collective-permute-start(bf16[2,2,160,1280]{3,2,1,0:T(8,128)(2,1)} %get-tuple-element.41), channel_id=1, source_target_pairs={{0,32},{1,129},{2,34},{3,131},{4,36},{5,133},{6,38},{7,135},{8,40}... | collective-permute-start | bytes 4915208 | tf_op jit(solution)/shard_map/ppermute | solution.py:41
  9.1 54.1 %collective-permute-start.2 = (bf16[2,2,160,1280]{3,2,1,0:T(8,128)(2,1)}, bf16[2,2,160,1280]{3,2,1,0:T(8,128)(2,1)}, u32[]{:S(2)}, u32[]{:S(2)}) collective-permute-start(bf16[2,2,160,1280]{3,2,1,0:T(8,128)(2,1)} %get-tuple-element.42), channel_id=1, source_target_pairs={{0,48},{1,193},{2,50},{3,195},{4,52},{5,197},{6,54},{7,199},{8,56}... | collective-permute-start | bytes 4915208 | tf_op jit(solution)/shard_map/ppermute | solution.py:41
  12.6 0.8 copy-start
  19.3 37.4 %all-to-all-start = ((bf16[256,2,640]{2,1,0:T(2,128)(2,1)}), bf16[256,2,640]{2,1,0:T(2,128)(2,1)}, u32[]{:S(2)}, u32[]{:S(2)}) async-start(bf16[256,2,640]{2,1,0:T(2,128)(2,1)} %reshape.12), calls=%async_computation | async-start | bytes 1310720 | tf_op jit(solution)/shard_map/all_to_all | solution.py:207
  36.0 29.5 %collective-permute-start.4 = (bf16[1,2,160,1280]{3,2,1,0:T(8,128)(2,1)}, bf16[1,2,160,1280]{3,2,1,0:T(8,128)(2,1)}, u32[]{:S(2)}, u32[]{:S(2)}) collective-permute-start(bf16[1,2,160,1280]{3,2,1,0:T(8,128)(2,1)} %get-tuple-element.47), channel_id=1, source_target_pairs={{0,16},{1,65},{2,18},{3,67},{4,20},{5,69},{6,22},{7,71},{8,24},{9,... | collective-permute-start | bytes 2457608 | tf_op jit(solution)/shard_map/ppermute | solution.py:41
  37.5 35.2 %collective-permute-start.5 = (bf16[1,2,160,1280]{3,2,1,0:T(8,128)(2,1)}, bf16[1,2,160,1280]{3,2,1,0:T(8,128)(2,1)}, u32[]{:S(2)}, u32[]{:S(2)}) collective-permute-start(bf16[1,2,160,1280]{3,2,1,0:T(8,128)(2,1)} %get-tuple-element.48), channel_id=1, source_target_pairs={{0,32},{1,129},{2,34},{3,131},{4,36},{5,133},{6,38},{7,135},{8,40}... | collective-permute-start | bytes 2457608 | tf_op jit(solution)/shard_map/ppermute | solution.py:41
  39.9 33.0 %collective-permute-start.6 = (bf16[1,2,160,1280]{3,2,1,0:T(8,128)(2,1)}, bf16[1,2,160,1280]{3,2,1,0:T(8,128)(2,1)}, u32[]{:S(2)}, u32[]{:S(2)}) collective-permute-start(bf16[1,2,160,1280]{3,2,1,0:T(8,128)(2,1)} %get-tuple-element.49), channel_id=1, source_target_pairs={{0,48},{1,193},{2,50},{3,195},{4,52},{5,197},{6,54},{7,199},{8,56}... | collective-permute-start | bytes 2457608 | tf_op jit(solution)/shard_map/ppermute | solution.py:41
  63.2 14.8 %collective-permute-start.3 = (bf16[256,1280]{1,0:T(8,128)(2,1)S(1)}, bf16[256,1280]{1,0:T(8,128)(2,1)S(1)}, u32[]{:S(2)}, u32[]{:S(2)}) collective-permute-start(bf16[256,1280]{1,0:T(8,128)(2,1)S(1)} %bitcast.13), channel_id=1, source_target_pairs={{0,128},{1,33},{2,130},{3,35},{4,132},{5,37},{6,134},{7,39},{8,136... | collective-permute-start | bytes 1966088 | tf_op jit(solution)/shard_map/ppermute | solution.py:41
  65.1 20.6 %collective-permute-start.7 = (bf16[256,1280]{1,0:T(8,128)(2,1)S(1)}, bf16[256,1280]{1,0:T(8,128)(2,1)S(1)}, u32[]{:S(2)}, u32[]{:S(2)}) collective-permute-start(bf16[256,1280]{1,0:T(8,128)(2,1)S(1)} %bitcast.14), channel_id=1, source_target_pairs={{0,64},{1,17},{2,66},{3,19},{4,68},{5,21},{6,70},{7,23},{8,72},{9,... | collective-permute-start | bytes 1966088 | tf_op jit(solution)/shard_map/ppermute | solution.py:41
  65.5 21.4 %collective-permute-start.8 = (bf16[256,1280]{1,0:T(8,128)(2,1)S(1)}, bf16[256,1280]{1,0:T(8,128)(2,1)S(1)}, u32[]{:S(2)}, u32[]{:S(2)}) collective-permute-start(bf16[256,1280]{1,0:T(8,128)(2,1)S(1)} %bitcast.15), channel_id=1, source_target_pairs={{0,192},{1,49},{2,194},{3,51},{4,196},{5,53},{6,198},{7,55},{8,200... | collective-permute-start | bytes 1966088 | tf_op jit(solution)/shard_map/ppermute | solution.py:41
  90.1 11.0 %collective-permute-start.11 = (bf16[256,1280]{1,0:T(8,128)(2,1)S(1)}, bf16[256,1280]{1,0:T(8,128)(2,1)S(1)}, u32[]{:S(2)}, u32[]{:S(2)}) collective-permute-start(bf16[256,1280]{1,0:T(8,128)(2,1)S(1)} %get-tuple-element.60), channel_id=1, source_target_pairs={{0,64},{1,17},{2,66},{3,19},{4,68},{5,21},{6,70},{7,23},{8,72},{9,... | collective-permute-start | bytes 1966088 | tf_op jit(solution)/shard_map/ppermute | solution.py:41
  90.2 17.2 %collective-permute-start.9 = (bf16[256,1280]{1,0:T(8,128)(2,1)S(1)}, bf16[256,1280]{1,0:T(8,128)(2,1)S(1)}, u32[]{:S(2)}, u32[]{:S(2)}) collective-permute-start(bf16[256,1280]{1,0:T(8,128)(2,1)S(1)} %get-tuple-element.58), channel_id=1, source_target_pairs={{0,192},{1,49},{2,194},{3,51},{4,196},{5,53},{6,198},{7,55},{8,200... | collective-permute-start | bytes 1966088 | tf_op jit(solution)/shard_map/ppermute | solution.py:41
  92.8 15.8 %collective-permute-start.10 = (bf16[256,1280]{1,0:T(8,128)(2,1)S(1)}, bf16[256,1280]{1,0:T(8,128)(2,1)S(1)}, u32[]{:S(2)}, u32[]{:S(2)}) collective-permute-start(bf16[256,1280]{1,0:T(8,128)(2,1)S(1)} %get-tuple-element.59), channel_id=1, source_target_pairs={{0,128},{1,33},{2,130},{3,35},{4,132},{5,37},{6,134},{7,39},{8,136... | collective-permute-start | bytes 1966088 | tf_op jit(solution)/shard_map/ppermute | solution.py:41

commit v3 on v2

v3 whole, which is shorter than its diff:
```python
import functools
import math

import jax
import jax.numpy as jnp
from jax import lax
from jax.experimental import pallas as pl
from jax.experimental.pallas import tpu as pltpu
from jax.sharding import PartitionSpec as P

D = 1280
EXPERTS = 128
TOK = 256
HS = 160
ROWS = 256
AXES = ("dp", "expert")
F32 = jnp.float32
BF16 = jnp.bfloat16


def place():
    dp = lax.axis_index("dp")
    core = lax.axis_index("expert") & 1
    y, x = dp >> 2, dp & 3
    p = jnp.where(core == 0, x, y)
    q = jnp.where(core == 0, y, x)
    return p, q


def shift_pairs(along_p, by):
    pairs = []
    for y in range(4):
        for x in range(4):
            for e in range(16):
                move_x = (e % 2 == 0) == along_p
                ny, nx = (y, (x + by) % 4) if move_x else ((y + by) % 4, x)
                pairs.append(((y * 4 + x) * 16 + e, (ny * 4 + nx) * 16 + e))
    return pairs


GROUPS = [
    [
        ((f * 4 + p) if core == 0 else (p * 4 + f)) * 16 + z * 2 + core
        for p in range(4)
        for z in range(8)
    ]
    for core in range(2)
    for f in range(4)
]


def exchange(rows):
    return lax.all_to_all(
        rows, AXES, split_axis=0, concat_axis=0, tiled=True, axis_index_groups=GROUPS
    )


def swap(value):
    return lax.ppermute(value, "expert", [(e, e ^ 1) for e in range(16)])


def shift(value, along_p, by):
    return lax.ppermute(value, AXES, shift_pairs(along_p, by))


def one_hot(chosen, lines):
    line = lax.broadcasted_iota(jnp.int32, (lines, ROWS), 0)
    return jnp.where(chosen == line, 1.0, 0.0).astype(BF16)


def columns(lines):
    return lax.broadcasted_iota(jnp.int32, (lines, ROWS), 1)


def front_kernel(tok_ref, router_ref, mine_ref, other_ref, comb_ref):
    row = columns(EXPERTS)
    core = (lax.axis_index("expert") & 1) ^ (row >> 7)
    expert = ((row >> 2) & 7) * 16 + core * 8 + ((row >> 5) & 3) * 2 + ((row >> 1) & 1)
    r = router_ref[...]
    r0 = r.astype(BF16)
    rest = r - r0.astype(F32)
    r1 = rest.astype(BF16)
    r2 = (rest - r1.astype(F32)).astype(BF16)
    rows = jnp.zeros((ROWS, D), F32)
    for i in range(2):
        tok = tok_ref[i]
        logits = (
            jnp.dot(tok, r2, preferred_element_type=F32)
            + jnp.dot(tok, r1, preferred_element_type=F32)
            + jnp.dot(tok, r0, preferred_element_type=F32)
        )
        select = one_hot(jnp.where((row & 1) == i, expert, -1), EXPERTS)
        ex = jnp.exp(logits - jnp.max(logits, axis=0, keepdims=True))
        disp = (ex / jnp.sum(ex, axis=0, keepdims=True)).astype(BF16)
        ec = jnp.exp(logits - jnp.max(logits, axis=1, keepdims=True))
        comb = (ec / jnp.sum(ec, axis=1, keepdims=True)).astype(BF16)
        disp_rows = jnp.dot(disp, select, preferred_element_type=F32)
        comb_ref[i] = jnp.dot(comb, select, preferred_element_type=F32).astype(BF16)
        rows = rows + jnp.dot(
            jnp.transpose(disp_rows).astype(BF16), tok, preferred_element_type=F32
        )
    mine_ref[...] = rows[:128].astype(BF16)
    other_ref[...] = rows[128:].astype(BF16)


def front(tokens, router):
    return pl.pallas_call(
        front_kernel,
        out_shape=(
            jax.ShapeDtypeStruct((128, D), BF16),
            jax.ShapeDtypeStruct((128, D), BF16),
            jax.ShapeDtypeStruct((2, TOK, ROWS), BF16),
        ),
        in_specs=[pl.BlockSpec(memory_space=pltpu.VMEM)] * 2,
        out_specs=(pl.BlockSpec(memory_space=pltpu.VMEM),) * 3,
        compiler_params=pltpu.CompilerParams(vmem_limit_bytes=20 * 2**20),
        cost_estimate=pl.CostEstimate(flops=900_000_000, bytes_accessed=3_000_000, transcendentals=131072),
    )(tokens, router)


def pack_kernel(plans, *refs):
    weights, outs, (buf, in_sem, out_sem) = refs[:3], refs[3 : 3 + len(plans)], refs[3 + len(plans) :]
    p, _ = place()
    loads, stores = [], []
    slot = 0
    for (by, which), out in zip(plans, outs):
        there = pl.ds(2 * ((p + by) & 3), 2)
        for n, t in enumerate(which):
            loads.append(pltpu.make_async_copy(weights[t].at[there], buf.at[slot], in_sem.at[slot]))
            stores.append(pltpu.make_async_copy(buf.at[slot], out.at[n], out_sem.at[slot]))
            slot += 1
    for c in loads:
        c.start()
    for load, store in zip(loads, stores):
        load.wait()
        store.start()
    for c in stores:
        c.wait()


def pack(weights, plans):
    slots = sum(len(which) for _, which in plans)
    return pl.pallas_call(
        functools.partial(pack_kernel, plans),
        out_shape=tuple(jax.ShapeDtypeStruct((len(which), 2, HS, D), BF16) for _, which in plans),
        in_specs=[pl.BlockSpec(memory_space=pl.ANY)] * 3,
        out_specs=(pl.BlockSpec(memory_space=pl.ANY),) * len(plans),
        scratch_shapes=[
            pltpu.VMEM((slots, 2, HS, D), BF16),
            pltpu.SemaphoreType.DMA((slots,)),
            pltpu.SemaphoreType.DMA((slots,)),
        ],
        compiler_params=pltpu.CompilerParams(vmem_limit_bytes=16 * 2**20),
        cost_estimate=pl.CostEstimate(flops=0, bytes_accessed=slots * 1_640_000, transcendentals=0),
    )(*in_hbm(weights))


def in_hbm(arrays):
    return [pltpu.with_memory_space_constraint(a, pltpu.HBM) for a in arrays]


def reorder_kernel(source, count, *refs):
    parts, outs = refs[:count], refs[count:]
    rows = jnp.concatenate([r[...].reshape(-1, D) for r in parts], axis=0)
    moved = lax.dot_general(
        one_hot(source(columns(ROWS)), ROWS),
        rows,
        (((0,), (0,)), ((), ())),
        preferred_element_type=F32,
    ).astype(BF16)
    start = 0
    for out in outs:
        size = math.prod(out.shape[:-1])
        out[...] = moved[start : start + size].reshape(out.shape)
        start += size


def reorder(parts, source, shapes):
    return pl.pallas_call(
        functools.partial(reorder_kernel, source, len(parts)),
        out_shape=tuple(jax.ShapeDtypeStruct(shape, BF16) for shape in shapes),
        in_specs=[pl.BlockSpec(memory_space=pltpu.VMEM)] * len(parts),
        out_specs=(pl.BlockSpec(memory_space=pltpu.VMEM),) * len(shapes),
        compiler_params=pltpu.CompilerParams(vmem_limit_bytes=16 * 2**20),
        cost_estimate=pl.CostEstimate(flops=170_000_000, bytes_accessed=1_300_000, transcendentals=0),
    )(*parts)


def weave(n):
    return ((n >> 2) & 1) * 128 + (n >> 3) * 4 + (n & 3)


def unweave(n):
    return ((n >> 2) & 31) * 8 + (n >> 7) * 4 + (n & 3)


def deal(n):
    return ((n >> 2) & 31) * 8 + ((n >> 1) & 1) * 4 + (n >> 7) * 2 + (n & 1)


def undeal(n):
    return ((n >> 1) & 1) * 128 + (n >> 3) * 4 + ((n >> 2) & 1) * 2 + (n & 1)


def collect_kernel(*refs):
    weights, moved, (out, sems) = refs[:-5], refs[-5:-2], refs[-2:]
    p, _ = place()
    copies = []
    for j in range(2):
        for t, w in enumerate(weights):
            sources = [w.at[2 * p + j]] + [m.at[t, j] for m in moved]
            for k, src in enumerate(sources):
                dst = out.at[j, pl.ds((4 * t + k) * HS, HS)]
                copies.append(pltpu.make_async_copy(src, dst, sems.at[j, t, k]))
    for c in copies:
        c.start()
    for c in copies:
        c.wait()


def collect(weights, moved):
    count = len(weights)
    return pl.pallas_call(
        collect_kernel,
        out_shape=jax.ShapeDtypeStruct((2, count * 4 * HS, D), BF16),
        in_specs=[pl.BlockSpec(memory_space=pl.ANY)] * (count + 3),
        out_specs=pl.BlockSpec(memory_space=pltpu.VMEM),
        scratch_shapes=[pltpu.SemaphoreType.DMA((2, count, 4))],
        compiler_params=pltpu.CompilerParams(vmem_limit_bytes=16 * 2**20),
        cost_estimate=pl.CostEstimate(flops=0, bytes_accessed=count * 6_600_000, transcendentals=0),
    )(*in_hbm(weights), *moved)


def experts_kernel(count, *refs):
    slots, (gu_ref, wd_ref), outs = refs[:count], refs[count : count + 2], refs[count + 2 :]
    for j in range(2):
        rows = jnp.concatenate([s[j] for s in slots], axis=0)
        gu = lax.dot_general(
            rows, gu_ref[j], (((1,), (1,)), ((), ())), preferred_element_type=F32
        )
        gate, up = gu[:, : 4 * HS], gu[:, 4 * HS :]
        act = (gate / (1.0 + jnp.exp(-gate)) * up).astype(BF16)
        out = jnp.dot(act, wd_ref[j], preferred_element_type=F32).astype(BF16)
        start = 0
        for o in outs:
            o[j] = out[start : start + o.shape[1]]
            start += o.shape[1]


def experts(slots, gu, down):
    rows = sum(2 * s.shape[1] for s in slots)
    return pl.pallas_call(
        functools.partial(experts_kernel, len(slots)),
        out_shape=tuple(jax.ShapeDtypeStruct(s.shape, BF16) for s in slots),
        in_specs=[pl.BlockSpec(memory_space=pltpu.VMEM)] * (len(slots) + 2),
        out_specs=(pl.BlockSpec(memory_space=pltpu.VMEM),) * len(slots),
        compiler_params=pltpu.CompilerParams(vmem_limit_bytes=24 * 2**20),
        cost_estimate=pl.CostEstimate(
            flops=rows * 4_900_000, bytes_accessed=2_000_000, transcendentals=rows * 1280
        ),
    )(*slots, gu, down)


def merge_kernel(o1, o3, x, y, out1, out3):
    half = x.shape[1]
    out3[:, :half] = (o3[:, :half].astype(F32) + x[...].astype(F32)).astype(BF16)
    out3[:, half:] = o3[:, half:]
    out1[:, :half] = o1[:, :half]
    out1[:, half:] = (o1[:, half:].astype(F32) + y[...].astype(F32)).astype(BF16)


def merge(o1, o3, x, y):
    return pl.pallas_call(
        merge_kernel,
        out_shape=(jax.ShapeDtypeStruct(o1.shape, BF16),) * 2,
        in_specs=[pl.BlockSpec(memory_space=pltpu.VMEM)] * 4,
        out_specs=(pl.BlockSpec(memory_space=pltpu.VMEM),) * 2,
        compiler_params=pltpu.CompilerParams(vmem_limit_bytes=8 * 2**20),
        cost_estimate=pl.CostEstimate(flops=400_000, bytes_accessed=3_000_000, transcendentals=0),
    )(o1, o3, x, y)


def body(tokens, router, w_gate, w_up, w_down):
    ups = pack((w_gate, w_up, w_down), tuple((by, (0, 1)) for by in (1, 2, 3)))
    tokens, router, *ups = lax.optimization_barrier((tokens, router, *ups))
    mine, other, comb = front(tokens, router)
    ups = [shift(w, True, by) for w, by in zip(ups, (1, 2, 3))]
    downs = pack((w_gate, w_up, w_down), tuple((by, (2,)) for by in (1, 2, 3)))
    downs = [shift(w, True, by) for w, by in zip(downs, (1, 2, 3))]
    (rows,) = reorder((mine, swap(other)), weave, ((ROWS, D),))
    rows = exchange(rows)
    rows, *ups = lax.optimization_barrier((rows, *ups))
    (s0,) = reorder((rows,), deal, ((2, 128, D),))
    s1, s3 = shift(s0, False, 1), shift(s0, False, 3)
    gu = collect((w_gate, w_up), ups)
    s1, s3, gu = lax.optimization_barrier((s1, s3, gu))
    far = shift(s1[:, :64], False, 1), shift(s3[:, 64:], False, 3)
    down = collect((w_down,), downs)
    o1, o3 = experts((s1, s3), gu, down)
    far, o1, o3 = lax.optimization_barrier((far, o1, o3))
    low, high = experts(far, gu, down)
    x, y = shift(low, False, 1), shift(high, False, 3)
    (o0,) = experts((s0,), gu, down)
    o1, o3 = merge(o1, o3, x, y)
    t1, t3 = shift(o1, False, 3), shift(o3, False, 1)
    total = o0.astype(F32) + t1.astype(F32) + t3.astype(F32)
    (rows,) = reorder((total.astype(BF16),), undeal, ((ROWS, D),))
    mine, other = reorder((exchange(rows),), unweave, ((128, D),) * 2)
    rows = jnp.concatenate([mine, swap(other)], axis=0)
    mixed = jnp.dot(comb.reshape(2 * TOK, ROWS), rows, preferred_element_type=F32)
    return mixed.astype(BF16).reshape(2, TOK, D)


def solution(mesh):
    return jax.shard_map(
        body,
        mesh=mesh,
        in_specs=(
            P(("dp", "expert"), None, None),
            P(),
            P("expert", "dp", None),
            P("expert", "dp", None),
            P("expert", "dp", None),
        ),
        out_specs=P(("dp", "expert"), None, None),
        check_vma=False,
    )
```

time: 154 us -> 142 us (0.922)
  blocking collectives: 41.3 us -> 27.6 us
  local copies, waits for them, and re-layouts: 11.1 us -> 0.05 us
  Pallas kernels: 19.4 us -> 26.6 us
  waiting for transfers between devices: 43.3 us -> 50.3 us
  other arithmetic: 4.25 us -> 0.24 us
  starting transfers between devices: 32.7 us -> 35 us
    all_to_all x1, blocking collectives: 41.3 us -> 27.6 us  [exchange(): lax.all_to_all(rows, AXES, split_axis=0, concat_axis=0, tiled=True, axis_...]
    unnamed x11 -> x4, local copies, waits for them, and re-layouts: 10.5 us -> 0.01 us
    pallas_call x4 -> x11, Pallas kernels: 12.4 us -> 19.6 us  [the longest x3 10.1 us: experts(): pl.pallas_call(functools.partial(experts_kernel, len(slots)), out_shape=t...]
    ppermute x12 -> x14, waiting for transfers between devices: 27.6 us -> 33.7 us  [shift(): return lax.ppermute(value, AXES, shift_pairs(along_p, by))]
    all_to_all x3 -> x0, other arithmetic: 4.25 us -> none  [the longest x1 2.84 us: body(): s0 = lax.all_to_all(rows, AXES, split_axis=0, concat_axis=0, tiled=True)]
    ppermute x12 -> x14, starting transfers between devices: 18.8 us -> 21.6 us  [shift(): return lax.ppermute(value, AXES, shift_pairs(along_p, by))]
    all_to_all x1, starting transfers between devices: 13.9 us -> 11.2 us  [exchange(): lax.all_to_all(rows, AXES, split_axis=0, concat_axis=0, tiled=True, axis_...]
    ppermute x0 -> x2, waiting for transfers between devices: none -> 2.51 us  [swap(): return lax.ppermute(value, 'expert', [(e, e ^ 1) for e in range(16)])]
  transfers between devices with their start and end apart: 13 -> 17, of which waited for: 9 -> 8; matrix products, arithmetic and copies ran while one was open for 8% -> 0% of each run, Pallas kernels for 8% -> 13%
where the time goes in v3:
time: 142 us; the launch traced here: 141 us
  waiting for transfers between devices  50.3 us (35%)
  starting transfers between devices  35 us (25%)
  blocking collectives  27.6 us (19%)
  Pallas kernels  26.6 us (19%)
  matrix products  1.56 us (1%)
    ppermute x14, waiting for transfers between devices, shift(): return lax.ppermute(value, AXES, shift_pairs(along_p, by))  33.7 us
    all_to_all x1, blocking collectives, exchange(): lax.all_to_all(rows, AXES, split_axis=0, concat_axis=0, tiled=True, axis_...  27.6 us
    ppermute x14, starting transfers between devices, shift(): return lax.ppermute(value, AXES, shift_pairs(along_p, by))  21.6 us
    all_to_all x1, waiting for transfers between devices, exchange(): lax.all_to_all(rows, AXES, split_axis=0, concat_axis=0, tiled=True, axis_...  14.1 us
    all_to_all x1, starting transfers between devices, exchange(): lax.all_to_all(rows, AXES, split_axis=0, concat_axis=0, tiled=True, axis_...  11.2 us
    pallas_call x3, Pallas kernels, experts(): pl.pallas_call(functools.partial(experts_kernel, len(slots)), out_shape=t...  10.1 us
    pallas_call x2, Pallas kernels, pack(): pl.pallas_call(functools.partial(pack_kernel, plans), out_shape=tuple((ja...  6.94 us
    pallas_call x2, Pallas kernels, collect(): pl.pallas_call(collect_kernel, out_shape=jax.ShapeDtypeStruct((2, count *...  4.61 us
  transfers between devices with their start and end apart: 17, of which 8 were waited for; matrix products, arithmetic and copies ran while one was open for 0% of the time, Pallas kernels for 13%

profile of v3, /device:TPU:1, one launch (start us, length us, event | category | flops | bytes accessed | tf_op | source)
XLA Modules:
  0.0 141.5 jit_solution(10654570593029518331)
XLA Ops:
  0.0 4.3 %shard_map.55 = (bf16[2,2,160,1280]{3,2,1,0:T(8,128)(2,1)}, bf16[2,2,160,1280]{3,2,1,0:T(8,128)(2,1)}, bf16[2,2,160,1280]{3,2,1,0:T(8,128)(2,1)}) custom-call(bf16[8,160,1280]{2,1,0:T(8,128)(2,1)} %refs_0_.6, bf16[8,160,1280]{2,1,0:T(8,128)(2,1)} %refs_1_.5, bf16[8,160,1280]{2,1,0:T(8,128)(2,1)} %refs_0_.7), custom_call_target="tpu_custom_call" | custom-call | bytes 9840000 | tf_op jit(solution)/shard_map/pallas_call | solution.py:143
  4.3 2.2 %collective-permute-start.1 = (bf16[2,2,160,1280]{3,2,1,0:T(8,128)(2,1)}, bf16[2,2,160,1280]{3,2,1,0:T(8,128)(2,1)S(1)}, u32[]{:S(2)}, u32[]{:S(2)}) collective-permute-start(bf16[2,2,160,1280]{3,2,1,0:T(8,128)(2,1)} %get-tuple-element.46), channel_id=1, source_target_pairs={{0,16},{1,65},{2,18},{3,67},{4,20},{5,69},{6,22},{7,71},{8,24},{9,... | collective-permute-start | bytes 4915208 | tf_op jit(solution)/shard_map/ppermute | solution.py:63
  6.5 2.6 %collective-permute-start.2 = (bf16[2,2,160,1280]{3,2,1,0:T(8,128)(2,1)}, bf16[2,2,160,1280]{3,2,1,0:T(8,128)(2,1)}, u32[]{:S(2)}, u32[]{:S(2)}) collective-permute-start(bf16[2,2,160,1280]{3,2,1,0:T(8,128)(2,1)} %get-tuple-element.47), channel_id=1, source_target_pairs={{0,32},{1,129},{2,34},{3,131},{4,36},{5,133},{6,38},{7,135},{8,40}... | collective-permute-start | bytes 4915208 | tf_op jit(solution)/shard_map/ppermute | solution.py:63
  10.2 2.4 %shard_map.56 = (bf16[128,1280]{1,0:T(8,128)(2,1)S(1)}, bf16[128,1280]{1,0:T(8,128)(2,1)S(1)}, bf16[2,256,256]{2,1,0:T(8,128)(2,1)S(1)}) custom-call(bf16[2,256,1280]{2,1,0:T(8,128)(2,1)S(1)} %copy-done, f32[1280,128]{1,0:T(8,128)S(1)} %copy-done.1), custom_call_target="tpu_custom_call" | custom-call | flops 900000000 | bytes 3000000 | tf_op jit(solution)/shard_map/pallas_call | solution.py:107
  16.5 11.2 %all-to-all-start = ((bf16[32,8,1280]{2,1,0:T(8,128)(2,1)}), bf16[32,8,1280]{2,1,0:T(8,128)(2,1)S(1)}, u32[]{:S(2)}, u32[]{:S(2)}) async-start(bf16[32,8,1280]{2,1,0:T(8,128)(2,1)} %bitcast.1), calls=%async_computation | async-start | bytes 1310720 | tf_op jit(solution)/shard_map/all_to_all | solution.py:53
  27.7 2.7 %shard_map.60 = (bf16[1,2,160,1280]{3,2,1,0:T(8,128)(2,1)}, bf16[1,2,160,1280]{3,2,1,0:T(8,128)(2,1)}, bf16[1,2,160,1280]{3,2,1,0:T(8,128)(2,1)}) custom-call(bf16[8,160,1280]{2,1,0:T(8,128)(2,1)} %refs_0_.6, bf16[8,160,1280]{2,1,0:T(8,128)(2,1)} %refs_1_.5, bf16[8,160,1280]{2,1,0:T(8,128)(2,1)} %refs_0_.7), custom_call_target="tpu_custom_call" | custom-call | bytes 4920000 | tf_op jit(solution)/shard_map/pallas_call | solution.py:143
  31.7 2.4 %collective-permute-start.7 = (bf16[1,2,160,1280]{3,2,1,0:T(8,128)(2,1)}, bf16[1,2,160,1280]{3,2,1,0:T(8,128)(2,1)}, u32[]{:S(2)}, u32[]{:S(2)}) collective-permute-start(bf16[1,2,160,1280]{3,2,1,0:T(8,128)(2,1)} %get-tuple-element.55), channel_id=1, source_target_pairs={{0,32},{1,129},{2,34},{3,131},{4,36},{5,133},{6,38},{7,135},{8,40}... | collective-permute-start | bytes 2457608 | tf_op jit(solution)/shard_map/ppermute | solution.py:63
  35.3 14.1 %all-to-all-done = bf16[32,8,1280]{2,1,0:T(8,128)(2,1)S(1)} async-done(((bf16[32,8,1280]{2,1,0:T(8,128)(2,1)}), bf16[32,8,1280]{2,1,0:T(8,128)(2,1)S(1)}, u32[]{:S(2)}, u32[]{:S(2)}) %all-to-all-start) | async-done | bytes 655392 | tf_op jit(solution)/shard_map/all_to_all | solution.py:53
  50.7 1.8 %collective-permute-start.5 = (bf16[2,128,1280]{2,1,0:T(8,128)(2,1)S(1)}, bf16[2,128,1280]{2,1,0:T(8,128)(2,1)S(1)}, u32[]{:S(2)}, u32[]{:S(2)}) collective-permute-start(bf16[2,128,1280]{2,1,0:T(8,128)(2,1)S(1)} %shard_map.58.refs_0_), channel_id=1, source_target_pairs={{0,192},{1,49},{2,194},{3,51},{4,196},{5,53},{6,198},{7,55},{8,200... | collective-permute-start | bytes 1966088 | tf_op jit(solution)/shard_map/ppermute | solution.py:63
  52.5 2.7 %shard_map.59.refs_1_.refs_2_ = bf16[2,1280,1280]{2,1,0:T(8,128)(2,1)S(1)} custom-call(bf16[8,160,1280]{2,1,0:T(8,128)(2,1)} %refs_0_.6, bf16[8,160,1280]{2,1,0:T(8,128)(2,1)} %refs_1_.5, bf16[2,2,160,1280]{3,2,1,0:T(8,128)(2,1)S(1)} %collective-permute-done.1.refs_2_, bf16[2,2,160,1280]{3,2,1,0:T(8,128)(2,1)} %collective-permute-done.2.refs_3_, ...), custom_call_target="tpu_custom_call" | custom-call | bytes 13200000 | tf_op jit(solution)/shard_map/pallas_call | solution.py:223
  55.3 19.9 %collective-permute-done.4.refs_0_ = bf16[2,128,1280]{2,1,0:T(8,128)(2,1)S(1)} collective-permute-done((bf16[2,128,1280]{2,1,0:T(8,128)(2,1)S(1)}, bf16[2,128,1280]{2,1,0:T(8,128)(2,1)S(1)}, u32[]{:S(2)}, u32[]{:S(2)}) %collective-permute-start.4) | collective-permute-done | bytes 655392 | tf_op jit(solution)/shard_map/ppermute | solution.py:63
  75.1 2.3 %collective-permute-start.10 = (bf16[2,64,1280]{2,1,0:T(8,128)(2,1)S(1)}, bf16[2,64,1280]{2,1,0:T(8,128)(2,1)S(1)}, u32[]{:S(2)}, u32[]{:S(2)}) collective-permute-start(bf16[2,64,1280]{2,1,0:T(8,128)(2,1)S(1)} %slice.7), channel_id=1, source_target_pairs={{0,192},{1,49},{2,194},{3,51},{4,196},{5,53},{6,198},{7,55},{8,200... | collective-permute-start | bytes 983048 | tf_op jit(solution)/shard_map/ppermute | solution.py:63
  77.8 1.9 %shard_map.61.refs_2_.refs_3_ = bf16[2,640,1280]{2,1,0:T(8,128)(2,1)S(1)} custom-call(bf16[8,160,1280]{2,1,0:T(8,128)(2,1)} %refs_0_.7, bf16[1,2,160,1280]{3,2,1,0:T(8,128)(2,1)S(1)} %collective-permute-done.6.refs_1_, bf16[1,2,160,1280]{3,2,1,0:T(8,128)(2,1)} %collective-permute-done.7.refs_2_, bf16[1,2,160,1280]{3,2,1,0:T(8,128)(2,1)} %collective-permute-done.8.refs_3_), custom_call_target="tpu_custom_call" | custom-call | bytes 6600000 | tf_op jit(solution)/shard_map/pallas_call | solution.py:223
  79.6 3.4 %shard_map.63 = (bf16[2,128,1280]{2,1,0:T(8,128)(2,1)S(1)}, bf16[2,128,1280]{2,1,0:T(8,128)(2,1)S(1)}) custom-call(bf16[2,128,1280]{2,1,0:T(8,128)(2,1)S(1)} %collective-permute-done.4.refs_0_, bf16[2,128,1280]{2,1,0:T(8,128)(2,1)S(1)} %collective-permute-done.5.refs_1_, bf16[2,1280,1280]{2,1,0:T(8,128)(2,1)S(1)} %shard_map.59.refs_1_.refs_2_, ...), custom_call_target="tpu_custom_call" | custom-call | flops 2508800000 | bytes 2000000 | tf_op jit(solution)/shard_map/pallas_call | solution.py:252
  83.1 1.8 %collective-permute-done.9.refs_0_ = bf16[2,64,1280]{2,1,0:T(8,128)(2,1)S(1)} collective-permute-done((bf16[2,64,1280]{2,1,0:T(8,128)(2,1)S(1)}, bf16[2,64,1280]{2,1,0:T(8,128)(2,1)S(1)}, u32[]{:S(2)}, u32[]{:S(2)}) %collective-permute-start.9) | collective-permute-done | bytes 327712 | tf_op jit(solution)/shard_map/ppermute | solution.py:63
  84.9 3.3 %shard_map.64 = (bf16[2,64,1280]{2,1,0:T(8,128)(2,1)S(1)}, bf16[2,64,1280]{2,1,0:T(8,128)(2,1)S(1)}) custom-call(bf16[2,64,1280]{2,1,0:T(8,128)(2,1)S(1)} %collective-permute-done.9.refs_0_, bf16[2,64,1280]{2,1,0:T(8,128)(2,1)S(1)} %collective-permute-done.10.refs_1_, bf16[2,1280,1280]{2,1,0:T(8,128)(2,1)S(1)} %shard_map.59.refs_1_.refs_2_, ...), custom_call_target="tpu_custom_call" | custom-call | flops 1254400000 | bytes 2000000 | tf_op jit(solution)/shard_map/pallas_call | solution.py:252
  88.3 2.7 %collective-permute-start.12 = (bf16[2,64,1280]{2,1,0:T(8,128)(2,1)S(1)}, bf16[2,64,1280]{2,1,0:T(8,128)(2,1)S(1)}, u32[]{:S(2)}, u32[]{:S(2)}) collective-permute-start(bf16[2,64,1280]{2,1,0:T(8,128)(2,1)S(1)} %get-tuple-element.66), channel_id=1, source_target_pairs={{0,192},{1,49},{2,194},{3,51},{4,196},{5,53},{6,198},{7,55},{8,200... | collective-permute-start | bytes 983048 | tf_op jit(solution)/shard_map/ppermute | solution.py:63
  91.0 4.5 %collective-permute-done.11.x = bf16[2,64,1280]{2,1,0:T(8,128)(2,1)S(1)} collective-permute-done((bf16[2,64,1280]{2,1,0:T(8,128)(2,1)S(1)}, bf16[2,64,1280]{2,1,0:T(8,128)(2,1)S(1)}, u32[]{:S(2)}, u32[]{:S(2)}) %collective-permute-start.11) | collective-permute-done | bytes 327712 | tf_op jit(solution)/shard_map/ppermute | solution.py:63
  95.6 2.7 %collective-permute-start.13 = (bf16[2,128,1280]{2,1,0:T(8,128)(2,1)S(1)}, bf16[2,128,1280]{2,1,0:T(8,128)(2,1)S(1)}, u32[]{:S(2)}, u32[]{:S(2)}) collective-permute-start(bf16[2,128,1280]{2,1,0:T(8,128)(2,1)S(1)} %get-tuple-element.67), channel_id=1, source_target_pairs={{0,192},{1,49},{2,194},{3,51},{4,196},{5,53},{6,198},{7,55},{8,200... | collective-permute-start | bytes 1966088 | tf_op jit(solution)/shard_map/ppermute | solution.py:63
  98.4 3.3 %shard_map.62 = bf16[2,128,1280]{2,1,0:T(8,128)(2,1)S(1)} custom-call(bf16[2,128,1280]{2,1,0:T(8,128)(2,1)S(1)} %shard_map.58.refs_0_, bf16[2,1280,1280]{2,1,0:T(8,128)(2,1)S(1)} %shard_map.59.refs_1_.refs_2_, bf16[2,640,1280]{2,1,0:T(8,128)(2,1)S(1)} %shard_map.61.refs_2_.refs_3_), custom_call_target="tpu_custom_call" | custom-call | flops 1254400000 | bytes 2000000 | tf_op jit(solution)/shard_map/pallas_call | solution.py:252
  101.7 4.2 %collective-permute-done.13 = bf16[2,128,1280]{2,1,0:T(8,128)(2,1)S(1)} collective-permute-done((bf16[2,128,1280]{2,1,0:T(8,128)(2,1)S(1)}, bf16[2,128,1280]{2,1,0:T(8,128)(2,1)S(1)}, u32[]{:S(2)}, u32[]{:S(2)}) %collective-permute-start.13) | collective-permute-done | bytes 655392 | tf_op jit(solution)/shard_map/ppermute | solution.py:63
  105.9 3.4 %collective-permute-done.14 = bf16[2,128,1280]{2,1,0:T(8,128)(2,1)S(1)} collective-permute-done((bf16[2,128,1280]{2,1,0:T(8,128)(2,1)S(1)}, bf16[2,128,1280]{2,1,0:T(8,128)(2,1)S(1)}, u32[]{:S(2)}, u32[]{:S(2)}) %collective-permute-start.14) | collective-permute-done | bytes 655392 | tf_op jit(solution)/shard_map/ppermute | solution.py:63
  109.9 27.6 %all_to_all.23 = bf16[32,8,1280]{2,1,0:T(8,128)(2,1)S(1)} all-to-all(bf16[32,8,1280]{2,1,0:T(8,128)(2,1)S(1)} %bitcast.9), channel_id=1, replica_groups={{0,2,4,6,8,10,12,14,16,18,20,22,24,26,28,30,32,34,36,38,40,42,44,46,48,..., dimensions={0} | all-to-all | bytes 1310720 | tf_op jit(solution)/shard_map/all_to_all | solution.py:53
  139.9 1.6 %convolution_convert_fusion = bf16[512,1280]{1,0:T(8,128)(2,1)} fusion(bf16[512,256]{1,0:T(8,128)(2,1)S(1)} %bitcast.10, bf16[128,1280]{1,0:T(8,128)(2,1)S(1)} %collective-permute-done.15, bf16[128,1280]{1,0:T(8,128)(2,1)S(1)} %get-tuple-element.69), kind=kOutput, calls=%fused_computation | convolution fusion | flops 337510400 | bytes 2228224 | tf_op jit(solution)/shard_map/dot_general | solution.py:310
  (32 shorter events, 12.4 us)
Async XLA Ops:
  0.0 10.2 %copy-start = (bf16[2,256,1280]{2,1,0:T(8,128)(2,1)S(1)}, bf16[2,256,1280]{2,1,0:T(8,128)(2,1)}, u32[]{:S(2)}) copy-start(bf16[2,256,1280]{2,1,0:T(8,128)(2,1)} %tok_ref) | copy-start | bytes 3932164
  0.0 10.2 %copy-start.1 = (f32[1280,128]{1,0:T(8,128)S(1)}, f32[1280,128]{1,0:T(8,128)}, u32[]{:S(2)}) copy-start(f32[1280,128]{1,0:T(8,128)} %router_ref) | copy-start | bytes 1966084
  4.3 29.8 %collective-permute-start.1 = (bf16[2,2,160,1280]{3,2,1,0:T(8,128)(2,1)}, bf16[2,2,160,1280]{3,2,1,0:T(8,128)(2,1)S(1)}, u32[]{:S(2)}, u32[]{:S(2)}) collective-permute-start(bf16[2,2,160,1280]{3,2,1,0:T(8,128)(2,1)} %get-tuple-element.46), channel_id=1, source_target_pairs={{0,16},{1,65},{2,18},{3,67},{4,20},{5,69},{6,22},{7,71},{8,24},{9,... | collective-permute-start | bytes 4915208 | tf_op jit(solution)/shard_map/ppermute | solution.py:63
  6.5 42.8 %collective-permute-start.2 = (bf16[2,2,160,1280]{3,2,1,0:T(8,128)(2,1)}, bf16[2,2,160,1280]{3,2,1,0:T(8,128)(2,1)}, u32[]{:S(2)}, u32[]{:S(2)}) collective-permute-start(bf16[2,2,160,1280]{3,2,1,0:T(8,128)(2,1)} %get-tuple-element.47), channel_id=1, source_target_pairs={{0,32},{1,129},{2,34},{3,131},{4,36},{5,133},{6,38},{7,135},{8,40}... | collective-permute-start | bytes 4915208 | tf_op jit(solution)/shard_map/ppermute | solution.py:63
  9.1 40.2 %collective-permute-start.3 = (bf16[2,2,160,1280]{3,2,1,0:T(8,128)(2,1)}, bf16[2,2,160,1280]{3,2,1,0:T(8,128)(2,1)}, u32[]{:S(2)}, u32[]{:S(2)}) collective-permute-start(bf16[2,2,160,1280]{3,2,1,0:T(8,128)(2,1)} %get-tuple-element.48), channel_id=1, source_target_pairs={{0,48},{1,193},{2,50},{3,195},{4,52},{5,197},{6,54},{7,199},{8,56}... | collective-permute-start | bytes 4915208 | tf_op jit(solution)/shard_map/ppermute | solution.py:63
  12.6 2.7 %collective-permute-start = (bf16[128,1280]{1,0:T(8,128)(2,1)S(1)}, bf16[128,1280]{1,0:T(8,128)(2,1)S(1)}, u32[]{:S(2)}, u32[]{:S(2)}) collective-permute-start(bf16[128,1280]{1,0:T(8,128)(2,1)S(1)} %get-tuple-element.45), channel_id=1, source_target_pairs={{0,1},{1,0},{2,3},{3,2},{4,5},{5,4},{6,7},{7,6},{8,9},{9,8},{10,11... | collective-permute-start | bytes 983048 | tf_op jit(solution)/shard_map/ppermute | solution.py:59
  16.5 32.8 %all-to-all-start = ((bf16[32,8,1280]{2,1,0:T(8,128)(2,1)}), bf16[32,8,1280]{2,1,0:T(8,128)(2,1)S(1)}, u32[]{:S(2)}, u32[]{:S(2)}) async-start(bf16[32,8,1280]{2,1,0:T(8,128)(2,1)} %bitcast.1), calls=%async_computation | async-start | bytes 1310720 | tf_op jit(solution)/shard_map/all_to_all | solution.py:53
  30.4 47.4 %collective-permute-start.6 = (bf16[1,2,160,1280]{3,2,1,0:T(8,128)(2,1)}, bf16[1,2,160,1280]{3,2,1,0:T(8,128)(2,1)S(1)}, u32[]{:S(2)}, u32[]{:S(2)}) collective-permute-start(bf16[1,2,160,1280]{3,2,1,0:T(8,128)(2,1)} %get-tuple-element.54), channel_id=1, source_target_pairs={{0,16},{1,65},{2,18},{3,67},{4,20},{5,69},{6,22},{7,71},{8,24},{9,... | collective-permute-start | bytes 2457608 | tf_op jit(solution)/shard_map/ppermute | solution.py:63
  31.7 46.1 %collective-permute-start.7 = (bf16[1,2,160,1280]{3,2,1,0:T(8,128)(2,1)}, bf16[1,2,160,1280]{3,2,1,0:T(8,128)(2,1)}, u32[]{:S(2)}, u32[]{:S(2)}) collective-permute-start(bf16[1,2,160,1280]{3,2,1,0:T(8,128)(2,1)} %get-tuple-element.55), channel_id=1, source_target_pairs={{0,32},{1,129},{2,34},{3,131},{4,36},{5,133},{6,38},{7,135},{8,40}... | collective-permute-start | bytes 2457608 | tf_op jit(solution)/shard_map/ppermute | solution.py:63
  34.1 43.6 %collective-permute-start.8 = (bf16[1,2,160,1280]{3,2,1,0:T(8,128)(2,1)}, bf16[1,2,160,1280]{3,2,1,0:T(8,128)(2,1)}, u32[]{:S(2)}, u32[]{:S(2)}) collective-permute-start(bf16[1,2,160,1280]{3,2,1,0:T(8,128)(2,1)} %get-tuple-element.56), channel_id=1, source_target_pairs={{0,48},{1,193},{2,50},{3,195},{4,52},{5,197},{6,54},{7,199},{8,56}... | collective-permute-start | bytes 2457608 | tf_op jit(solution)/shard_map/ppermute | solution.py:63
  49.8 25.4 %collective-permute-start.4 = (bf16[2,128,1280]{2,1,0:T(8,128)(2,1)S(1)}, bf16[2,128,1280]{2,1,0:T(8,128)(2,1)S(1)}, u32[]{:S(2)}, u32[]{:S(2)}) collective-permute-start(bf16[2,128,1280]{2,1,0:T(8,128)(2,1)S(1)} %shard_map.58.refs_0_), channel_id=1, source_target_pairs={{0,64},{1,17},{2,66},{3,19},{4,68},{5,21},{6,70},{7,23},{8,72},{9,... | collective-permute-start | bytes 1966088 | tf_op jit(solution)/shard_map/ppermute | solution.py:63
  50.7 24.5 %collective-permute-start.5 = (bf16[2,128,1280]{2,1,0:T(8,128)(2,1)S(1)}, bf16[2,128,1280]{2,1,0:T(8,128)(2,1)S(1)}, u32[]{:S(2)}, u32[]{:S(2)}) collective-permute-start(bf16[2,128,1280]{2,1,0:T(8,128)(2,1)S(1)} %shard_map.58.refs_0_), channel_id=1, source_target_pairs={{0,192},{1,49},{2,194},{3,51},{4,196},{5,53},{6,198},{7,55},{8,200... | collective-permute-start | bytes 1966088 | tf_op jit(solution)/shard_map/ppermute | solution.py:63
  75.1 7.9 %collective-permute-start.10 = (bf16[2,64,1280]{2,1,0:T(8,128)(2,1)S(1)}, bf16[2,64,1280]{2,1,0:T(8,128)(2,1)S(1)}, u32[]{:S(2)}, u32[]{:S(2)}) collective-permute-start(bf16[2,64,1280]{2,1,0:T(8,128)(2,1)S(1)} %slice.7), channel_id=1, source_target_pairs={{0,192},{1,49},{2,194},{3,51},{4,196},{5,53},{6,198},{7,55},{8,200... | collective-permute-start | bytes 983048 | tf_op jit(solution)/shard_map/ppermute | solution.py:63
  77.5 7.4 %collective-permute-start.9 = (bf16[2,64,1280]{2,1,0:T(8,128)(2,1)S(1)}, bf16[2,64,1280]{2,1,0:T(8,128)(2,1)S(1)}, u32[]{:S(2)}, u32[]{:S(2)}) collective-permute-start(bf16[2,64,1280]{2,1,0:T(8,128)(2,1)S(1)} %slice.6), channel_id=1, source_target_pairs={{0,64},{1,17},{2,66},{3,19},{4,68},{5,21},{6,70},{7,23},{8,72},{9,... | collective-permute-start | bytes 983048 | tf_op jit(solution)/shard_map/ppermute | solution.py:63
  88.2 7.2 %collective-permute-start.11 = (bf16[2,64,1280]{2,1,0:T(8,128)(2,1)S(1)}, bf16[2,64,1280]{2,1,0:T(8,128)(2,1)S(1)}, u32[]{:S(2)}, u32[]{:S(2)}) collective-permute-start(bf16[2,64,1280]{2,1,0:T(8,128)(2,1)S(1)} %get-tuple-element.65), channel_id=1, source_target_pairs={{0,64},{1,17},{2,66},{3,19},{4,68},{5,21},{6,70},{7,23},{8,72},{9,... | collective-permute-start | bytes 983048 | tf_op jit(solution)/shard_map/ppermute | solution.py:63
  88.3 7.1 %collective-permute-start.12 = (bf16[2,64,1280]{2,1,0:T(8,128)(2,1)S(1)}, bf16[2,64,1280]{2,1,0:T(8,128)(2,1)S(1)}, u32[]{:S(2)}, u32[]{:S(2)}) collective-permute-start(bf16[2,64,1280]{2,1,0:T(8,128)(2,1)S(1)} %get-tuple-element.66), channel_id=1, source_target_pairs={{0,192},{1,49},{2,194},{3,51},{4,196},{5,53},{6,198},{7,55},{8,200... | collective-permute-start | bytes 983048 | tf_op jit(solution)/shard_map/ppermute | solution.py:63
  95.6 10.3 %collective-permute-start.13 = (bf16[2,128,1280]{2,1,0:T(8,128)(2,1)S(1)}, bf16[2,128,1280]{2,1,0:T(8,128)(2,1)S(1)}, u32[]{:S(2)}, u32[]{:S(2)}) collective-permute-start(bf16[2,128,1280]{2,1,0:T(8,128)(2,1)S(1)} %get-tuple-element.67), channel_id=1, source_target_pairs={{0,192},{1,49},{2,194},{3,51},{4,196},{5,53},{6,198},{7,55},{8,200... | collective-permute-start | bytes 1966088 | tf_op jit(solution)/shard_map/ppermute | solution.py:63
  98.3 10.9 %collective-permute-start.14 = (bf16[2,128,1280]{2,1,0:T(8,128)(2,1)S(1)}, bf16[2,128,1280]{2,1,0:T(8,128)(2,1)S(1)}, u32[]{:S(2)}, u32[]{:S(2)}) collective-permute-start(bf16[2,128,1280]{2,1,0:T(8,128)(2,1)S(1)} %get-tuple-element.68), channel_id=1, source_target_pairs={{0,64},{1,17},{2,66},{3,19},{4,68},{5,21},{6,70},{7,23},{8,72},{9,... | collective-permute-start | bytes 1966088 | tf_op jit(solution)/shard_map/ppermute | solution.py:63
  137.9 2.0 %collective-permute-start.15 = (bf16[128,1280]{1,0:T(8,128)(2,1)S(1)}, bf16[128,1280]{1,0:T(8,128)(2,1)S(1)}, u32[]{:S(2)}, u32[]{:S(2)}) collective-permute-start(bf16[128,1280]{1,0:T(8,128)(2,1)S(1)} %get-tuple-element.70), channel_id=1, source_target_pairs={{0,1},{1,0},{2,3},{3,2},{4,5},{5,4},{6,7},{7,6},{8,9},{9,8},{10,11... | collective-permute-start | bytes 983048 | tf_op jit(solution)/shard_map/ppermute | solution.py:59

commit v4 on v3

--- a/solution.py
+++ b/solution.py
@@ -118,6 +118,10 @@
     )(tokens, router)
 
 
+def in_hbm(arrays):
+    return [pltpu.with_memory_space_constraint(a, pltpu.HBM) for a in arrays]
+
+
 def pack_kernel(plans, *refs):
     weights, outs, (buf, in_sem, out_sem) = refs[:3], refs[3 : 3 + len(plans)], refs[3 + len(plans) :]
     p, _ = place()
@@ -155,10 +159,6 @@
     )(*in_hbm(weights))
 
 
-def in_hbm(arrays):
-    return [pltpu.with_memory_space_constraint(a, pltpu.HBM) for a in arrays]
-
-
 def reorder_kernel(source, count, *refs):
     parts, outs = refs[:count], refs[count:]
     rows = jnp.concatenate([r[...].reshape(-1, D) for r in parts], axis=0)
@@ -231,53 +231,69 @@
     )(*in_hbm(weights), *moved)
 
 
+def run_expert(rows, gu, down):
+    gu = lax.dot_general(rows, gu, (((1,), (1,)), ((), ())), preferred_element_type=F32)
+    gate, up = gu[:, : 4 * HS], gu[:, 4 * HS :]
+    act = (gate / (1.0 + jnp.exp(-gate)) * up).astype(BF16)
+    return jnp.dot(act, down(), preferred_element_type=F32).astype(BF16)
+
+
 def experts_kernel(count, *refs):
-    slots, (gu_ref, wd_ref), outs = refs[:count], refs[count : count + 2], refs[count + 2 :]
+    slots, (gu_ref, wd_ref, out) = refs[:count], refs[count:]
     for j in range(2):
         rows = jnp.concatenate([s[j] for s in slots], axis=0)
-        gu = lax.dot_general(
-            rows, gu_ref[j], (((1,), (1,)), ((), ())), preferred_element_type=F32
-        )
-        gate, up = gu[:, : 4 * HS], gu[:, 4 * HS :]
-        act = (gate / (1.0 + jnp.exp(-gate)) * up).astype(BF16)
-        out = jnp.dot(act, wd_ref[j], preferred_element_type=F32).astype(BF16)
-        start = 0
-        for o in outs:
-            o[j] = out[start : start + o.shape[1]]
-            start += o.shape[1]
+        out[j] = run_expert(rows, gu_ref[j], lambda j=j: wd_ref[j])
 
 
 def experts(slots, gu, down):
-    rows = sum(2 * s.shape[1] for s in slots)
     return pl.pallas_call(
         functools.partial(experts_kernel, len(slots)),
-        out_shape=tuple(jax.ShapeDtypeStruct(s.shape, BF16) for s in slots),
+        out_shape=jax.ShapeDtypeStruct((2, 128, D), BF16),
         in_specs=[pl.BlockSpec(memory_space=pltpu.VMEM)] * (len(slots) + 2),
-        out_specs=(pl.BlockSpec(memory_space=pltpu.VMEM),) * len(slots),
+        out_specs=pl.BlockSpec(memory_space=pltpu.VMEM),
         compiler_params=pltpu.CompilerParams(vmem_limit_bytes=24 * 2**20),
         cost_estimate=pl.CostEstimate(
-            flops=rows * 4_900_000, bytes_accessed=2_000_000, transcendentals=rows * 1280
+            flops=1_260_000_000, bytes_accessed=2_000_000, transcendentals=327680
         ),
     )(*slots, gu, down)
 
 
-def merge_kernel(o1, o3, x, y, out1, out3):
-    half = x.shape[1]
-    out3[:, :half] = (o3[:, :half].astype(F32) + x[...].astype(F32)).astype(BF16)
-    out3[:, half:] = o3[:, half:]
-    out1[:, :half] = o1[:, :half]
-    out1[:, half:] = (o1[:, half:].astype(F32) + y[...].astype(F32)).astype(BF16)
-
-
-def merge(o1, o3, x, y):
-    return pl.pallas_call(
-        merge_kernel,
-        out_shape=(jax.ShapeDtypeStruct(o1.shape, BF16),) * 2,
-        in_specs=[pl.BlockSpec(memory_space=pltpu.VMEM)] * 4,
-        out_specs=(pl.BlockSpec(memory_space=pltpu.VMEM),) * 2,
-        compiler_params=pltpu.CompilerParams(vmem_limit_bytes=8 * 2**20),
-        cost_estimate=pl.CostEstimate(flops=400_000, bytes_accessed=3_000_000, transcendentals=0),
-    )(o1, o3, x, y)
+def first_kernel(sa, sb, gu_ref, wd, d1, d2, d3, oa, ob, down_ref, sems):
+    p, _ = place()
+    copies = []
+    for j in range(2):
+        for k, src in enumerate((wd.at[2 * p + j], d1.at[0, j], d2.at[0, j], d3.at[0, j])):
+            dst = down_ref.at[j, pl.ds(k * HS, HS)]
+            copies.append(pltpu.make_async_copy(src, dst, sems.at[j, k]))
+    for c in copies:
+        c.start()
+
+    for j in range(2):
+
+        def down(j=j):
+            for c in copies[4 * j : 4 * (j + 1)]:
+                c.wait()
+            return down_ref[j]
+
+        out = run_expert(jnp.concatenate([sa[j], sb[j]], axis=0), gu_ref[j], down)
+        oa[j] = out[:128]
+        ob[j] = out[128:]
+
+
+def first_experts(slots, gu, w_down, downs):
+    out = jax.ShapeDtypeStruct((2, 128, D), BF16)
+    vmem, anywhere = pl.BlockSpec(memory_space=pltpu.VMEM), pl.BlockSpec(memory_space=pl.ANY)
+    return pl.pallas_call(
+        first_kernel,
+        out_shape=(out, out, jax.ShapeDtypeStruct((2, 4 * HS, D), BF16)),
+        in_specs=[vmem] * 3 + [anywhere] * 4,
+        out_specs=(vmem,) * 3,
+        scratch_shapes=[pltpu.SemaphoreType.DMA((2, 4))],
+        compiler_params=pltpu.CompilerParams(vmem_limit_bytes=24 * 2**20),
+        cost_estimate=pl.CostEstimate(
+            flops=2_520_000_000, bytes_accessed=9_000_000, transcendentals=655360
+        ),
+    )(*slots, gu, *in_hbm((w_down,)), *downs)
 
 
 def body(tokens, router, w_gate, w_up, w_down):
@@ -295,15 +311,14 @@
     gu = collect((w_gate, w_up), ups)
     s1, s3, gu = lax.optimization_barrier((s1, s3, gu))
     far = shift(s1[:, :64], False, 1), shift(s3[:, 64:], False, 3)
-    down = collect((w_down,), downs)
-    o1, o3 = experts((s1, s3), gu, down)
-    far, o1, o3 = lax.optimization_barrier((far, o1, o3))
-    low, high = experts(far, gu, down)
-    x, y = shift(low, False, 1), shift(high, False, 3)
-    (o0,) = experts((s0,), gu, down)
-    o1, o3 = merge(o1, o3, x, y)
+    o1, o3, down = first_experts((s1, s3), gu, w_down, downs)
     t1, t3 = shift(o1, False, 3), shift(o3, False, 1)
-    total = o0.astype(F32) + t1.astype(F32) + t3.astype(F32)
+    *far, _, _ = lax.optimization_barrier((*far, o1, o3))
+    o2 = experts(far, gu, down)
+    t2 = shift(o2, False, 2)
+    s0, _, _ = lax.optimization_barrier((s0, t1, t3))
+    o0 = experts((s0,), gu, down)
+    total = o0.astype(F32) + t1.astype(F32) + t2.astype(F32) + t3.astype(F32)
     (rows,) = reorder((total.astype(BF16),), undeal, ((ROWS, D),))
     mine, other = reorder((exchange(rows),), unweave, ((128, D),) * 2)
     rows = jnp.concatenate([mine, swap(other)], axis=0)

time: 142 us -> 137 us (0.965)
  waiting for transfers between devices: 50.3 us -> 48 us
  blocking collectives: 27.6 us -> 25.6 us
    ppermute x2, starting transfers between devices: 2.18 us -> 4.59 us  [swap(): return lax.ppermute(value, 'expert', [(e, e ^ 1) for e in range(16)])]
    ppermute x14 -> x13, waiting for transfers between devices: 33.7 us -> 31.4 us  [shift(): return lax.ppermute(value, AXES, shift_pairs(along_p, by))]
    ppermute x14 -> x13, starting transfers between devices: 21.6 us -> 19.4 us  [shift(): return lax.ppermute(value, AXES, shift_pairs(along_p, by))]
    all_to_all x1, blocking collectives: 27.6 us -> 25.6 us  [exchange(): lax.all_to_all(rows, AXES, split_axis=0, concat_axis=0, tiled=True, axis_...]
    pallas_call x2 -> x1, Pallas kernels: 4.61 us -> 2.75 us  [collect(): pl.pallas_call(collect_kernel, out_shape=jax.ShapeDtypeStruct((2, count *...]
    pallas_call x4 -> x3, Pallas kernels: 10.3 us -> 11 us  [the longest x2 6.67 us: experts(): pl.pallas_call(functools.partial(experts_kernel, len(slots)), out_shape=j...]
  transfers between devices with their start and end apart: 17 -> 16, of which waited for: 8 -> 5; matrix products, arithmetic and copies ran while one was open for 0% -> 0% of each run, Pallas kernels for 13% -> 15%
where the time goes in v4:
time: 137 us; the launch traced here: 136 us
  waiting for transfers between devices  48 us (35%)
  starting transfers between devices  35.2 us (26%)
  blocking collectives  25.6 us (19%)
  Pallas kernels  25.4 us (19%)
  matrix products  1.56 us (1%)
    ppermute x13, waiting for transfers between devices, shift(): return lax.ppermute(value, AXES, shift_pairs(along_p, by))  31.4 us
    all_to_all x1, blocking collectives, exchange(): lax.all_to_all(rows, AXES, split_axis=0, concat_axis=0, tiled=True, axis_...  25.6 us
    ppermute x13, starting transfers between devices, shift(): return lax.ppermute(value, AXES, shift_pairs(along_p, by))  19.4 us
    all_to_all x1, waiting for transfers between devices, exchange(): lax.all_to_all(rows, AXES, split_axis=0, concat_axis=0, tiled=True, axis_...  14.1 us
    all_to_all x1, starting transfers between devices, exchange(): lax.all_to_all(rows, AXES, split_axis=0, concat_axis=0, tiled=True, axis_...  11.2 us
    pallas_call x2, Pallas kernels, pack(): pl.pallas_call(functools.partial(pack_kernel, plans), out_shape=tuple((ja...  6.94 us
    pallas_call x2, Pallas kernels, experts(): pl.pallas_call(functools.partial(experts_kernel, len(slots)), out_shape=j...  6.67 us
    ppermute x2, starting transfers between devices, swap(): return lax.ppermute(value, 'expert', [(e, e ^ 1) for e in range(16)])  4.59 us
  transfers between devices with their start and end apart: 16, of which 5 were waited for; matrix products, arithmetic and copies ran while one was open for 0% of the time, Pallas kernels for 15%

profile of v4, /device:TPU:1, one launch (start us, length us, event | category | flops | bytes accessed | tf_op | source)
XLA Modules:
  0.0 136.3 jit_solution(8984431282589839730)
XLA Ops:
  0.0 4.3 %shard_map.55 = (bf16[2,2,160,1280]{3,2,1,0:T(8,128)(2,1)}, bf16[2,2,160,1280]{3,2,1,0:T(8,128)(2,1)}, bf16[2,2,160,1280]{3,2,1,0:T(8,128)(2,1)}) custom-call(bf16[8,160,1280]{2,1,0:T(8,128)(2,1)} %refs_0_.5, bf16[8,160,1280]{2,1,0:T(8,128)(2,1)} %refs_1_.5, bf16[8,160,1280]{2,1,0:T(8,128)(2,1)} %wd.1), custom_call_target="tpu_custom_call" | custom-call | bytes 9840000 | tf_op jit(solution)/shard_map/pallas_call | solution.py:147
  4.3 2.2 %collective-permute-start.1 = (bf16[2,2,160,1280]{3,2,1,0:T(8,128)(2,1)}, bf16[2,2,160,1280]{3,2,1,0:T(8,128)(2,1)S(1)}, u32[]{:S(2)}, u32[]{:S(2)}) collective-permute-start(bf16[2,2,160,1280]{3,2,1,0:T(8,128)(2,1)} %get-tuple-element.42), channel_id=1, source_target_pairs={{0,16},{1,65},{2,18},{3,67},{4,20},{5,69},{6,22},{7,71},{8,24},{9,... | collective-permute-start | bytes 4915208 | tf_op jit(solution)/shard_map/ppermute | solution.py:63
  6.5 2.6 %collective-permute-start.2 = (bf16[2,2,160,1280]{3,2,1,0:T(8,128)(2,1)}, bf16[2,2,160,1280]{3,2,1,0:T(8,128)(2,1)}, u32[]{:S(2)}, u32[]{:S(2)}) collective-permute-start(bf16[2,2,160,1280]{3,2,1,0:T(8,128)(2,1)} %get-tuple-element.43), channel_id=1, source_target_pairs={{0,32},{1,129},{2,34},{3,131},{4,36},{5,133},{6,38},{7,135},{8,40}... | collective-permute-start | bytes 4915208 | tf_op jit(solution)/shard_map/ppermute | solution.py:63
  10.2 2.4 %shard_map.56 = (bf16[128,1280]{1,0:T(8,128)(2,1)S(1)}, bf16[128,1280]{1,0:T(8,128)(2,1)S(1)}, bf16[2,256,256]{2,1,0:T(8,128)(2,1)S(1)}) custom-call(bf16[2,256,1280]{2,1,0:T(8,128)(2,1)S(1)} %copy-done, f32[1280,128]{1,0:T(8,128)S(1)} %copy-done.1), custom_call_target="tpu_custom_call" | custom-call | flops 900000000 | bytes 3000000 | tf_op jit(solution)/shard_map/pallas_call | solution.py:107
  12.6 1.4 %collective-permute-start = (bf16[128,1280]{1,0:T(8,128)(2,1)S(1)}, bf16[128,1280]{1,0:T(8,128)(2,1)S(1)}, u32[]{:S(2)}, u32[]{:S(2)}) collective-permute-start(bf16[128,1280]{1,0:T(8,128)(2,1)S(1)} %get-tuple-element.41), channel_id=1, source_target_pairs={{0,1},{1,0},{2,3},{3,2},{4,5},{5,4},{6,7},{7,6},{8,9},{9,8},{10,11... | collective-permute-start | bytes 983048 | tf_op jit(solution)/shard_map/ppermute | solution.py:59
  14.0 1.3 collective-permute-done.refs_1_
  16.5 11.2 %all-to-all-start = ((bf16[32,8,1280]{2,1,0:T(8,128)(2,1)}), bf16[32,8,1280]{2,1,0:T(8,128)(2,1)S(1)}, u32[]{:S(2)}, u32[]{:S(2)}) async-start(bf16[32,8,1280]{2,1,0:T(8,128)(2,1)} %bitcast.1), calls=%async_computation | async-start | bytes 1310720 | tf_op jit(solution)/shard_map/all_to_all | solution.py:53
  27.7 2.6 %shard_map.60 = (bf16[1,2,160,1280]{3,2,1,0:T(8,128)(2,1)}, bf16[1,2,160,1280]{3,2,1,0:T(8,128)(2,1)}, bf16[1,2,160,1280]{3,2,1,0:T(8,128)(2,1)}) custom-call(bf16[8,160,1280]{2,1,0:T(8,128)(2,1)} %refs_0_.5, bf16[8,160,1280]{2,1,0:T(8,128)(2,1)} %refs_1_.5, bf16[8,160,1280]{2,1,0:T(8,128)(2,1)} %wd.1), custom_call_target="tpu_custom_call" | custom-call | bytes 4920000 | tf_op jit(solution)/shard_map/pallas_call | solution.py:147
  30.4 1.3 collective-permute-start.6
  31.7 2.4 %collective-permute-start.7 = (bf16[1,2,160,1280]{3,2,1,0:T(8,128)(2,1)}, bf16[1,2,160,1280]{3,2,1,0:T(8,128)(2,1)}, u32[]{:S(2)}, u32[]{:S(2)}) collective-permute-start(bf16[1,2,160,1280]{3,2,1,0:T(8,128)(2,1)} %get-tuple-element.53), channel_id=1, source_target_pairs={{0,32},{1,129},{2,34},{3,131},{4,36},{5,133},{6,38},{7,135},{8,40}... | collective-permute-start | bytes 2457608 | tf_op jit(solution)/shard_map/ppermute | solution.py:63
  35.3 14.1 %all-to-all-done = bf16[32,8,1280]{2,1,0:T(8,128)(2,1)S(1)} async-done(((bf16[32,8,1280]{2,1,0:T(8,128)(2,1)}), bf16[32,8,1280]{2,1,0:T(8,128)(2,1)S(1)}, u32[]{:S(2)}, u32[]{:S(2)}) %all-to-all-start) | async-done | bytes 655392 | tf_op jit(solution)/shard_map/all_to_all | solution.py:53
  50.7 1.8 %collective-permute-start.5 = (bf16[2,128,1280]{2,1,0:T(8,128)(2,1)S(1)}, bf16[2,128,1280]{2,1,0:T(8,128)(2,1)S(1)}, u32[]{:S(2)}, u32[]{:S(2)}) collective-permute-start(bf16[2,128,1280]{2,1,0:T(8,128)(2,1)S(1)} %shard_map.58.refs_0_), channel_id=1, source_target_pairs={{0,192},{1,49},{2,194},{3,51},{4,196},{5,53},{6,198},{7,55},{8,200... | collective-permute-start | bytes 1966088 | tf_op jit(solution)/shard_map/ppermute | solution.py:63
  52.5 2.7 %shard_map.59.gu_ref.refs_1_.refs_2_ = bf16[2,1280,1280]{2,1,0:T(8,128)(2,1)S(1)} custom-call(bf16[8,160,1280]{2,1,0:T(8,128)(2,1)} %refs_0_.5, bf16[8,160,1280]{2,1,0:T(8,128)(2,1)} %refs_1_.5, bf16[2,2,160,1280]{3,2,1,0:T(8,128)(2,1)S(1)} %collective-permute-done.1.refs_2_, bf16[2,2,160,1280]{3,2,1,0:T(8,128)(2,1)} %collective-permute-done.2.refs_3_, ...), custom_call_target="tpu_custom_call" | custom-call | bytes 13200000 | tf_op jit(solution)/shard_map/pallas_call | solution.py:223
  55.3 19.9 %collective-permute-done.4.sa = bf16[2,128,1280]{2,1,0:T(8,128)(2,1)S(1)} collective-permute-done((bf16[2,128,1280]{2,1,0:T(8,128)(2,1)S(1)}, bf16[2,128,1280]{2,1,0:T(8,128)(2,1)S(1)}, u32[]{:S(2)}, u32[]{:S(2)}) %collective-permute-start.4) | collective-permute-done | bytes 655392 | tf_op jit(solution)/shard_map/ppermute | solution.py:63
  75.4 2.8 %collective-permute-start.12 = (bf16[2,64,1280]{2,1,0:T(8,128)(2,1)S(1)}, bf16[2,64,1280]{2,1,0:T(8,128)(2,1)S(1)}, u32[]{:S(2)}, u32[]{:S(2)}) collective-permute-start(bf16[2,64,1280]{2,1,0:T(8,128)(2,1)S(1)} %slice.7), channel_id=1, source_target_pairs={{0,192},{1,49},{2,194},{3,51},{4,196},{5,53},{6,198},{7,55},{8,200... | collective-permute-start | bytes 983048 | tf_op jit(solution)/shard_map/ppermute | solution.py:63
  78.2 4.3 %shard_map.61 = (bf16[2,128,1280]{2,1,0:T(8,128)(2,1)S(1)}, bf16[2,128,1280]{2,1,0:T(8,128)(2,1)S(1)}, bf16[2,640,1280]{2,1,0:T(8,128)(2,1)S(1)}) custom-call(bf16[2,128,1280]{2,1,0:T(8,128)(2,1)S(1)} %collective-permute-done.4.sa, bf16[2,128,1280]{2,1,0:T(8,128)(2,1)S(1)} %collective-permute-done.5.sb, ...), custom_call_target="tpu_custom_call" | custom-call | flops 2520000000 | bytes 9000000 | tf_op jit(solution)/shard_map/pallas_call | solution.py:286
  82.6 2.7 %collective-permute-start.9 = (bf16[2,128,1280]{2,1,0:T(8,128)(2,1)S(1)}, bf16[2,128,1280]{2,1,0:T(8,128)(2,1)S(1)}, u32[]{:S(2)}, u32[]{:S(2)}) collective-permute-start(bf16[2,128,1280]{2,1,0:T(8,128)(2,1)S(1)} %get-tuple-element.55), channel_id=1, source_target_pairs={{0,192},{1,49},{2,194},{3,51},{4,196},{5,53},{6,198},{7,55},{8,200... | collective-permute-start | bytes 1966088 | tf_op jit(solution)/shard_map/ppermute | solution.py:63
  85.3 3.3 %shard_map.63 = bf16[2,128,1280]{2,1,0:T(8,128)(2,1)S(1)} custom-call(bf16[2,64,1280]{2,1,0:T(8,128)(2,1)S(1)} %collective-permute-done.11.refs_0_, bf16[2,64,1280]{2,1,0:T(8,128)(2,1)S(1)} %collective-permute-done.12.refs_1_, bf16[2,1280,1280]{2,1,0:T(8,128)(2,1)S(1)} %shard_map.59.gu_ref.refs_1_.refs_2_, ...), custom_call_target="tpu_custom_call" | custom-call | flops 1260000000 | bytes 2000000 | tf_op jit(solution)/shard_map/pallas_call | solution.py:249
  88.7 11.5 %collective-permute-done.10 = bf16[2,128,1280]{2,1,0:T(8,128)(2,1)S(1)} collective-permute-done((bf16[2,128,1280]{2,1,0:T(8,128)(2,1)S(1)}, bf16[2,128,1280]{2,1,0:T(8,128)(2,1)S(1)}, u32[]{:S(2)}, u32[]{:S(2)}) %collective-permute-start.10) | collective-permute-done | bytes 655392 | tf_op jit(solution)/shard_map/ppermute | solution.py:63
  100.3 3.3 %shard_map.62 = bf16[2,128,1280]{2,1,0:T(8,128)(2,1)S(1)} custom-call(bf16[2,128,1280]{2,1,0:T(8,128)(2,1)S(1)} %shard_map.58.refs_0_, bf16[2,1280,1280]{2,1,0:T(8,128)(2,1)S(1)} %shard_map.59.gu_ref.refs_1_.refs_2_, bf16[2,640,1280]{2,1,0:T(8,128)(2,1)S(1)} %get-tuple-element.58.refs_2_.refs_3_), custom_call_target="tpu_custom_call" | custom-call | flops 1260000000 | bytes 2000000 | tf_op jit(solution)/shard_map/pallas_call | solution.py:249
  104.3 25.6 %all_to_all.23 = bf16[32,8,1280]{2,1,0:T(8,128)(2,1)S(1)} all-to-all(bf16[32,8,1280]{2,1,0:T(8,128)(2,1)S(1)} %bitcast.9), channel_id=1, replica_groups={{0,2,4,6,8,10,12,14,16,18,20,22,24,26,28,30,32,34,36,38,40,42,44,46,48,..., dimensions={0} | all-to-all | bytes 1310720 | tf_op jit(solution)/shard_map/all_to_all | solution.py:53
  130.3 3.2 %collective-permute-start.14 = (bf16[128,1280]{1,0:T(8,128)(2,1)S(1)}, bf16[128,1280]{1,0:T(8,128)(2,1)S(1)}, u32[]{:S(2)}, u32[]{:S(2)}) collective-permute-start(bf16[128,1280]{1,0:T(8,128)(2,1)S(1)} %get-tuple-element.62), channel_id=1, source_target_pairs={{0,1},{1,0},{2,3},{3,2},{4,5},{5,4},{6,7},{7,6},{8,9},{9,8},{10,11... | collective-permute-start | bytes 983048 | tf_op jit(solution)/shard_map/ppermute | solution.py:59
  133.5 1.3 collective-permute-done.14
  134.7 1.6 %convolution_convert_fusion = bf16[512,1280]{1,0:T(8,128)(2,1)} fusion(bf16[512,256]{1,0:T(8,128)(2,1)S(1)} %bitcast.10, bf16[128,1280]{1,0:T(8,128)(2,1)S(1)} %collective-permute-done.14, bf16[128,1280]{1,0:T(8,128)(2,1)S(1)} %get-tuple-element.61), kind=kOutput, calls=%fused_computation | convolution fusion | flops 337510400 | bytes 2228224 | tf_op jit(solution)/shard_map/dot_general | solution.py:325
  (28 shorter events, 6.3 us)
Async XLA Ops:
  0.0 10.2 %copy-start = (bf16[2,256,1280]{2,1,0:T(8,128)(2,1)S(1)}, bf16[2,256,1280]{2,1,0:T(8,128)(2,1)}, u32[]{:S(2)}) copy-start(bf16[2,256,1280]{2,1,0:T(8,128)(2,1)} %tok_ref) | copy-start | bytes 3932164
  0.0 10.2 %copy-start.1 = (f32[1280,128]{1,0:T(8,128)S(1)}, f32[1280,128]{1,0:T(8,128)}, u32[]{:S(2)}) copy-start(f32[1280,128]{1,0:T(8,128)} %router_ref) | copy-start | bytes 1966084
  4.3 29.8 %collective-permute-start.1 = (bf16[2,2,160,1280]{3,2,1,0:T(8,128)(2,1)}, bf16[2,2,160,1280]{3,2,1,0:T(8,128)(2,1)S(1)}, u32[]{:S(2)}, u32[]{:S(2)}) collective-permute-start(bf16[2,2,160,1280]{3,2,1,0:T(8,128)(2,1)} %get-tuple-element.42), channel_id=1, source_target_pairs={{0,16},{1,65},{2,18},{3,67},{4,20},{5,69},{6,22},{7,71},{8,24},{9,... | collective-permute-start | bytes 4915208 | tf_op jit(solution)/shard_map/ppermute | solution.py:63
  6.5 42.8 %collective-permute-start.2 = (bf16[2,2,160,1280]{3,2,1,0:T(8,128)(2,1)}, bf16[2,2,160,1280]{3,2,1,0:T(8,128)(2,1)}, u32[]{:S(2)}, u32[]{:S(2)}) collective-permute-start(bf16[2,2,160,1280]{3,2,1,0:T(8,128)(2,1)} %get-tuple-element.43), channel_id=1, source_target_pairs={{0,32},{1,129},{2,34},{3,131},{4,36},{5,133},{6,38},{7,135},{8,40}... | collective-permute-start | bytes 4915208 | tf_op jit(solution)/shard_map/ppermute | solution.py:63
  9.1 40.2 %collective-permute-start.3 = (bf16[2,2,160,1280]{3,2,1,0:T(8,128)(2,1)}, bf16[2,2,160,1280]{3,2,1,0:T(8,128)(2,1)}, u32[]{:S(2)}, u32[]{:S(2)}) collective-permute-start(bf16[2,2,160,1280]{3,2,1,0:T(8,128)(2,1)} %get-tuple-element.44), channel_id=1, source_target_pairs={{0,48},{1,193},{2,50},{3,195},{4,52},{5,197},{6,54},{7,199},{8,56}... | collective-permute-start | bytes 4915208 | tf_op jit(solution)/shard_map/ppermute | solution.py:63
  12.6 2.7 %collective-permute-start = (bf16[128,1280]{1,0:T(8,128)(2,1)S(1)}, bf16[128,1280]{1,0:T(8,128)(2,1)S(1)}, u32[]{:S(2)}, u32[]{:S(2)}) collective-permute-start(bf16[128,1280]{1,0:T(8,128)(2,1)S(1)} %get-tuple-element.41), channel_id=1, source_target_pairs={{0,1},{1,0},{2,3},{3,2},{4,5},{5,4},{6,7},{7,6},{8,9},{9,8},{10,11... | collective-permute-start | bytes 983048 | tf_op jit(solution)/shard_map/ppermute | solution.py:59
  16.5 32.8 %all-to-all-start = ((bf16[32,8,1280]{2,1,0:T(8,128)(2,1)}), bf16[32,8,1280]{2,1,0:T(8,128)(2,1)S(1)}, u32[]{:S(2)}, u32[]{:S(2)}) async-start(bf16[32,8,1280]{2,1,0:T(8,128)(2,1)} %bitcast.1), calls=%async_computation | async-start | bytes 1310720 | tf_op jit(solution)/shard_map/all_to_all | solution.py:53
  30.4 47.8 %collective-permute-start.6 = (bf16[1,2,160,1280]{3,2,1,0:T(8,128)(2,1)}, bf16[1,2,160,1280]{3,2,1,0:T(8,128)(2,1)S(1)}, u32[]{:S(2)}, u32[]{:S(2)}) collective-permute-start(bf16[1,2,160,1280]{3,2,1,0:T(8,128)(2,1)} %get-tuple-element.52), channel_id=1, source_target_pairs={{0,16},{1,65},{2,18},{3,67},{4,20},{5,69},{6,22},{7,71},{8,24},{9,... | collective-permute-start | bytes 2457608 | tf_op jit(solution)/shard_map/ppermute | solution.py:63
  31.7 46.5 %collective-permute-start.7 = (bf16[1,2,160,1280]{3,2,1,0:T(8,128)(2,1)}, bf16[1,2,160,1280]{3,2,1,0:T(8,128)(2,1)}, u32[]{:S(2)}, u32[]{:S(2)}) collective-permute-start(bf16[1,2,160,1280]{3,2,1,0:T(8,128)(2,1)} %get-tuple-element.53), channel_id=1, source_target_pairs={{0,32},{1,129},{2,34},{3,131},{4,36},{5,133},{6,38},{7,135},{8,40}... | collective-permute-start | bytes 2457608 | tf_op jit(solution)/shard_map/ppermute | solution.py:63
  34.1 44.1 %collective-permute-start.8 = (bf16[1,2,160,1280]{3,2,1,0:T(8,128)(2,1)}, bf16[1,2,160,1280]{3,2,1,0:T(8,128)(2,1)}, u32[]{:S(2)}, u32[]{:S(2)}) collective-permute-start(bf16[1,2,160,1280]{3,2,1,0:T(8,128)(2,1)} %get-tuple-element.54), channel_id=1, source_target_pairs={{0,48},{1,193},{2,50},{3,195},{4,52},{5,197},{6,54},{7,199},{8,56}... | collective-permute-start | bytes 2457608 | tf_op jit(solution)/shard_map/ppermute | solution.py:63
  49.8 25.4 %collective-permute-start.4 = (bf16[2,128,1280]{2,1,0:T(8,128)(2,1)S(1)}, bf16[2,128,1280]{2,1,0:T(8,128)(2,1)S(1)}, u32[]{:S(2)}, u32[]{:S(2)}) collective-permute-start(bf16[2,128,1280]{2,1,0:T(8,128)(2,1)S(1)} %shard_map.58.refs_0_), channel_id=1, source_target_pairs={{0,64},{1,17},{2,66},{3,19},{4,68},{5,21},{6,70},{7,23},{8,72},{9,... | collective-permute-start | bytes 1966088 | tf_op jit(solution)/shard_map/ppermute | solution.py:63
  50.7 24.5 %collective-permute-start.5 = (bf16[2,128,1280]{2,1,0:T(8,128)(2,1)S(1)}, bf16[2,128,1280]{2,1,0:T(8,128)(2,1)S(1)}, u32[]{:S(2)}, u32[]{:S(2)}) collective-permute-start(bf16[2,128,1280]{2,1,0:T(8,128)(2,1)S(1)} %shard_map.58.refs_0_), channel_id=1, source_target_pairs={{0,192},{1,49},{2,194},{3,51},{4,196},{5,53},{6,198},{7,55},{8,200... | collective-permute-start | bytes 1966088 | tf_op jit(solution)/shard_map/ppermute | solution.py:63
  75.2 10.1 %collective-permute-start.11 = (bf16[2,64,1280]{2,1,0:T(8,128)(2,1)S(1)}, bf16[2,64,1280]{2,1,0:T(8,128)(2,1)S(1)}, u32[]{:S(2)}, u32[]{:S(2)}) collective-permute-start(bf16[2,64,1280]{2,1,0:T(8,128)(2,1)S(1)} %slice.6), channel_id=1, source_target_pairs={{0,64},{1,17},{2,66},{3,19},{4,68},{5,21},{6,70},{7,23},{8,72},{9,... | collective-permute-start | bytes 983048 | tf_op jit(solution)/shard_map/ppermute | solution.py:63
  75.4 9.9 %collective-permute-start.12 = (bf16[2,64,1280]{2,1,0:T(8,128)(2,1)S(1)}, bf16[2,64,1280]{2,1,0:T(8,128)(2,1)S(1)}, u32[]{:S(2)}, u32[]{:S(2)}) collective-permute-start(bf16[2,64,1280]{2,1,0:T(8,128)(2,1)S(1)} %slice.7), channel_id=1, source_target_pairs={{0,192},{1,49},{2,194},{3,51},{4,196},{5,53},{6,198},{7,55},{8,200... | collective-permute-start | bytes 983048 | tf_op jit(solution)/shard_map/ppermute | solution.py:63
  82.5 17.7 %collective-permute-start.10 = (bf16[2,128,1280]{2,1,0:T(8,128)(2,1)S(1)}, bf16[2,128,1280]{2,1,0:T(8,128)(2,1)S(1)}, u32[]{:S(2)}, u32[]{:S(2)}) collective-permute-start(bf16[2,128,1280]{2,1,0:T(8,128)(2,1)S(1)} %get-tuple-element.56), channel_id=1, source_target_pairs={{0,64},{1,17},{2,66},{3,19},{4,68},{5,21},{6,70},{7,23},{8,72},{9,... | collective-permute-start | bytes 1966088 | tf_op jit(solution)/shard_map/ppermute | solution.py:63
  82.6 17.7 %collective-permute-start.9 = (bf16[2,128,1280]{2,1,0:T(8,128)(2,1)S(1)}, bf16[2,128,1280]{2,1,0:T(8,128)(2,1)S(1)}, u32[]{:S(2)}, u32[]{:S(2)}) collective-permute-start(bf16[2,128,1280]{2,1,0:T(8,128)(2,1)S(1)} %get-tuple-element.55), channel_id=1, source_target_pairs={{0,192},{1,49},{2,194},{3,51},{4,196},{5,53},{6,198},{7,55},{8,200... | collective-permute-start | bytes 1966088 | tf_op jit(solution)/shard_map/ppermute | solution.py:63
  88.6 15.0 %collective-permute-start.13 = (bf16[2,128,1280]{2,1,0:T(8,128)(2,1)S(1)}, bf16[2,128,1280]{2,1,0:T(8,128)(2,1)S(1)}, u32[]{:S(2)}, u32[]{:S(2)}) collective-permute-start(bf16[2,128,1280]{2,1,0:T(8,128)(2,1)S(1)} %shard_map.63), channel_id=1, source_target_pairs={{0,128},{1,33},{2,130},{3,35},{4,132},{5,37},{6,134},{7,39},{8,136... | collective-permute-start | bytes 1966088 | tf_op jit(solution)/shard_map/ppermute | solution.py:63
  130.3 4.4 %collective-permute-start.14 = (bf16[128,1280]{1,0:T(8,128)(2,1)S(1)}, bf16[128,1280]{1,0:T(8,128)(2,1)S(1)}, u32[]{:S(2)}, u32[]{:S(2)}) collective-permute-start(bf16[128,1280]{1,0:T(8,128)(2,1)S(1)} %get-tuple-element.62), channel_id=1, source_target_pairs={{0,1},{1,0},{2,3},{3,2},{4,5},{5,4},{6,7},{7,6},{8,9},{9,8},{10,11... | collective-permute-start | bytes 983048 | tf_op jit(solution)/shard_map/ppermute | solution.py:59

commit v5 on v4

--- a/solution.py
+++ b/solution.py
@@ -159,9 +159,14 @@
     )(*in_hbm(weights))
 
 
-def reorder_kernel(source, count, *refs):
-    parts, outs = refs[:count], refs[count:]
+def reorder_kernel(source, count, added, *refs):
+    parts, terms, outs = refs[:count], refs[count : count + added], refs[count + added :]
     rows = jnp.concatenate([r[...].reshape(-1, D) for r in parts], axis=0)
+    if terms:
+        rows = rows.astype(F32)
+        for t in terms:
+            rows = rows + t[...].reshape(-1, D).astype(F32)
+        rows = rows.astype(BF16)
     moved = lax.dot_general(
         one_hot(source(columns(ROWS)), ROWS),
         rows,
@@ -175,15 +180,15 @@
         start += size
 
 
-def reorder(parts, source, shapes):
-    return pl.pallas_call(
-        functools.partial(reorder_kernel, source, len(parts)),
+def reorder(parts, source, shapes, terms=()):
+    return pl.pallas_call(
+        functools.partial(reorder_kernel, source, len(parts), len(terms)),
         out_shape=tuple(jax.ShapeDtypeStruct(shape, BF16) for shape in shapes),
-        in_specs=[pl.BlockSpec(memory_space=pltpu.VMEM)] * len(parts),
+        in_specs=[pl.BlockSpec(memory_space=pltpu.VMEM)] * (len(parts) + len(terms)),
         out_specs=(pl.BlockSpec(memory_space=pltpu.VMEM),) * len(shapes),
         compiler_params=pltpu.CompilerParams(vmem_limit_bytes=16 * 2**20),
         cost_estimate=pl.CostEstimate(flops=170_000_000, bytes_accessed=1_300_000, transcendentals=0),
-    )(*parts)
+    )(*parts, *terms)
 
 
 def weave(n):
@@ -238,24 +243,40 @@
     return jnp.dot(act, down(), preferred_element_type=F32).astype(BF16)
 
 
-def experts_kernel(count, *refs):
-    slots, (gu_ref, wd_ref, out) = refs[:count], refs[count:]
+def experts_kernel(far_low, far_high, own, gu_ref, wd_ref, far_out, own_out):
     for j in range(2):
-        rows = jnp.concatenate([s[j] for s in slots], axis=0)
-        out[j] = run_expert(rows, gu_ref[j], lambda j=j: wd_ref[j])
+        rows = jnp.concatenate([far_low[j], far_high[j], own[j]], axis=0)
+        out = run_expert(rows, gu_ref[j], lambda j=j: wd_ref[j])
+        far_out[j] = out[:128]
+        own_out[j] = out[128:]
 
 
 def experts(slots, gu, down):
     return pl.pallas_call(
-        functools.partial(experts_kernel, len(slots)),
-        out_shape=jax.ShapeDtypeStruct((2, 128, D), BF16),
-        in_specs=[pl.BlockSpec(memory_space=pltpu.VMEM)] * (len(slots) + 2),
-        out_specs=pl.BlockSpec(memory_space=pltpu.VMEM),
+        experts_kernel,
+        out_shape=(jax.ShapeDtypeStruct((2, 128, D), BF16),) * 2,
+        in_specs=[pl.BlockSpec(memory_space=pltpu.VMEM)] * 5,
+        out_specs=(pl.BlockSpec(memory_space=pltpu.VMEM),) * 2,
         compiler_params=pltpu.CompilerParams(vmem_limit_bytes=24 * 2**20),
         cost_estimate=pl.CostEstimate(
             flops=1_260_000_000, bytes_accessed=2_000_000, transcendentals=327680
         ),
     )(*slots, gu, down)
+
+
+def add_kernel(a, b, c, out):
+    out[...] = a[...].astype(F32) + b[...].astype(F32) + c[...].astype(F32)
+
+
+def add(a, b, c):
+    return pl.pallas_call(
+        add_kernel,
+        out_shape=jax.ShapeDtypeStruct(a.shape, F32),
+        in_specs=[pl.BlockSpec(memory_space=pltpu.VMEM)] * 3,
+        out_specs=pl.BlockSpec(memory_space=pltpu.VMEM),
+        compiler_params=pltpu.CompilerParams(vmem_limit_bytes=16 * 2**20),
+        cost_estimate=pl.CostEstimate(flops=1_260_000_000, bytes_accessed=3_300_000, transcendentals=0),
+    )(a, b, c)
 
 
 def first_kernel(sa, sb, gu_ref, wd, d1, d2, d3, oa, ob, down_ref, sems):
@@ -314,12 +335,10 @@
     o1, o3, down = first_experts((s1, s3), gu, w_down, downs)
     t1, t3 = shift(o1, False, 3), shift(o3, False, 1)
     *far, _, _ = lax.optimization_barrier((*far, o1, o3))
-    o2 = experts(far, gu, down)
+    o2, o0 = experts((*far, s0), gu, down)
     t2 = shift(o2, False, 2)
-    s0, _, _ = lax.optimization_barrier((s0, t1, t3))
-    o0 = experts((s0,), gu, down)
-    total = o0.astype(F32) + t1.astype(F32) + t2.astype(F32) + t3.astype(F32)
-    (rows,) = reorder((total.astype(BF16),), undeal, ((ROWS, D),))
+    partial = add(o0, t1, t3)
+    (rows,) = reorder((partial,), undeal, ((ROWS, D),), (t2,))
     mine, other = reorder((exchange(rows),), unweave, ((128, D),) * 2)
     rows = jnp.concatenate([mine, swap(other)], axis=0)
     mixed = jnp.dot(comb.reshape(2 * TOK, ROWS), rows, preferred_element_type=F32)

time: 137 us -> 135 us (0.985)
  blocking collectives: 25.6 us -> 21.6 us
  starting transfers between devices: 35.2 us -> 38.5 us
  Pallas kernels: 25.4 us -> 22.4 us
  waiting for transfers between devices: 48 us -> 50.1 us
    ppermute x2, starting transfers between devices: 4.59 us -> 9.7 us  [swap(): return lax.ppermute(value, 'expert', [(e, e ^ 1) for e in range(16)])]
    all_to_all x1, blocking collectives: 25.6 us -> 21.6 us  [exchange(): lax.all_to_all(rows, AXES, split_axis=0, concat_axis=0, tiled=True, axis_...]
    pallas_call x6, Pallas kernels: 9.05 us -> 6.04 us  [the longest x1 3.43 us: experts(): pl.pallas_call(experts_kernel, out_shape=(jax.ShapeDtypeStruct((2, 128, D...]
    ppermute x13, starting transfers between devices: 19.4 us -> 17.6 us  [shift(): return lax.ppermute(value, AXES, shift_pairs(along_p, by))]
    ppermute x13, waiting for transfers between devices: 31.4 us -> 32.9 us  [shift(): return lax.ppermute(value, AXES, shift_pairs(along_p, by))]
  transfers between devices with their start and end apart: 16 -> 16, of which waited for: 5 -> 6; matrix products, arithmetic and copies ran while one was open for 0% -> 0% of each run, Pallas kernels for 15% -> 13%
where the time goes in v5:
time: 135 us; the launch traced here: 134 us
  waiting for transfers between devices  50.1 us (37%)
  starting transfers between devices  38.5 us (29%)
  Pallas kernels  22.4 us (17%)
  blocking collectives  21.6 us (16%)
  matrix products  1.56 us (1%)
    ppermute x13, waiting for transfers between devices, shift(): return lax.ppermute(value, AXES, shift_pairs(along_p, by))  32.9 us
    all_to_all x1, blocking collectives, exchange(): lax.all_to_all(rows, AXES, split_axis=0, concat_axis=0, tiled=True, axis_...  21.6 us
    ppermute x13, starting transfers between devices, shift(): return lax.ppermute(value, AXES, shift_pairs(along_p, by))  17.6 us
    all_to_all x1, waiting for transfers between devices, exchange(): lax.all_to_all(rows, AXES, split_axis=0, concat_axis=0, tiled=True, axis_...  14.6 us
    all_to_all x1, starting transfers between devices, exchange(): lax.all_to_all(rows, AXES, split_axis=0, concat_axis=0, tiled=True, axis_...  11.2 us
    ppermute x2, starting transfers between devices, swap(): return lax.ppermute(value, 'expert', [(e, e ^ 1) for e in range(16)])  9.7 us
    pallas_call x2, Pallas kernels, pack(): pl.pallas_call(functools.partial(pack_kernel, plans), out_shape=tuple((ja...  6.95 us
    pallas_call x1, Pallas kernels, first_experts(): pl.pallas_call(first_kernel, out_shape=(out, out, jax.ShapeDtypeStruct((2...  4.31 us
  transfers between devices with their start and end apart: 16, of which 6 were waited for; matrix products, arithmetic and copies ran while one was open for 0% of the time, Pallas kernels for 13%

profile of v5, /device:TPU:1, one launch (start us, length us, event | category | flops | bytes accessed | tf_op | source)
XLA Modules:
  0.0 134.4 jit_solution(14685033039409869059)
XLA Ops:
  0.0 4.3 %shard_map.55 = (bf16[2,2,160,1280]{3,2,1,0:T(8,128)(2,1)}, bf16[2,2,160,1280]{3,2,1,0:T(8,128)(2,1)}, bf16[2,2,160,1280]{3,2,1,0:T(8,128)(2,1)}) custom-call(bf16[8,160,1280]{2,1,0:T(8,128)(2,1)} %refs_0_.5, bf16[8,160,1280]{2,1,0:T(8,128)(2,1)} %refs_1_.5, bf16[8,160,1280]{2,1,0:T(8,128)(2,1)} %wd.1), custom_call_target="tpu_custom_call" | custom-call | bytes 9840000 | tf_op jit(solution)/shard_map/pallas_call | solution.py:147
  4.3 2.2 %collective-permute-start.1 = (bf16[2,2,160,1280]{3,2,1,0:T(8,128)(2,1)}, bf16[2,2,160,1280]{3,2,1,0:T(8,128)(2,1)S(1)}, u32[]{:S(2)}, u32[]{:S(2)}) collective-permute-start(bf16[2,2,160,1280]{3,2,1,0:T(8,128)(2,1)} %get-tuple-element.43), channel_id=1, source_target_pairs={{0,16},{1,65},{2,18},{3,67},{4,20},{5,69},{6,22},{7,71},{8,24},{9,... | collective-permute-start | bytes 4915208 | tf_op jit(solution)/shard_map/ppermute | solution.py:63
  6.5 2.6 %collective-permute-start.2 = (bf16[2,2,160,1280]{3,2,1,0:T(8,128)(2,1)}, bf16[2,2,160,1280]{3,2,1,0:T(8,128)(2,1)}, u32[]{:S(2)}, u32[]{:S(2)}) collective-permute-start(bf16[2,2,160,1280]{3,2,1,0:T(8,128)(2,1)} %get-tuple-element.44), channel_id=1, source_target_pairs={{0,32},{1,129},{2,34},{3,131},{4,36},{5,133},{6,38},{7,135},{8,40}... | collective-permute-start | bytes 4915208 | tf_op jit(solution)/shard_map/ppermute | solution.py:63
  10.2 2.4 %shard_map.56 = (bf16[128,1280]{1,0:T(8,128)(2,1)S(1)}, bf16[128,1280]{1,0:T(8,128)(2,1)S(1)}, bf16[2,256,256]{2,1,0:T(8,128)(2,1)S(1)}) custom-call(bf16[2,256,1280]{2,1,0:T(8,128)(2,1)S(1)} %copy-done, f32[1280,128]{1,0:T(8,128)S(1)} %copy-done.1), custom_call_target="tpu_custom_call" | custom-call | flops 900000000 | bytes 3000000 | tf_op jit(solution)/shard_map/pallas_call | solution.py:107
  12.6 1.4 %collective-permute-start = (bf16[128,1280]{1,0:T(8,128)(2,1)S(1)}, bf16[128,1280]{1,0:T(8,128)(2,1)S(1)}, u32[]{:S(2)}, u32[]{:S(2)}) collective-permute-start(bf16[128,1280]{1,0:T(8,128)(2,1)S(1)} %get-tuple-element.42), channel_id=1, source_target_pairs={{0,1},{1,0},{2,3},{3,2},{4,5},{5,4},{6,7},{7,6},{8,9},{9,8},{10,11... | collective-permute-start | bytes 983048 | tf_op jit(solution)/shard_map/ppermute | solution.py:59
  14.0 1.3 collective-permute-done.refs_1_
  16.5 11.2 %all-to-all-start = ((bf16[32,8,1280]{2,1,0:T(8,128)(2,1)}), bf16[32,8,1280]{2,1,0:T(8,128)(2,1)S(1)}, u32[]{:S(2)}, u32[]{:S(2)}) async-start(bf16[32,8,1280]{2,1,0:T(8,128)(2,1)} %bitcast.1), calls=%async_computation | async-start | bytes 1310720 | tf_op jit(solution)/shard_map/all_to_all | solution.py:53
  27.7 2.7 %shard_map.60 = (bf16[1,2,160,1280]{3,2,1,0:T(8,128)(2,1)}, bf16[1,2,160,1280]{3,2,1,0:T(8,128)(2,1)}, bf16[1,2,160,1280]{3,2,1,0:T(8,128)(2,1)}) custom-call(bf16[8,160,1280]{2,1,0:T(8,128)(2,1)} %refs_0_.5, bf16[8,160,1280]{2,1,0:T(8,128)(2,1)} %refs_1_.5, bf16[8,160,1280]{2,1,0:T(8,128)(2,1)} %wd.1), custom_call_target="tpu_custom_call" | custom-call | bytes 4920000 | tf_op jit(solution)/shard_map/pallas_call | solution.py:147
  30.4 2.6 %collective-permute-start.10 = (bf16[1,2,160,1280]{3,2,1,0:T(8,128)(2,1)}, bf16[1,2,160,1280]{3,2,1,0:T(8,128)(2,1)S(1)}, u32[]{:S(2)}, u32[]{:S(2)}) collective-permute-start(bf16[1,2,160,1280]{3,2,1,0:T(8,128)(2,1)} %get-tuple-element.55), channel_id=1, source_target_pairs={{0,48},{1,193},{2,50},{3,195},{4,52},{5,197},{6,54},{7,199},{8,56}... | collective-permute-start | bytes 2457608 | tf_op jit(solution)/shard_map/ppermute | solution.py:63
  33.0 1.7 %collective-permute-start.9 = (bf16[1,2,160,1280]{3,2,1,0:T(8,128)(2,1)}, bf16[1,2,160,1280]{3,2,1,0:T(8,128)(2,1)}, u32[]{:S(2)}, u32[]{:S(2)}) collective-permute-start(bf16[1,2,160,1280]{3,2,1,0:T(8,128)(2,1)} %get-tuple-element.54), channel_id=1, source_target_pairs={{0,32},{1,129},{2,34},{3,131},{4,36},{5,133},{6,38},{7,135},{8,40}... | collective-permute-start | bytes 2457608 | tf_op jit(solution)/shard_map/ppermute | solution.py:63
  34.7 14.6 %all-to-all-done = bf16[32,8,1280]{2,1,0:T(8,128)(2,1)S(1)} async-done(((bf16[32,8,1280]{2,1,0:T(8,128)(2,1)}), bf16[32,8,1280]{2,1,0:T(8,128)(2,1)S(1)}, u32[]{:S(2)}, u32[]{:S(2)}) %all-to-all-start) | async-done | bytes 655392 | tf_op jit(solution)/shard_map/all_to_all | solution.py:53
  50.7 1.8 %collective-permute-start.5 = (bf16[2,128,1280]{2,1,0:T(8,128)(2,1)S(1)}, bf16[2,128,1280]{2,1,0:T(8,128)(2,1)S(1)}, u32[]{:S(2)}, u32[]{:S(2)}) collective-permute-start(bf16[2,128,1280]{2,1,0:T(8,128)(2,1)S(1)} %shard_map.58.own), channel_id=1, source_target_pairs={{0,192},{1,49},{2,194},{3,51},{4,196},{5,53},{6,198},{7,55},{8,200... | collective-permute-start | bytes 1966088 | tf_op jit(solution)/shard_map/ppermute | solution.py:63
  52.5 2.7 %shard_map.59.gu_ref = bf16[2,1280,1280]{2,1,0:T(8,128)(2,1)S(1)} custom-call(bf16[8,160,1280]{2,1,0:T(8,128)(2,1)} %refs_0_.5, bf16[8,160,1280]{2,1,0:T(8,128)(2,1)} %refs_1_.5, bf16[2,2,160,1280]{3,2,1,0:T(8,128)(2,1)S(1)} %collective-permute-done.1.refs_2_, bf16[2,2,160,1280]{3,2,1,0:T(8,128)(2,1)} %collective-permute-done.2.refs_3_, ...), custom_call_target="tpu_custom_call" | custom-call | bytes 13200000 | tf_op jit(solution)/shard_map/pallas_call | solution.py:228
  55.3 19.9 %collective-permute-done.4.sa = bf16[2,128,1280]{2,1,0:T(8,128)(2,1)S(1)} collective-permute-done((bf16[2,128,1280]{2,1,0:T(8,128)(2,1)S(1)}, bf16[2,128,1280]{2,1,0:T(8,128)(2,1)S(1)}, u32[]{:S(2)}, u32[]{:S(2)}) %collective-permute-start.4) | collective-permute-done | bytes 655392 | tf_op jit(solution)/shard_map/ppermute | solution.py:63
  75.3 2.9 %collective-permute-start.7 = (bf16[2,64,1280]{2,1,0:T(8,128)(2,1)S(1)}, bf16[2,64,1280]{2,1,0:T(8,128)(2,1)S(1)}, u32[]{:S(2)}, u32[]{:S(2)}) collective-permute-start(bf16[2,64,1280]{2,1,0:T(8,128)(2,1)S(1)} %slice.7), channel_id=1, source_target_pairs={{0,192},{1,49},{2,194},{3,51},{4,196},{5,53},{6,198},{7,55},{8,200... | collective-permute-start | bytes 983048 | tf_op jit(solution)/shard_map/ppermute | solution.py:63
  78.2 4.3 %shard_map.61 = (bf16[2,128,1280]{2,1,0:T(8,128)(2,1)S(1)}, bf16[2,128,1280]{2,1,0:T(8,128)(2,1)S(1)}, bf16[2,640,1280]{2,1,0:T(8,128)(2,1)S(1)}) custom-call(bf16[2,128,1280]{2,1,0:T(8,128)(2,1)S(1)} %collective-permute-done.4.sa, bf16[2,128,1280]{2,1,0:T(8,128)(2,1)S(1)} %collective-permute-done.5.sb, bf16[2,1280,1280]{2,1,0:T(8,128)(2,1)S(1)} %shard_map.59.gu_ref, ...), custom_call_target="tpu_custom_call" | custom-call | flops 2520000000 | bytes 9000000 | tf_op jit(solution)/shard_map/pallas_call | solution.py:307
  82.6 1.4 %collective-permute-start.12 = (bf16[2,128,1280]{2,1,0:T(8,128)(2,1)S(1)}, bf16[2,128,1280]{2,1,0:T(8,128)(2,1)S(1)}, u32[]{:S(2)}, u32[]{:S(2)}) collective-permute-start(bf16[2,128,1280]{2,1,0:T(8,128)(2,1)S(1)} %get-tuple-element.57), channel_id=1, source_target_pairs={{0,64},{1,17},{2,66},{3,19},{4,68},{5,21},{6,70},{7,23},{8,72},{9,... | collective-permute-start | bytes 1966088 | tf_op jit(solution)/shard_map/ppermute | solution.py:63
  84.1 3.4 %shard_map.62 = (bf16[2,128,1280]{2,1,0:T(8,128)(2,1)S(1)}, bf16[2,128,1280]{2,1,0:T(8,128)(2,1)S(1)}) custom-call(bf16[2,64,1280]{2,1,0:T(8,128)(2,1)S(1)} %collective-permute-done.6.far_low, bf16[2,64,1280]{2,1,0:T(8,128)(2,1)S(1)} %collective-permute-done.7.far_high, bf16[2,128,1280]{2,1,0:T(8,128)(2,1)S(1)} %shard_map.58.own, ...), custom_call_target="tpu_custom_call" | custom-call | flops 1260000000 | bytes 2000000 | tf_op jit(solution)/shard_map/pallas_call | solution.py:255
  87.6 4.7 %collective-permute-done.11.b = bf16[2,128,1280]{2,1,0:T(8,128)(2,1)S(1)} collective-permute-done((bf16[2,128,1280]{2,1,0:T(8,128)(2,1)S(1)}, bf16[2,128,1280]{2,1,0:T(8,128)(2,1)S(1)}, u32[]{:S(2)}, u32[]{:S(2)}) %collective-permute-start.11) | collective-permute-done | bytes 655392 | tf_op jit(solution)/shard_map/ppermute | solution.py:63
  92.3 8.3 %collective-permute-done.12.c = bf16[2,128,1280]{2,1,0:T(8,128)(2,1)S(1)} collective-permute-done((bf16[2,128,1280]{2,1,0:T(8,128)(2,1)S(1)}, bf16[2,128,1280]{2,1,0:T(8,128)(2,1)S(1)}, u32[]{:S(2)}, u32[]{:S(2)}) %collective-permute-start.12) | collective-permute-done | bytes 655392 | tf_op jit(solution)/shard_map/ppermute | solution.py:63
  101.3 21.6 %all_to_all.23 = bf16[32,8,1280]{2,1,0:T(8,128)(2,1)S(1)} all-to-all(bf16[32,8,1280]{2,1,0:T(8,128)(2,1)S(1)} %bitcast.7), channel_id=1, replica_groups={{0,2,4,6,8,10,12,14,16,18,20,22,24,26,28,30,32,34,36,38,40,42,44,46,48,..., dimensions={0} | all-to-all | bytes 1310720 | tf_op jit(solution)/shard_map/all_to_all | solution.py:53
  123.3 8.3 %collective-permute-start.14 = (bf16[128,1280]{1,0:T(8,128)(2,1)S(1)}, bf16[128,1280]{1,0:T(8,128)(2,1)S(1)}, u32[]{:S(2)}, u32[]{:S(2)}) collective-permute-start(bf16[128,1280]{1,0:T(8,128)(2,1)S(1)} %get-tuple-element.64), channel_id=1, source_target_pairs={{0,1},{1,0},{2,3},{3,2},{4,5},{5,4},{6,7},{7,6},{8,9},{9,8},{10,11... | collective-permute-start | bytes 983048 | tf_op jit(solution)/shard_map/ppermute | solution.py:59
  131.6 1.3 collective-permute-done.14
  132.8 1.6 %convolution_convert_fusion = bf16[512,1280]{1,0:T(8,128)(2,1)} fusion(bf16[512,256]{1,0:T(8,128)(2,1)S(1)} %bitcast.10, bf16[128,1280]{1,0:T(8,128)(2,1)S(1)} %collective-permute-done.14, bf16[128,1280]{1,0:T(8,128)(2,1)S(1)} %get-tuple-element.63), kind=kOutput, calls=%fused_computation | convolution fusion | flops 337510400 | bytes 2228224 | tf_op jit(solution)/shard_map/dot_general | solution.py:344
  (27 shorter events, 5.0 us)
Async XLA Ops:
  0.0 10.2 %copy-start = (bf16[2,256,1280]{2,1,0:T(8,128)(2,1)S(1)}, bf16[2,256,1280]{2,1,0:T(8,128)(2,1)}, u32[]{:S(2)}) copy-start(bf16[2,256,1280]{2,1,0:T(8,128)(2,1)} %tok_ref) | copy-start | bytes 3932164
  0.0 10.2 %copy-start.1 = (f32[1280,128]{1,0:T(8,128)S(1)}, f32[1280,128]{1,0:T(8,128)}, u32[]{:S(2)}) copy-start(f32[1280,128]{1,0:T(8,128)} %router_ref) | copy-start | bytes 1966084
  4.3 28.7 %collective-permute-start.1 = (bf16[2,2,160,1280]{3,2,1,0:T(8,128)(2,1)}, bf16[2,2,160,1280]{3,2,1,0:T(8,128)(2,1)S(1)}, u32[]{:S(2)}, u32[]{:S(2)}) collective-permute-start(bf16[2,2,160,1280]{3,2,1,0:T(8,128)(2,1)} %get-tuple-element.43), channel_id=1, source_target_pairs={{0,16},{1,65},{2,18},{3,67},{4,20},{5,69},{6,22},{7,71},{8,24},{9,... | collective-permute-start | bytes 4915208 | tf_op jit(solution)/shard_map/ppermute | solution.py:63
  6.5 42.8 %collective-permute-start.2 = (bf16[2,2,160,1280]{3,2,1,0:T(8,128)(2,1)}, bf16[2,2,160,1280]{3,2,1,0:T(8,128)(2,1)}, u32[]{:S(2)}, u32[]{:S(2)}) collective-permute-start(bf16[2,2,160,1280]{3,2,1,0:T(8,128)(2,1)} %get-tuple-element.44), channel_id=1, source_target_pairs={{0,32},{1,129},{2,34},{3,131},{4,36},{5,133},{6,38},{7,135},{8,40}... | collective-permute-start | bytes 4915208 | tf_op jit(solution)/shard_map/ppermute | solution.py:63
  9.1 40.2 %collective-permute-start.3 = (bf16[2,2,160,1280]{3,2,1,0:T(8,128)(2,1)}, bf16[2,2,160,1280]{3,2,1,0:T(8,128)(2,1)}, u32[]{:S(2)}, u32[]{:S(2)}) collective-permute-start(bf16[2,2,160,1280]{3,2,1,0:T(8,128)(2,1)} %get-tuple-element.45), channel_id=1, source_target_pairs={{0,48},{1,193},{2,50},{3,195},{4,52},{5,197},{6,54},{7,199},{8,56}... | collective-permute-start | bytes 4915208 | tf_op jit(solution)/shard_map/ppermute | solution.py:63
  12.6 2.7 %collective-permute-start = (bf16[128,1280]{1,0:T(8,128)(2,1)S(1)}, bf16[128,1280]{1,0:T(8,128)(2,1)S(1)}, u32[]{:S(2)}, u32[]{:S(2)}) collective-permute-start(bf16[128,1280]{1,0:T(8,128)(2,1)S(1)} %get-tuple-element.42), channel_id=1, source_target_pairs={{0,1},{1,0},{2,3},{3,2},{4,5},{5,4},{6,7},{7,6},{8,9},{9,8},{10,11... | collective-permute-start | bytes 983048 | tf_op jit(solution)/shard_map/ppermute | solution.py:59
  16.5 32.8 %all-to-all-start = ((bf16[32,8,1280]{2,1,0:T(8,128)(2,1)}), bf16[32,8,1280]{2,1,0:T(8,128)(2,1)S(1)}, u32[]{:S(2)}, u32[]{:S(2)}) async-start(bf16[32,8,1280]{2,1,0:T(8,128)(2,1)} %bitcast.1), calls=%async_computation | async-start | bytes 1310720 | tf_op jit(solution)/shard_map/all_to_all | solution.py:53
  30.4 47.8 %collective-permute-start.10 = (bf16[1,2,160,1280]{3,2,1,0:T(8,128)(2,1)}, bf16[1,2,160,1280]{3,2,1,0:T(8,128)(2,1)S(1)}, u32[]{:S(2)}, u32[]{:S(2)}) collective-permute-start(bf16[1,2,160,1280]{3,2,1,0:T(8,128)(2,1)} %get-tuple-element.55), channel_id=1, source_target_pairs={{0,48},{1,193},{2,50},{3,195},{4,52},{5,197},{6,54},{7,199},{8,56}... | collective-permute-start | bytes 2457608 | tf_op jit(solution)/shard_map/ppermute | solution.py:63
  33.0 45.2 %collective-permute-start.8 = (bf16[1,2,160,1280]{3,2,1,0:T(8,128)(2,1)}, bf16[1,2,160,1280]{3,2,1,0:T(8,128)(2,1)}, u32[]{:S(2)}, u32[]{:S(2)}) collective-permute-start(bf16[1,2,160,1280]{3,2,1,0:T(8,128)(2,1)} %get-tuple-element.53), channel_id=1, source_target_pairs={{0,16},{1,65},{2,18},{3,67},{4,20},{5,69},{6,22},{7,71},{8,24},{9,... | collective-permute-start | bytes 2457608 | tf_op jit(solution)/shard_map/ppermute | solution.py:63
  33.0 45.2 %collective-permute-start.9 = (bf16[1,2,160,1280]{3,2,1,0:T(8,128)(2,1)}, bf16[1,2,160,1280]{3,2,1,0:T(8,128)(2,1)}, u32[]{:S(2)}, u32[]{:S(2)}) collective-permute-start(bf16[1,2,160,1280]{3,2,1,0:T(8,128)(2,1)} %get-tuple-element.54), channel_id=1, source_target_pairs={{0,32},{1,129},{2,34},{3,131},{4,36},{5,133},{6,38},{7,135},{8,40}... | collective-permute-start | bytes 2457608 | tf_op jit(solution)/shard_map/ppermute | solution.py:63
  49.8 25.4 %collective-permute-start.4 = (bf16[2,128,1280]{2,1,0:T(8,128)(2,1)S(1)}, bf16[2,128,1280]{2,1,0:T(8,128)(2,1)S(1)}, u32[]{:S(2)}, u32[]{:S(2)}) collective-permute-start(bf16[2,128,1280]{2,1,0:T(8,128)(2,1)S(1)} %shard_map.58.own), channel_id=1, source_target_pairs={{0,64},{1,17},{2,66},{3,19},{4,68},{5,21},{6,70},{7,23},{8,72},{9,... | collective-permute-start | bytes 1966088 | tf_op jit(solution)/shard_map/ppermute | solution.py:63
  50.7 24.5 %collective-permute-start.5 = (bf16[2,128,1280]{2,1,0:T(8,128)(2,1)S(1)}, bf16[2,128,1280]{2,1,0:T(8,128)(2,1)S(1)}, u32[]{:S(2)}, u32[]{:S(2)}) collective-permute-start(bf16[2,128,1280]{2,1,0:T(8,128)(2,1)S(1)} %shard_map.58.own), channel_id=1, source_target_pairs={{0,192},{1,49},{2,194},{3,51},{4,196},{5,53},{6,198},{7,55},{8,200... | collective-permute-start | bytes 1966088 | tf_op jit(solution)/shard_map/ppermute | solution.py:63
  75.2 8.9 %collective-permute-start.6 = (bf16[2,64,1280]{2,1,0:T(8,128)(2,1)S(1)}, bf16[2,64,1280]{2,1,0:T(8,128)(2,1)S(1)}, u32[]{:S(2)}, u32[]{:S(2)}) collective-permute-start(bf16[2,64,1280]{2,1,0:T(8,128)(2,1)S(1)} %slice.6), channel_id=1, source_target_pairs={{0,64},{1,17},{2,66},{3,19},{4,68},{5,21},{6,70},{7,23},{8,72},{9,... | collective-permute-start | bytes 983048 | tf_op jit(solution)/shard_map/ppermute | solution.py:63
  75.3 8.8 %collective-permute-start.7 = (bf16[2,64,1280]{2,1,0:T(8,128)(2,1)S(1)}, bf16[2,64,1280]{2,1,0:T(8,128)(2,1)S(1)}, u32[]{:S(2)}, u32[]{:S(2)}) collective-permute-start(bf16[2,64,1280]{2,1,0:T(8,128)(2,1)S(1)} %slice.7), channel_id=1, source_target_pairs={{0,192},{1,49},{2,194},{3,51},{4,196},{5,53},{6,198},{7,55},{8,200... | collective-permute-start | bytes 983048 | tf_op jit(solution)/shard_map/ppermute | solution.py:63
  82.5 9.8 %collective-permute-start.11 = (bf16[2,128,1280]{2,1,0:T(8,128)(2,1)S(1)}, bf16[2,128,1280]{2,1,0:T(8,128)(2,1)S(1)}, u32[]{:S(2)}, u32[]{:S(2)}) collective-permute-start(bf16[2,128,1280]{2,1,0:T(8,128)(2,1)S(1)} %get-tuple-element.56), channel_id=1, source_target_pairs={{0,192},{1,49},{2,194},{3,51},{4,196},{5,53},{6,198},{7,55},{8,200... | collective-permute-start | bytes 1966088 | tf_op jit(solution)/shard_map/ppermute | solution.py:63
  82.6 18.0 %collective-permute-start.12 = (bf16[2,128,1280]{2,1,0:T(8,128)(2,1)S(1)}, bf16[2,128,1280]{2,1,0:T(8,128)(2,1)S(1)}, u32[]{:S(2)}, u32[]{:S(2)}) collective-permute-start(bf16[2,128,1280]{2,1,0:T(8,128)(2,1)S(1)} %get-tuple-element.57), channel_id=1, source_target_pairs={{0,64},{1,17},{2,66},{3,19},{4,68},{5,21},{6,70},{7,23},{8,72},{9,... | collective-permute-start | bytes 1966088 | tf_op jit(solution)/shard_map/ppermute | solution.py:63
  87.5 13.4 %collective-permute-start.13 = (bf16[2,128,1280]{2,1,0:T(8,128)(2,1)S(1)}, bf16[2,128,1280]{2,1,0:T(8,128)(2,1)S(1)}, u32[]{:S(2)}, u32[]{:S(2)}) collective-permute-start(bf16[2,128,1280]{2,1,0:T(8,128)(2,1)S(1)} %get-tuple-element.62), channel_id=1, source_target_pairs={{0,128},{1,33},{2,130},{3,35},{4,132},{5,37},{6,134},{7,39},{8,136... | collective-permute-start | bytes 1966088 | tf_op jit(solution)/shard_map/ppermute | solution.py:63
  123.3 9.5 %collective-permute-start.14 = (bf16[128,1280]{1,0:T(8,128)(2,1)S(1)}, bf16[128,1280]{1,0:T(8,128)(2,1)S(1)}, u32[]{:S(2)}, u32[]{:S(2)}) collective-permute-start(bf16[128,1280]{1,0:T(8,128)(2,1)S(1)} %get-tuple-element.64), channel_id=1, source_target_pairs={{0,1},{1,0},{2,3},{3,2},{4,5},{5,4},{6,7},{7,6},{8,9},{9,8},{10,11... | collective-permute-start | bytes 983048 | tf_op jit(solution)/shard_map/ppermute | solution.py:59

commit v6 on v5

--- a/solution.py
+++ b/solution.py
@@ -236,17 +236,17 @@
     )(*in_hbm(weights), *moved)
 
 
-def run_expert(rows, gu, down):
+def run_up(rows, gu):
     gu = lax.dot_general(rows, gu, (((1,), (1,)), ((), ())), preferred_element_type=F32)
     gate, up = gu[:, : 4 * HS], gu[:, 4 * HS :]
-    act = (gate / (1.0 + jnp.exp(-gate)) * up).astype(BF16)
-    return jnp.dot(act, down(), preferred_element_type=F32).astype(BF16)
+    return (gate / (1.0 + jnp.exp(-gate)) * up).astype(BF16)
 
 
 def experts_kernel(far_low, far_high, own, gu_ref, wd_ref, far_out, own_out):
     for j in range(2):
         rows = jnp.concatenate([far_low[j], far_high[j], own[j]], axis=0)
-        out = run_expert(rows, gu_ref[j], lambda j=j: wd_ref[j])
+        act = run_up(rows, gu_ref[j])
+        out = jnp.dot(act, wd_ref[j], preferred_element_type=F32).astype(BF16)
         far_out[j] = out[:128]
         own_out[j] = out[128:]
 
@@ -279,7 +279,25 @@
     )(a, b, c)
 
 
-def first_kernel(sa, sb, gu_ref, wd, d1, d2, d3, oa, ob, down_ref, sems):
+def up_kernel(sa, sb, gu_ref, act_ref):
+    for j in range(2):
+        act_ref[j] = run_up(jnp.concatenate([sa[j], sb[j]], axis=0), gu_ref[j])
+
+
+def up_half(sa, sb, gu):
+    return pl.pallas_call(
+        up_kernel,
+        out_shape=jax.ShapeDtypeStruct((2, 256, 4 * HS), BF16),
+        in_specs=[pl.BlockSpec(memory_space=pltpu.VMEM)] * 3,
+        out_specs=pl.BlockSpec(memory_space=pltpu.VMEM),
+        compiler_params=pltpu.CompilerParams(vmem_limit_bytes=16 * 2**20),
+        cost_estimate=pl.CostEstimate(
+            flops=0, bytes_accessed=0, transcendentals=0
+        ),
+    )(sa, sb, gu)
+
+
+def down_kernel(act, wd, d1, d3, d2, oa, ob, down_ref, sems):
     p, _ = place()
     copies = []
     for j in range(2):
@@ -288,51 +306,45 @@
             copies.append(pltpu.make_async_copy(src, dst, sems.at[j, k]))
     for c in copies:
         c.start()
-
-    for j in range(2):
-
-        def down(j=j):
-            for c in copies[4 * j : 4 * (j + 1)]:
-                c.wait()
-            return down_ref[j]
-
-        out = run_expert(jnp.concatenate([sa[j], sb[j]], axis=0), gu_ref[j], down)
+    for j in range(2):
+        for c in copies[4 * j : 4 * (j + 1)]:
+            c.wait()
+        out = jnp.dot(act[j], down_ref[j], preferred_element_type=F32).astype(BF16)
         oa[j] = out[:128]
         ob[j] = out[128:]
 
 
-def first_experts(slots, gu, w_down, downs):
+def down_half(act, w_down, downs):
     out = jax.ShapeDtypeStruct((2, 128, D), BF16)
     vmem, anywhere = pl.BlockSpec(memory_space=pltpu.VMEM), pl.BlockSpec(memory_space=pl.ANY)
     return pl.pallas_call(
-        first_kernel,
+        down_kernel,
         out_shape=(out, out, jax.ShapeDtypeStruct((2, 4 * HS, D), BF16)),
-        in_specs=[vmem] * 3 + [anywhere] * 4,
+        in_specs=[vmem] + [anywhere] * 4,
         out_specs=(vmem,) * 3,
         scratch_shapes=[pltpu.SemaphoreType.DMA((2, 4))],
-        compiler_params=pltpu.CompilerParams(vmem_limit_bytes=24 * 2**20),
-        cost_estimate=pl.CostEstimate(
-            flops=2_520_000_000, bytes_accessed=9_000_000, transcendentals=655360
-        ),
-    )(*slots, gu, *in_hbm((w_down,)), *downs)
+        compiler_params=pltpu.CompilerParams(vmem_limit_bytes=16 * 2**20),
+        cost_estimate=pl.CostEstimate(flops=2_520_000_000, bytes_accessed=9_000_000, transcendentals=655360),
+    )(act, *in_hbm((w_down,)), *downs)
 
 
 def body(tokens, router, w_gate, w_up, w_down):
-    ups = pack((w_gate, w_up, w_down), tuple((by, (0, 1)) for by in (1, 2, 3)))
+    ups = pack((w_gate, w_up, w_down), tuple((by, (0, 1)) for by in (2, 1, 3)))
     tokens, router, *ups = lax.optimization_barrier((tokens, router, *ups))
     mine, other, comb = front(tokens, router)
-    ups = [shift(w, True, by) for w, by in zip(ups, (1, 2, 3))]
+    ups = [shift(w, True, by) for w, by in zip(ups, (2, 1, 3))]
     downs = pack((w_gate, w_up, w_down), tuple((by, (2,)) for by in (1, 2, 3)))
     downs = [shift(w, True, by) for w, by in zip(downs, (1, 2, 3))]
     (rows,) = reorder((mine, swap(other)), weave, ((ROWS, D),))
     rows = exchange(rows)
     rows, *ups = lax.optimization_barrier((rows, *ups))
+    ups = [ups[n] for n in (1, 0, 2)]
     (s0,) = reorder((rows,), deal, ((2, 128, D),))
     s1, s3 = shift(s0, False, 1), shift(s0, False, 3)
     gu = collect((w_gate, w_up), ups)
     s1, s3, gu = lax.optimization_barrier((s1, s3, gu))
     far = shift(s1[:, :64], False, 1), shift(s3[:, 64:], False, 3)
-    o1, o3, down = first_experts((s1, s3), gu, w_down, downs)
+    o1, o3, down = down_half(up_half(s1, s3, gu), w_down, (downs[0], downs[2], downs[1]))
     t1, t3 = shift(o1, False, 3), shift(o3, False, 1)
     *far, _, _ = lax.optimization_barrier((*far, o1, o3))
     o2, o0 = experts((*far, s0), gu, down)

time: 135 us -> 133 us (0.985)
  waiting for transfers between devices: 50.1 us -> 42.7 us
  blocking collectives: 21.6 us -> 24.6 us
  starting transfers between devices: 38.5 us -> 40.5 us
    ppermute x13, waiting for transfers between devices: 32.9 us -> 27 us  [shift(): return lax.ppermute(value, AXES, shift_pairs(along_p, by))]
    all_to_all x1, blocking collectives: 21.6 us -> 24.6 us  [exchange(): lax.all_to_all(rows, AXES, split_axis=0, concat_axis=0, tiled=True, axis_...]
    ppermute x13, starting transfers between devices: 17.6 us -> 20.3 us  [shift(): return lax.ppermute(value, AXES, shift_pairs(along_p, by))]
    all_to_all x1, waiting for transfers between devices: 14.6 us -> 13.2 us  [exchange(): lax.all_to_all(rows, AXES, split_axis=0, concat_axis=0, tiled=True, axis_...]
    pallas_call x1 -> x2, Pallas kernels: 4.31 us -> 4.9 us  [the longest x1 3.01 us: down_half(): pl.pallas_call(down_kernel, out_shape=(out, out, jax.ShapeDtypeStruct((2,...]
  transfers between devices with their start and end apart: 16 -> 16, of which waited for: 6 -> 7; matrix products, arithmetic and copies ran while one was open for 0% -> 0% of each run, Pallas kernels for 13% -> 13%
where the time goes in v6:
time: 133 us
  waiting for transfers between devices  42.7 us (32%)
  starting transfers between devices  40.5 us (30%)
  blocking collectives  24.6 us (18%)
  Pallas kernels  23 us (17%)
  matrix products  1.56 us (1%)
    ppermute x13, waiting for transfers between devices, shift(): return lax.ppermute(value, AXES, shift_pairs(along_p, by))  27 us
    all_to_all x1, blocking collectives, exchange(): lax.all_to_all(rows, AXES, split_axis=0, concat_axis=0, tiled=True, axis_...  24.6 us
    ppermute x13, starting transfers between devices, shift(): return lax.ppermute(value, AXES, shift_pairs(along_p, by))  20.3 us
    all_to_all x1, waiting for transfers between devices, exchange(): lax.all_to_all(rows, AXES, split_axis=0, concat_axis=0, tiled=True, axis_...  13.2 us
    all_to_all x1, starting transfers between devices, exchange(): lax.all_to_all(rows, AXES, split_axis=0, concat_axis=0, tiled=True, axis_...  11.2 us
    ppermute x2, starting transfers between devices, swap(): return lax.ppermute(value, 'expert', [(e, e ^ 1) for e in range(16)])  9.04 us
    pallas_call x2, Pallas kernels, pack(): pl.pallas_call(functools.partial(pack_kernel, plans), out_shape=tuple((ja...  6.95 us
    pallas_call x1, Pallas kernels, experts(): pl.pallas_call(experts_kernel, out_shape=(jax.ShapeDtypeStruct((2, 128, D...  3.43 us
  transfers between devices with their start and end apart: 16, of which 7 were waited for; matrix products, arithmetic and copies ran while one was open for 0% of the time, Pallas kernels for 13%

profile of v6, /device:TPU:1, one launch (start us, length us, event | category | flops | bytes accessed | tf_op | source)
XLA Modules:
  0.0 132.6 jit_solution(14163487008449093049)
XLA Ops:
  0.0 4.3 %shard_map.55 = (bf16[2,2,160,1280]{3,2,1,0:T(8,128)(2,1)}, bf16[2,2,160,1280]{3,2,1,0:T(8,128)(2,1)}, bf16[2,2,160,1280]{3,2,1,0:T(8,128)(2,1)}) custom-call(bf16[8,160,1280]{2,1,0:T(8,128)(2,1)} %refs_0_.5, bf16[8,160,1280]{2,1,0:T(8,128)(2,1)} %refs_1_.5, bf16[8,160,1280]{2,1,0:T(8,128)(2,1)} %wd.1), custom_call_target="tpu_custom_call" | custom-call | bytes 9840000 | tf_op jit(solution)/shard_map/pallas_call | solution.py:147
  4.3 3.8 %collective-permute-start.1 = (bf16[2,2,160,1280]{3,2,1,0:T(8,128)(2,1)}, bf16[2,2,160,1280]{3,2,1,0:T(8,128)(2,1)S(1)}, u32[]{:S(2)}, u32[]{:S(2)}) collective-permute-start(bf16[2,2,160,1280]{3,2,1,0:T(8,128)(2,1)} %get-tuple-element.43), channel_id=1, source_target_pairs={{0,32},{1,129},{2,34},{3,131},{4,36},{5,133},{6,38},{7,135},{8,40}... | collective-permute-start | bytes 4915208 | tf_op jit(solution)/shard_map/ppermute | solution.py:63
  8.5 2.3 %collective-permute-start.3 = (bf16[2,2,160,1280]{3,2,1,0:T(8,128)(2,1)}, bf16[2,2,160,1280]{3,2,1,0:T(8,128)(2,1)}, u32[]{:S(2)}, u32[]{:S(2)}) collective-permute-start(bf16[2,2,160,1280]{3,2,1,0:T(8,128)(2,1)} %get-tuple-element.45), channel_id=1, source_target_pairs={{0,48},{1,193},{2,50},{3,195},{4,52},{5,197},{6,54},{7,199},{8,56}... | collective-permute-start | bytes 4915208 | tf_op jit(solution)/shard_map/ppermute | solution.py:63
  10.8 2.4 %shard_map.56 = (bf16[128,1280]{1,0:T(8,128)(2,1)S(1)}, bf16[128,1280]{1,0:T(8,128)(2,1)S(1)}, bf16[2,256,256]{2,1,0:T(8,128)(2,1)S(1)}) custom-call(bf16[2,256,1280]{2,1,0:T(8,128)(2,1)S(1)} %copy-done, f32[1280,128]{1,0:T(8,128)S(1)} %copy-done.1), custom_call_target="tpu_custom_call" | custom-call | flops 900000000 | bytes 3000000 | tf_op jit(solution)/shard_map/pallas_call | solution.py:107
  13.2 1.4 %collective-permute-start = (bf16[128,1280]{1,0:T(8,128)(2,1)S(1)}, bf16[128,1280]{1,0:T(8,128)(2,1)S(1)}, u32[]{:S(2)}, u32[]{:S(2)}) collective-permute-start(bf16[128,1280]{1,0:T(8,128)(2,1)S(1)} %get-tuple-element.42), channel_id=1, source_target_pairs={{0,1},{1,0},{2,3},{3,2},{4,5},{5,4},{6,7},{7,6},{8,9},{9,8},{10,11... | collective-permute-start | bytes 983048 | tf_op jit(solution)/shard_map/ppermute | solution.py:59
  17.1 11.2 %all-to-all-start = ((bf16[32,8,1280]{2,1,0:T(8,128)(2,1)}), bf16[32,8,1280]{2,1,0:T(8,128)(2,1)S(1)}, u32[]{:S(2)}, u32[]{:S(2)}) async-start(bf16[32,8,1280]{2,1,0:T(8,128)(2,1)} %bitcast.1), calls=%async_computation | async-start | bytes 1310720 | tf_op jit(solution)/shard_map/all_to_all | solution.py:53
  28.4 2.7 %shard_map.61 = (bf16[1,2,160,1280]{3,2,1,0:T(8,128)(2,1)}, bf16[1,2,160,1280]{3,2,1,0:T(8,128)(2,1)}, bf16[1,2,160,1280]{3,2,1,0:T(8,128)(2,1)}) custom-call(bf16[8,160,1280]{2,1,0:T(8,128)(2,1)} %refs_0_.5, bf16[8,160,1280]{2,1,0:T(8,128)(2,1)} %refs_1_.5, bf16[8,160,1280]{2,1,0:T(8,128)(2,1)} %wd.1), custom_call_target="tpu_custom_call" | custom-call | bytes 4920000 | tf_op jit(solution)/shard_map/pallas_call | solution.py:147
  31.0 1.3 collective-permute-start.8
  32.3 1.4 %collective-permute-start.9 = (bf16[1,2,160,1280]{3,2,1,0:T(8,128)(2,1)}, bf16[1,2,160,1280]{3,2,1,0:T(8,128)(2,1)}, u32[]{:S(2)}, u32[]{:S(2)}) collective-permute-start(bf16[1,2,160,1280]{3,2,1,0:T(8,128)(2,1)} %get-tuple-element.54), channel_id=1, source_target_pairs={{0,48},{1,193},{2,50},{3,195},{4,52},{5,197},{6,54},{7,199},{8,56}... | collective-permute-start | bytes 2457608 | tf_op jit(solution)/shard_map/ppermute | solution.py:63
  33.8 1.5 %collective-permute-start.10 = (bf16[1,2,160,1280]{3,2,1,0:T(8,128)(2,1)}, bf16[1,2,160,1280]{3,2,1,0:T(8,128)(2,1)}, u32[]{:S(2)}, u32[]{:S(2)}) collective-permute-start(bf16[1,2,160,1280]{3,2,1,0:T(8,128)(2,1)} %get-tuple-element.55), channel_id=1, source_target_pairs={{0,32},{1,129},{2,34},{3,131},{4,36},{5,133},{6,38},{7,135},{8,40}... | collective-permute-start | bytes 2457608 | tf_op jit(solution)/shard_map/ppermute | solution.py:63
  35.3 13.2 %all-to-all-done = bf16[32,8,1280]{2,1,0:T(8,128)(2,1)S(1)} async-done(((bf16[32,8,1280]{2,1,0:T(8,128)(2,1)}), bf16[32,8,1280]{2,1,0:T(8,128)(2,1)S(1)}, u32[]{:S(2)}, u32[]{:S(2)}) %all-to-all-start) | async-done | bytes 655392 | tf_op jit(solution)/shard_map/all_to_all | solution.py:53
  50.2 1.5 %collective-permute-start.5 = (bf16[2,128,1280]{2,1,0:T(8,128)(2,1)S(1)}, bf16[2,128,1280]{2,1,0:T(8,128)(2,1)S(1)}, u32[]{:S(2)}, u32[]{:S(2)}) collective-permute-start(bf16[2,128,1280]{2,1,0:T(8,128)(2,1)S(1)} %shard_map.58.own), channel_id=1, source_target_pairs={{0,192},{1,49},{2,194},{3,51},{4,196},{5,53},{6,198},{7,55},{8,200... | collective-permute-start | bytes 1966088 | tf_op jit(solution)/shard_map/ppermute | solution.py:63
  51.7 2.7 %shard_map.59.gu_ref = bf16[2,1280,1280]{2,1,0:T(8,128)(2,1)S(1)} custom-call(bf16[8,160,1280]{2,1,0:T(8,128)(2,1)} %refs_0_.5, bf16[8,160,1280]{2,1,0:T(8,128)(2,1)} %refs_1_.5, bf16[2,2,160,1280]{3,2,1,0:T(8,128)(2,1)} %collective-permute-done.2.refs_2_, bf16[2,2,160,1280]{3,2,1,0:T(8,128)(2,1)S(1)} %collective-permute-done.1.refs_3_, ...), custom_call_target="tpu_custom_call" | custom-call | bytes 13200000 | tf_op jit(solution)/shard_map/pallas_call | solution.py:228
  54.4 13.7 %collective-permute-done.4.sa = bf16[2,128,1280]{2,1,0:T(8,128)(2,1)S(1)} collective-permute-done((bf16[2,128,1280]{2,1,0:T(8,128)(2,1)S(1)}, bf16[2,128,1280]{2,1,0:T(8,128)(2,1)S(1)}, u32[]{:S(2)}, u32[]{:S(2)}) %collective-permute-start.4) | collective-permute-done | bytes 655392 | tf_op jit(solution)/shard_map/ppermute | solution.py:63
  69.0 2.1 %collective-permute-start.7 = (bf16[2,64,1280]{2,1,0:T(8,128)(2,1)S(1)}, bf16[2,64,1280]{2,1,0:T(8,128)(2,1)S(1)}, u32[]{:S(2)}, u32[]{:S(2)}) collective-permute-start(bf16[2,64,1280]{2,1,0:T(8,128)(2,1)S(1)} %slice.7), channel_id=1, source_target_pairs={{0,192},{1,49},{2,194},{3,51},{4,196},{5,53},{6,198},{7,55},{8,200... | collective-permute-start | bytes 983048 | tf_op jit(solution)/shard_map/ppermute | solution.py:63
  71.1 1.9 %shard_map.60.act = bf16[2,256,640]{2,1,0:T(8,128)(2,1)S(1)} custom-call(bf16[2,128,1280]{2,1,0:T(8,128)(2,1)S(1)} %collective-permute-done.4.sa, bf16[2,128,1280]{2,1,0:T(8,128)(2,1)S(1)} %collective-permute-done.5.sb, bf16[2,1280,1280]{2,1,0:T(8,128)(2,1)S(1)} %shard_map.59.gu_ref), custom_call_target="tpu_custom_call" | custom-call | tf_op jit(solution)/shard_map/pallas_call | solution.py:288
  73.0 3.0 %shard_map.62 = (bf16[2,128,1280]{2,1,0:T(8,128)(2,1)S(1)}, bf16[2,128,1280]{2,1,0:T(8,128)(2,1)S(1)}, bf16[2,640,1280]{2,1,0:T(8,128)(2,1)S(1)}) custom-call(bf16[2,256,640]{2,1,0:T(8,128)(2,1)S(1)} %shard_map.60.act, bf16[8,160,1280]{2,1,0:T(8,128)(2,1)} %wd.1, bf16[1,2,160,1280]{3,2,1,0:T(8,128)(2,1)S(1)} %collective-permute-done.8.d1, ...), custom_call_target="tpu_custom_call" | custom-call | flops 2520000000 | bytes 9000000 | tf_op jit(solution)/shard_map/pallas_call | solution.py:320
  76.1 2.5 %collective-permute-start.11 = (bf16[2,128,1280]{2,1,0:T(8,128)(2,1)S(1)}, bf16[2,128,1280]{2,1,0:T(8,128)(2,1)S(1)}, u32[]{:S(2)}, u32[]{:S(2)}) collective-permute-start(bf16[2,128,1280]{2,1,0:T(8,128)(2,1)S(1)} %get-tuple-element.56), channel_id=1, source_target_pairs={{0,192},{1,49},{2,194},{3,51},{4,196},{5,53},{6,198},{7,55},{8,200... | collective-permute-start | bytes 1966088 | tf_op jit(solution)/shard_map/ppermute | solution.py:63
  79.2 3.4 %shard_map.63 = (bf16[2,128,1280]{2,1,0:T(8,128)(2,1)S(1)}, bf16[2,128,1280]{2,1,0:T(8,128)(2,1)S(1)}) custom-call(bf16[2,64,1280]{2,1,0:T(8,128)(2,1)S(1)} %collective-permute-done.6.far_low, bf16[2,64,1280]{2,1,0:T(8,128)(2,1)S(1)} %collective-permute-done.7.far_high, bf16[2,128,1280]{2,1,0:T(8,128)(2,1)S(1)} %shard_map.58.own, ...), custom_call_target="tpu_custom_call" | custom-call | flops 1260000000 | bytes 2000000 | tf_op jit(solution)/shard_map/pallas_call | solution.py:255
  83.9 9.2 %collective-permute-done.11.b = bf16[2,128,1280]{2,1,0:T(8,128)(2,1)S(1)} collective-permute-done((bf16[2,128,1280]{2,1,0:T(8,128)(2,1)S(1)}, bf16[2,128,1280]{2,1,0:T(8,128)(2,1)S(1)}, u32[]{:S(2)}, u32[]{:S(2)}) %collective-permute-start.11) | collective-permute-done | bytes 655392 | tf_op jit(solution)/shard_map/ppermute | solution.py:63
  93.1 3.4 %collective-permute-done.12.c = bf16[2,128,1280]{2,1,0:T(8,128)(2,1)S(1)} collective-permute-done((bf16[2,128,1280]{2,1,0:T(8,128)(2,1)S(1)}, bf16[2,128,1280]{2,1,0:T(8,128)(2,1)S(1)}, u32[]{:S(2)}, u32[]{:S(2)}) %collective-permute-start.12) | collective-permute-done | bytes 655392 | tf_op jit(solution)/shard_map/ppermute | solution.py:63
  97.1 24.6 %all_to_all.23 = bf16[32,8,1280]{2,1,0:T(8,128)(2,1)S(1)} all-to-all(bf16[32,8,1280]{2,1,0:T(8,128)(2,1)S(1)} %bitcast.7), channel_id=1, replica_groups={{0,2,4,6,8,10,12,14,16,18,20,22,24,26,28,30,32,34,36,38,40,42,44,46,48,..., dimensions={0} | all-to-all | bytes 1310720 | tf_op jit(solution)/shard_map/all_to_all | solution.py:53
  122.1 7.6 %collective-permute-start.14 = (bf16[128,1280]{1,0:T(8,128)(2,1)S(1)}, bf16[128,1280]{1,0:T(8,128)(2,1)S(1)}, u32[]{:S(2)}, u32[]{:S(2)}) collective-permute-start(bf16[128,1280]{1,0:T(8,128)(2,1)S(1)} %get-tuple-element.64), channel_id=1, source_target_pairs={{0,1},{1,0},{2,3},{3,2},{4,5},{5,4},{6,7},{7,6},{8,9},{9,8},{10,11... | collective-permute-start | bytes 983048 | tf_op jit(solution)/shard_map/ppermute | solution.py:59
  131.0 1.6 %convolution_convert_fusion = bf16[512,1280]{1,0:T(8,128)(2,1)} fusion(bf16[512,256]{1,0:T(8,128)(2,1)S(1)} %bitcast.10, bf16[128,1280]{1,0:T(8,128)(2,1)S(1)} %collective-permute-done.14, bf16[128,1280]{1,0:T(8,128)(2,1)S(1)} %get-tuple-element.63), kind=kOutput, calls=%fused_computation | convolution fusion | flops 337510400 | bytes 2228224 | tf_op jit(solution)/shard_map/dot_general | solution.py:356
  (28 shorter events, 9.7 us)
Async XLA Ops:
  0.0 10.8 %copy-start = (bf16[2,256,1280]{2,1,0:T(8,128)(2,1)S(1)}, bf16[2,256,1280]{2,1,0:T(8,128)(2,1)}, u32[]{:S(2)}) copy-start(bf16[2,256,1280]{2,1,0:T(8,128)(2,1)} %tok_ref) | copy-start | bytes 3932164
  0.0 10.8 %copy-start.1 = (f32[1280,128]{1,0:T(8,128)S(1)}, f32[1280,128]{1,0:T(8,128)}, u32[]{:S(2)}) copy-start(f32[1280,128]{1,0:T(8,128)} %router_ref) | copy-start | bytes 1966084
  4.3 29.5 %collective-permute-start.1 = (bf16[2,2,160,1280]{3,2,1,0:T(8,128)(2,1)}, bf16[2,2,160,1280]{3,2,1,0:T(8,128)(2,1)S(1)}, u32[]{:S(2)}, u32[]{:S(2)}) collective-permute-start(bf16[2,2,160,1280]{3,2,1,0:T(8,128)(2,1)} %get-tuple-element.43), channel_id=1, source_target_pairs={{0,32},{1,129},{2,34},{3,131},{4,36},{5,133},{6,38},{7,135},{8,40}... | collective-permute-start | bytes 4915208 | tf_op jit(solution)/shard_map/ppermute | solution.py:63
  8.1 40.4 %collective-permute-start.2 = (bf16[2,2,160,1280]{3,2,1,0:T(8,128)(2,1)}, bf16[2,2,160,1280]{3,2,1,0:T(8,128)(2,1)}, u32[]{:S(2)}, u32[]{:S(2)}) collective-permute-start(bf16[2,2,160,1280]{3,2,1,0:T(8,128)(2,1)} %get-tuple-element.44), channel_id=1, source_target_pairs={{0,16},{1,65},{2,18},{3,67},{4,20},{5,69},{6,22},{7,71},{8,24},{9,... | collective-permute-start | bytes 4915208 | tf_op jit(solution)/shard_map/ppermute | solution.py:63
  8.5 40.0 %collective-permute-start.3 = (bf16[2,2,160,1280]{3,2,1,0:T(8,128)(2,1)}, bf16[2,2,160,1280]{3,2,1,0:T(8,128)(2,1)}, u32[]{:S(2)}, u32[]{:S(2)}) collective-permute-start(bf16[2,2,160,1280]{3,2,1,0:T(8,128)(2,1)} %get-tuple-element.45), channel_id=1, source_target_pairs={{0,48},{1,193},{2,50},{3,195},{4,52},{5,197},{6,54},{7,199},{8,56}... | collective-permute-start | bytes 4915208 | tf_op jit(solution)/shard_map/ppermute | solution.py:63
  13.2 2.7 %collective-permute-start = (bf16[128,1280]{1,0:T(8,128)(2,1)S(1)}, bf16[128,1280]{1,0:T(8,128)(2,1)S(1)}, u32[]{:S(2)}, u32[]{:S(2)}) collective-permute-start(bf16[128,1280]{1,0:T(8,128)(2,1)S(1)} %get-tuple-element.42), channel_id=1, source_target_pairs={{0,1},{1,0},{2,3},{3,2},{4,5},{5,4},{6,7},{7,6},{8,9},{9,8},{10,11... | collective-permute-start | bytes 983048 | tf_op jit(solution)/shard_map/ppermute | solution.py:59
  17.1 31.4 %all-to-all-start = ((bf16[32,8,1280]{2,1,0:T(8,128)(2,1)}), bf16[32,8,1280]{2,1,0:T(8,128)(2,1)S(1)}, u32[]{:S(2)}, u32[]{:S(2)}) async-start(bf16[32,8,1280]{2,1,0:T(8,128)(2,1)} %bitcast.1), calls=%async_computation | async-start | bytes 1310720 | tf_op jit(solution)/shard_map/all_to_all | solution.py:53
  31.0 42.0 %collective-permute-start.8 = (bf16[1,2,160,1280]{3,2,1,0:T(8,128)(2,1)}, bf16[1,2,160,1280]{3,2,1,0:T(8,128)(2,1)S(1)}, u32[]{:S(2)}, u32[]{:S(2)}) collective-permute-start(bf16[1,2,160,1280]{3,2,1,0:T(8,128)(2,1)} %get-tuple-element.53), channel_id=1, source_target_pairs={{0,16},{1,65},{2,18},{3,67},{4,20},{5,69},{6,22},{7,71},{8,24},{9,... | collective-permute-start | bytes 2457608 | tf_op jit(solution)/shard_map/ppermute | solution.py:63
  32.3 40.7 %collective-permute-start.9 = (bf16[1,2,160,1280]{3,2,1,0:T(8,128)(2,1)}, bf16[1,2,160,1280]{3,2,1,0:T(8,128)(2,1)}, u32[]{:S(2)}, u32[]{:S(2)}) collective-permute-start(bf16[1,2,160,1280]{3,2,1,0:T(8,128)(2,1)} %get-tuple-element.54), channel_id=1, source_target_pairs={{0,48},{1,193},{2,50},{3,195},{4,52},{5,197},{6,54},{7,199},{8,56}... | collective-permute-start | bytes 2457608 | tf_op jit(solution)/shard_map/ppermute | solution.py:63
  33.8 39.3 %collective-permute-start.10 = (bf16[1,2,160,1280]{3,2,1,0:T(8,128)(2,1)}, bf16[1,2,160,1280]{3,2,1,0:T(8,128)(2,1)}, u32[]{:S(2)}, u32[]{:S(2)}) collective-permute-start(bf16[1,2,160,1280]{3,2,1,0:T(8,128)(2,1)} %get-tuple-element.55), channel_id=1, source_target_pairs={{0,32},{1,129},{2,34},{3,131},{4,36},{5,133},{6,38},{7,135},{8,40}... | collective-permute-start | bytes 2457608 | tf_op jit(solution)/shard_map/ppermute | solution.py:63
  48.9 19.1 %collective-permute-start.4 = (bf16[2,128,1280]{2,1,0:T(8,128)(2,1)S(1)}, bf16[2,128,1280]{2,1,0:T(8,128)(2,1)S(1)}, u32[]{:S(2)}, u32[]{:S(2)}) collective-permute-start(bf16[2,128,1280]{2,1,0:T(8,128)(2,1)S(1)} %shard_map.58.own), channel_id=1, source_target_pairs={{0,64},{1,17},{2,66},{3,19},{4,68},{5,21},{6,70},{7,23},{8,72},{9,... | collective-permute-start | bytes 1966088 | tf_op jit(solution)/shard_map/ppermute | solution.py:63
  50.2 17.8 %collective-permute-start.5 = (bf16[2,128,1280]{2,1,0:T(8,128)(2,1)S(1)}, bf16[2,128,1280]{2,1,0:T(8,128)(2,1)S(1)}, u32[]{:S(2)}, u32[]{:S(2)}) collective-permute-start(bf16[2,128,1280]{2,1,0:T(8,128)(2,1)S(1)} %shard_map.58.own), channel_id=1, source_target_pairs={{0,192},{1,49},{2,194},{3,51},{4,196},{5,53},{6,198},{7,55},{8,200... | collective-permute-start | bytes 1966088 | tf_op jit(solution)/shard_map/ppermute | solution.py:63
  68.1 11.1 %collective-permute-start.6 = (bf16[2,64,1280]{2,1,0:T(8,128)(2,1)S(1)}, bf16[2,64,1280]{2,1,0:T(8,128)(2,1)S(1)}, u32[]{:S(2)}, u32[]{:S(2)}) collective-permute-start(bf16[2,64,1280]{2,1,0:T(8,128)(2,1)S(1)} %slice.6), channel_id=1, source_target_pairs={{0,64},{1,17},{2,66},{3,19},{4,68},{5,21},{6,70},{7,23},{8,72},{9,... | collective-permute-start | bytes 983048 | tf_op jit(solution)/shard_map/ppermute | solution.py:63
  69.0 10.2 %collective-permute-start.7 = (bf16[2,64,1280]{2,1,0:T(8,128)(2,1)S(1)}, bf16[2,64,1280]{2,1,0:T(8,128)(2,1)S(1)}, u32[]{:S(2)}, u32[]{:S(2)}) collective-permute-start(bf16[2,64,1280]{2,1,0:T(8,128)(2,1)S(1)} %slice.7), channel_id=1, source_target_pairs={{0,192},{1,49},{2,194},{3,51},{4,196},{5,53},{6,198},{7,55},{8,200... | collective-permute-start | bytes 983048 | tf_op jit(solution)/shard_map/ppermute | solution.py:63
  76.1 17.0 %collective-permute-start.11 = (bf16[2,128,1280]{2,1,0:T(8,128)(2,1)S(1)}, bf16[2,128,1280]{2,1,0:T(8,128)(2,1)S(1)}, u32[]{:S(2)}, u32[]{:S(2)}) collective-permute-start(bf16[2,128,1280]{2,1,0:T(8,128)(2,1)S(1)} %get-tuple-element.56), channel_id=1, source_target_pairs={{0,192},{1,49},{2,194},{3,51},{4,196},{5,53},{6,198},{7,55},{8,200... | collective-permute-start | bytes 1966088 | tf_op jit(solution)/shard_map/ppermute | solution.py:63
  78.5 18.0 %collective-permute-start.12 = (bf16[2,128,1280]{2,1,0:T(8,128)(2,1)S(1)}, bf16[2,128,1280]{2,1,0:T(8,128)(2,1)S(1)}, u32[]{:S(2)}, u32[]{:S(2)}) collective-permute-start(bf16[2,128,1280]{2,1,0:T(8,128)(2,1)S(1)} %get-tuple-element.57), channel_id=1, source_target_pairs={{0,64},{1,17},{2,66},{3,19},{4,68},{5,21},{6,70},{7,23},{8,72},{9,... | collective-permute-start | bytes 1966088 | tf_op jit(solution)/shard_map/ppermute | solution.py:63
  82.6 14.1 %collective-permute-start.13 = (bf16[2,128,1280]{2,1,0:T(8,128)(2,1)S(1)}, bf16[2,128,1280]{2,1,0:T(8,128)(2,1)S(1)}, u32[]{:S(2)}, u32[]{:S(2)}) collective-permute-start(bf16[2,128,1280]{2,1,0:T(8,128)(2,1)S(1)} %get-tuple-element.62), channel_id=1, source_target_pairs={{0,128},{1,33},{2,130},{3,35},{4,132},{5,37},{6,134},{7,39},{8,136... | collective-permute-start | bytes 1966088 | tf_op jit(solution)/shard_map/ppermute | solution.py:63
  122.1 8.9 %collective-permute-start.14 = (bf16[128,1280]{1,0:T(8,128)(2,1)S(1)}, bf16[128,1280]{1,0:T(8,128)(2,1)S(1)}, u32[]{:S(2)}, u32[]{:S(2)}) collective-permute-start(bf16[128,1280]{1,0:T(8,128)(2,1)S(1)} %get-tuple-element.64), channel_id=1, source_target_pairs={{0,1},{1,0},{2,3},{3,2},{4,5},{5,4},{6,7},{7,6},{8,9},{9,8},{10,11... | collective-permute-start | bytes 983048 | tf_op jit(solution)/shard_map/ppermute | solution.py:59

commit v7 on v6

--- a/solution.py
+++ b/solution.py
@@ -342,7 +342,7 @@
     (s0,) = reorder((rows,), deal, ((2, 128, D),))
     s1, s3 = shift(s0, False, 1), shift(s0, False, 3)
     gu = collect((w_gate, w_up), ups)
-    s1, s3, gu = lax.optimization_barrier((s1, s3, gu))
+    s1, gu = lax.optimization_barrier((s1, gu))
     far = shift(s1[:, :64], False, 1), shift(s3[:, 64:], False, 3)
     o1, o3, down = down_half(up_half(s1, s3, gu), w_down, (downs[0], downs[2], downs[1]))
     t1, t3 = shift(o1, False, 3), shift(o3, False, 1)

time: 133 us -> 133 us (level)
  starting transfers between devices: 40.5 us -> 38.2 us
  blocking collectives: 24.6 us -> 26.6 us
    ppermute x2, starting transfers between devices: 9.04 us -> 6.93 us  [swap(): return lax.ppermute(value, 'expert', [(e, e ^ 1) for e in range(16)])]
    all_to_all x1, blocking collectives: 24.6 us -> 26.6 us  [exchange(): lax.all_to_all(rows, AXES, split_axis=0, concat_axis=0, tiled=True, axis_...]
where the time goes in v7:
time: 133 us
  waiting for transfers between devices  43 us (32%)
  starting transfers between devices  38.2 us (29%)
  blocking collectives  26.6 us (20%)
  Pallas kernels  23 us (17%)
  matrix products  1.56 us (1%)
    ppermute x13, waiting for transfers between devices, shift(): return lax.ppermute(value, AXES, shift_pairs(along_p, by))  27.3 us
    all_to_all x1, blocking collectives, exchange(): lax.all_to_all(rows, AXES, split_axis=0, concat_axis=0, tiled=True, axis_...  26.6 us
    ppermute x13, starting transfers between devices, shift(): return lax.ppermute(value, AXES, shift_pairs(along_p, by))  20 us
    all_to_all x1, waiting for transfers between devices, exchange(): lax.all_to_all(rows, AXES, split_axis=0, concat_axis=0, tiled=True, axis_...  13.2 us
    all_to_all x1, starting transfers between devices, exchange(): lax.all_to_all(rows, AXES, split_axis=0, concat_axis=0, tiled=True, axis_...  11.2 us
    pallas_call x2, Pallas kernels, pack(): pl.pallas_call(functools.partial(pack_kernel, plans), out_shape=tuple((ja...  6.95 us
    ppermute x2, starting transfers between devices, swap(): return lax.ppermute(value, 'expert', [(e, e ^ 1) for e in range(16)])  6.93 us
    pallas_call x1, Pallas kernels, experts(): pl.pallas_call(experts_kernel, out_shape=(jax.ShapeDtypeStruct((2, 128, D...  3.43 us
  transfers between devices with their start and end apart: 16, of which 7 were waited for; matrix products, arithmetic and copies ran while one was open for 0% of the time, Pallas kernels for 13%

profile of v7, /device:TPU:1, one launch (start us, length us, event | category | flops | bytes accessed | tf_op | source)
XLA Modules:
  0.0 132.5 jit_solution(6086404142780122930)
XLA Ops:
  0.0 4.3 %shard_map.55 = (bf16[2,2,160,1280]{3,2,1,0:T(8,128)(2,1)}, bf16[2,2,160,1280]{3,2,1,0:T(8,128)(2,1)}, bf16[2,2,160,1280]{3,2,1,0:T(8,128)(2,1)}) custom-call(bf16[8,160,1280]{2,1,0:T(8,128)(2,1)} %refs_0_.5, bf16[8,160,1280]{2,1,0:T(8,128)(2,1)} %refs_1_.5, bf16[8,160,1280]{2,1,0:T(8,128)(2,1)} %wd.1), custom_call_target="tpu_custom_call" | custom-call | bytes 9840000 | tf_op jit(solution)/shard_map/pallas_call | solution.py:147
  4.3 3.8 %collective-permute-start.1 = (bf16[2,2,160,1280]{3,2,1,0:T(8,128)(2,1)}, bf16[2,2,160,1280]{3,2,1,0:T(8,128)(2,1)S(1)}, u32[]{:S(2)}, u32[]{:S(2)}) collective-permute-start(bf16[2,2,160,1280]{3,2,1,0:T(8,128)(2,1)} %get-tuple-element.42), channel_id=1, source_target_pairs={{0,32},{1,129},{2,34},{3,131},{4,36},{5,133},{6,38},{7,135},{8,40}... | collective-permute-start | bytes 4915208 | tf_op jit(solution)/shard_map/ppermute | solution.py:63
  8.5 2.3 %collective-permute-start.3 = (bf16[2,2,160,1280]{3,2,1,0:T(8,128)(2,1)}, bf16[2,2,160,1280]{3,2,1,0:T(8,128)(2,1)}, u32[]{:S(2)}, u32[]{:S(2)}) collective-permute-start(bf16[2,2,160,1280]{3,2,1,0:T(8,128)(2,1)} %get-tuple-element.44), channel_id=1, source_target_pairs={{0,48},{1,193},{2,50},{3,195},{4,52},{5,197},{6,54},{7,199},{8,56}... | collective-permute-start | bytes 4915208 | tf_op jit(solution)/shard_map/ppermute | solution.py:63
  10.8 2.4 %shard_map.56 = (bf16[128,1280]{1,0:T(8,128)(2,1)S(1)}, bf16[128,1280]{1,0:T(8,128)(2,1)S(1)}, bf16[2,256,256]{2,1,0:T(8,128)(2,1)S(1)}) custom-call(bf16[2,256,1280]{2,1,0:T(8,128)(2,1)S(1)} %copy-done, f32[1280,128]{1,0:T(8,128)S(1)} %copy-done.1), custom_call_target="tpu_custom_call" | custom-call | flops 900000000 | bytes 3000000 | tf_op jit(solution)/shard_map/pallas_call | solution.py:107
  13.2 1.4 %collective-permute-start = (bf16[128,1280]{1,0:T(8,128)(2,1)S(1)}, bf16[128,1280]{1,0:T(8,128)(2,1)S(1)}, u32[]{:S(2)}, u32[]{:S(2)}) collective-permute-start(bf16[128,1280]{1,0:T(8,128)(2,1)S(1)} %get-tuple-element.41), channel_id=1, source_target_pairs={{0,1},{1,0},{2,3},{3,2},{4,5},{5,4},{6,7},{7,6},{8,9},{9,8},{10,11... | collective-permute-start | bytes 983048 | tf_op jit(solution)/shard_map/ppermute | solution.py:59
  17.1 11.2 %all-to-all-start = ((bf16[32,8,1280]{2,1,0:T(8,128)(2,1)}), bf16[32,8,1280]{2,1,0:T(8,128)(2,1)S(1)}, u32[]{:S(2)}, u32[]{:S(2)}) async-start(bf16[32,8,1280]{2,1,0:T(8,128)(2,1)} %bitcast.1), calls=%async_computation | async-start | bytes 1310720 | tf_op jit(solution)/shard_map/all_to_all | solution.py:53
  28.4 2.7 %shard_map.61 = (bf16[1,2,160,1280]{3,2,1,0:T(8,128)(2,1)}, bf16[1,2,160,1280]{3,2,1,0:T(8,128)(2,1)}, bf16[1,2,160,1280]{3,2,1,0:T(8,128)(2,1)}) custom-call(bf16[8,160,1280]{2,1,0:T(8,128)(2,1)} %refs_0_.5, bf16[8,160,1280]{2,1,0:T(8,128)(2,1)} %refs_1_.5, bf16[8,160,1280]{2,1,0:T(8,128)(2,1)} %wd.1), custom_call_target="tpu_custom_call" | custom-call | bytes 4920000 | tf_op jit(solution)/shard_map/pallas_call | solution.py:147
  31.0 1.3 collective-permute-start.8
  32.3 1.4 %collective-permute-start.9 = (bf16[1,2,160,1280]{3,2,1,0:T(8,128)(2,1)}, bf16[1,2,160,1280]{3,2,1,0:T(8,128)(2,1)}, u32[]{:S(2)}, u32[]{:S(2)}) collective-permute-start(bf16[1,2,160,1280]{3,2,1,0:T(8,128)(2,1)} %get-tuple-element.52), channel_id=1, source_target_pairs={{0,48},{1,193},{2,50},{3,195},{4,52},{5,197},{6,54},{7,199},{8,56}... | collective-permute-start | bytes 2457608 | tf_op jit(solution)/shard_map/ppermute | solution.py:63
  33.8 1.5 %collective-permute-start.10 = (bf16[1,2,160,1280]{3,2,1,0:T(8,128)(2,1)}, bf16[1,2,160,1280]{3,2,1,0:T(8,128)(2,1)}, u32[]{:S(2)}, u32[]{:S(2)}) collective-permute-start(bf16[1,2,160,1280]{3,2,1,0:T(8,128)(2,1)} %get-tuple-element.53), channel_id=1, source_target_pairs={{0,32},{1,129},{2,34},{3,131},{4,36},{5,133},{6,38},{7,135},{8,40}... | collective-permute-start | bytes 2457608 | tf_op jit(solution)/shard_map/ppermute | solution.py:63
  35.3 13.2 %all-to-all-done = bf16[32,8,1280]{2,1,0:T(8,128)(2,1)S(1)} async-done(((bf16[32,8,1280]{2,1,0:T(8,128)(2,1)}), bf16[32,8,1280]{2,1,0:T(8,128)(2,1)S(1)}, u32[]{:S(2)}, u32[]{:S(2)}) %all-to-all-start) | async-done | bytes 655392 | tf_op jit(solution)/shard_map/all_to_all | solution.py:53
  50.2 1.5 %collective-permute-start.6 = (bf16[2,128,1280]{2,1,0:T(8,128)(2,1)S(1)}, bf16[2,128,1280]{2,1,0:T(8,128)(2,1)S(1)}, u32[]{:S(2)}, u32[]{:S(2)}) collective-permute-start(bf16[2,128,1280]{2,1,0:T(8,128)(2,1)S(1)} %shard_map.58.own), channel_id=1, source_target_pairs={{0,192},{1,49},{2,194},{3,51},{4,196},{5,53},{6,198},{7,55},{8,200... | collective-permute-start | bytes 1966088 | tf_op jit(solution)/shard_map/ppermute | solution.py:63
  51.7 2.7 %shard_map.59.gu_ref = bf16[2,1280,1280]{2,1,0:T(8,128)(2,1)S(1)} custom-call(bf16[8,160,1280]{2,1,0:T(8,128)(2,1)} %refs_0_.5, bf16[8,160,1280]{2,1,0:T(8,128)(2,1)} %refs_1_.5, bf16[2,2,160,1280]{3,2,1,0:T(8,128)(2,1)} %collective-permute-done.2.refs_2_, bf16[2,2,160,1280]{3,2,1,0:T(8,128)(2,1)S(1)} %collective-permute-done.1.refs_3_, ...), custom_call_target="tpu_custom_call" | custom-call | bytes 13200000 | tf_op jit(solution)/shard_map/pallas_call | solution.py:228
  54.4 13.7 %collective-permute-done.4.sa = bf16[2,128,1280]{2,1,0:T(8,128)(2,1)S(1)} collective-permute-done((bf16[2,128,1280]{2,1,0:T(8,128)(2,1)S(1)}, bf16[2,128,1280]{2,1,0:T(8,128)(2,1)S(1)}, u32[]{:S(2)}, u32[]{:S(2)}) %collective-permute-start.4) | collective-permute-done | bytes 655392 | tf_op jit(solution)/shard_map/ppermute | solution.py:63
  68.2 2.9 %collective-permute-start.7 = (bf16[2,64,1280]{2,1,0:T(8,128)(2,1)S(1)}, bf16[2,64,1280]{2,1,0:T(8,128)(2,1)S(1)}, u32[]{:S(2)}, u32[]{:S(2)}) collective-permute-start(bf16[2,64,1280]{2,1,0:T(8,128)(2,1)S(1)} %slice.8), channel_id=1, source_target_pairs={{0,192},{1,49},{2,194},{3,51},{4,196},{5,53},{6,198},{7,55},{8,200... | collective-permute-start | bytes 983048 | tf_op jit(solution)/shard_map/ppermute | solution.py:63
  71.1 1.9 %shard_map.60.act = bf16[2,256,640]{2,1,0:T(8,128)(2,1)S(1)} custom-call(bf16[2,128,1280]{2,1,0:T(8,128)(2,1)S(1)} %collective-permute-done.4.sa, bf16[2,128,1280]{2,1,0:T(8,128)(2,1)S(1)} %collective-permute-done.6.sb, bf16[2,1280,1280]{2,1,0:T(8,128)(2,1)S(1)} %shard_map.59.gu_ref), custom_call_target="tpu_custom_call" | custom-call | tf_op jit(solution)/shard_map/pallas_call | solution.py:288
  73.1 3.0 %shard_map.62 = (bf16[2,128,1280]{2,1,0:T(8,128)(2,1)S(1)}, bf16[2,128,1280]{2,1,0:T(8,128)(2,1)S(1)}, bf16[2,640,1280]{2,1,0:T(8,128)(2,1)S(1)}) custom-call(bf16[2,256,640]{2,1,0:T(8,128)(2,1)S(1)} %shard_map.60.act, bf16[8,160,1280]{2,1,0:T(8,128)(2,1)} %wd.1, bf16[1,2,160,1280]{3,2,1,0:T(8,128)(2,1)S(1)} %collective-permute-done.8.d1, ...), custom_call_target="tpu_custom_call" | custom-call | flops 2520000000 | bytes 9000000 | tf_op jit(solution)/shard_map/pallas_call | solution.py:320
  76.1 2.6 %collective-permute-start.11 = (bf16[2,128,1280]{2,1,0:T(8,128)(2,1)S(1)}, bf16[2,128,1280]{2,1,0:T(8,128)(2,1)S(1)}, u32[]{:S(2)}, u32[]{:S(2)}) collective-permute-start(bf16[2,128,1280]{2,1,0:T(8,128)(2,1)S(1)} %get-tuple-element.54), channel_id=1, source_target_pairs={{0,192},{1,49},{2,194},{3,51},{4,196},{5,53},{6,198},{7,55},{8,200... | collective-permute-start | bytes 1966088 | tf_op jit(solution)/shard_map/ppermute | solution.py:63
  79.5 3.4 %shard_map.63 = (bf16[2,128,1280]{2,1,0:T(8,128)(2,1)S(1)}, bf16[2,128,1280]{2,1,0:T(8,128)(2,1)S(1)}) custom-call(bf16[2,64,1280]{2,1,0:T(8,128)(2,1)S(1)} %collective-permute-done.5.far_low, bf16[2,64,1280]{2,1,0:T(8,128)(2,1)S(1)} %collective-permute-done.7.far_high, bf16[2,128,1280]{2,1,0:T(8,128)(2,1)S(1)} %shard_map.58.own, ...), custom_call_target="tpu_custom_call" | custom-call | flops 1260000000 | bytes 2000000 | tf_op jit(solution)/shard_map/pallas_call | solution.py:255
  83.9 9.3 %collective-permute-done.11.b = bf16[2,128,1280]{2,1,0:T(8,128)(2,1)S(1)} collective-permute-done((bf16[2,128,1280]{2,1,0:T(8,128)(2,1)S(1)}, bf16[2,128,1280]{2,1,0:T(8,128)(2,1)S(1)}, u32[]{:S(2)}, u32[]{:S(2)}) %collective-permute-start.11) | collective-permute-done | bytes 655392 | tf_op jit(solution)/shard_map/ppermute | solution.py:63
  93.2 3.4 %collective-permute-done.12.c = bf16[2,128,1280]{2,1,0:T(8,128)(2,1)S(1)} collective-permute-done((bf16[2,128,1280]{2,1,0:T(8,128)(2,1)S(1)}, bf16[2,128,1280]{2,1,0:T(8,128)(2,1)S(1)}, u32[]{:S(2)}, u32[]{:S(2)}) %collective-permute-start.12) | collective-permute-done | bytes 655392 | tf_op jit(solution)/shard_map/ppermute | solution.py:63
  97.2 26.6 %all_to_all.23 = bf16[32,8,1280]{2,1,0:T(8,128)(2,1)S(1)} all-to-all(bf16[32,8,1280]{2,1,0:T(8,128)(2,1)S(1)} %bitcast.7), channel_id=1, replica_groups={{0,2,4,6,8,10,12,14,16,18,20,22,24,26,28,30,32,34,36,38,40,42,44,46,48,..., dimensions={0} | all-to-all | bytes 1310720 | tf_op jit(solution)/shard_map/all_to_all | solution.py:53
  124.2 5.5 %collective-permute-start.14 = (bf16[128,1280]{1,0:T(8,128)(2,1)S(1)}, bf16[128,1280]{1,0:T(8,128)(2,1)S(1)}, u32[]{:S(2)}, u32[]{:S(2)}) collective-permute-start(bf16[128,1280]{1,0:T(8,128)(2,1)S(1)} %get-tuple-element.62), channel_id=1, source_target_pairs={{0,1},{1,0},{2,3},{3,2},{4,5},{5,4},{6,7},{7,6},{8,9},{9,8},{10,11... | collective-permute-start | bytes 983048 | tf_op jit(solution)/shard_map/ppermute | solution.py:59
  131.0 1.6 %convolution_convert_fusion = bf16[512,1280]{1,0:T(8,128)(2,1)} fusion(bf16[512,256]{1,0:T(8,128)(2,1)S(1)} %bitcast.10, bf16[128,1280]{1,0:T(8,128)(2,1)S(1)} %collective-permute-done.14, bf16[128,1280]{1,0:T(8,128)(2,1)S(1)} %get-tuple-element.61), kind=kOutput, calls=%fused_computation | convolution fusion | flops 337510400 | bytes 2228224 | tf_op jit(solution)/shard_map/dot_general | solution.py:356
  (28 shorter events, 8.8 us)
Async XLA Ops:
  0.0 10.8 %copy-start = (bf16[2,256,1280]{2,1,0:T(8,128)(2,1)S(1)}, bf16[2,256,1280]{2,1,0:T(8,128)(2,1)}, u32[]{:S(2)}) copy-start(bf16[2,256,1280]{2,1,0:T(8,128)(2,1)} %tok_ref) | copy-start | bytes 3932164
  0.0 10.8 %copy-start.1 = (f32[1280,128]{1,0:T(8,128)S(1)}, f32[1280,128]{1,0:T(8,128)}, u32[]{:S(2)}) copy-start(f32[1280,128]{1,0:T(8,128)} %router_ref) | copy-start | bytes 1966084
  4.3 29.5 %collective-permute-start.1 = (bf16[2,2,160,1280]{3,2,1,0:T(8,128)(2,1)}, bf16[2,2,160,1280]{3,2,1,0:T(8,128)(2,1)S(1)}, u32[]{:S(2)}, u32[]{:S(2)}) collective-permute-start(bf16[2,2,160,1280]{3,2,1,0:T(8,128)(2,1)} %get-tuple-element.42), channel_id=1, source_target_pairs={{0,32},{1,129},{2,34},{3,131},{4,36},{5,133},{6,38},{7,135},{8,40}... | collective-permute-start | bytes 4915208 | tf_op jit(solution)/shard_map/ppermute | solution.py:63
  8.1 40.4 %collective-permute-start.2 = (bf16[2,2,160,1280]{3,2,1,0:T(8,128)(2,1)}, bf16[2,2,160,1280]{3,2,1,0:T(8,128)(2,1)}, u32[]{:S(2)}, u32[]{:S(2)}) collective-permute-start(bf16[2,2,160,1280]{3,2,1,0:T(8,128)(2,1)} %get-tuple-element.43), channel_id=1, source_target_pairs={{0,16},{1,65},{2,18},{3,67},{4,20},{5,69},{6,22},{7,71},{8,24},{9,... | collective-permute-start | bytes 4915208 | tf_op jit(solution)/shard_map/ppermute | solution.py:63
  8.5 40.0 %collective-permute-start.3 = (bf16[2,2,160,1280]{3,2,1,0:T(8,128)(2,1)}, bf16[2,2,160,1280]{3,2,1,0:T(8,128)(2,1)}, u32[]{:S(2)}, u32[]{:S(2)}) collective-permute-start(bf16[2,2,160,1280]{3,2,1,0:T(8,128)(2,1)} %get-tuple-element.44), channel_id=1, source_target_pairs={{0,48},{1,193},{2,50},{3,195},{4,52},{5,197},{6,54},{7,199},{8,56}... | collective-permute-start | bytes 4915208 | tf_op jit(solution)/shard_map/ppermute | solution.py:63
  13.2 2.7 %collective-permute-start = (bf16[128,1280]{1,0:T(8,128)(2,1)S(1)}, bf16[128,1280]{1,0:T(8,128)(2,1)S(1)}, u32[]{:S(2)}, u32[]{:S(2)}) collective-permute-start(bf16[128,1280]{1,0:T(8,128)(2,1)S(1)} %get-tuple-element.41), channel_id=1, source_target_pairs={{0,1},{1,0},{2,3},{3,2},{4,5},{5,4},{6,7},{7,6},{8,9},{9,8},{10,11... | collective-permute-start | bytes 983048 | tf_op jit(solution)/shard_map/ppermute | solution.py:59
  17.1 31.4 %all-to-all-start = ((bf16[32,8,1280]{2,1,0:T(8,128)(2,1)}), bf16[32,8,1280]{2,1,0:T(8,128)(2,1)S(1)}, u32[]{:S(2)}, u32[]{:S(2)}) async-start(bf16[32,8,1280]{2,1,0:T(8,128)(2,1)} %bitcast.1), calls=%async_computation | async-start | bytes 1310720 | tf_op jit(solution)/shard_map/all_to_all | solution.py:53
  31.0 42.0 %collective-permute-start.8 = (bf16[1,2,160,1280]{3,2,1,0:T(8,128)(2,1)}, bf16[1,2,160,1280]{3,2,1,0:T(8,128)(2,1)S(1)}, u32[]{:S(2)}, u32[]{:S(2)}) collective-permute-start(bf16[1,2,160,1280]{3,2,1,0:T(8,128)(2,1)} %get-tuple-element.51), channel_id=1, source_target_pairs={{0,16},{1,65},{2,18},{3,67},{4,20},{5,69},{6,22},{7,71},{8,24},{9,... | collective-permute-start | bytes 2457608 | tf_op jit(solution)/shard_map/ppermute | solution.py:63
  32.3 40.7 %collective-permute-start.9 = (bf16[1,2,160,1280]{3,2,1,0:T(8,128)(2,1)}, bf16[1,2,160,1280]{3,2,1,0:T(8,128)(2,1)}, u32[]{:S(2)}, u32[]{:S(2)}) collective-permute-start(bf16[1,2,160,1280]{3,2,1,0:T(8,128)(2,1)} %get-tuple-element.52), channel_id=1, source_target_pairs={{0,48},{1,193},{2,50},{3,195},{4,52},{5,197},{6,54},{7,199},{8,56}... | collective-permute-start | bytes 2457608 | tf_op jit(solution)/shard_map/ppermute | solution.py:63
  33.8 39.3 %collective-permute-start.10 = (bf16[1,2,160,1280]{3,2,1,0:T(8,128)(2,1)}, bf16[1,2,160,1280]{3,2,1,0:T(8,128)(2,1)}, u32[]{:S(2)}, u32[]{:S(2)}) collective-permute-start(bf16[1,2,160,1280]{3,2,1,0:T(8,128)(2,1)} %get-tuple-element.53), channel_id=1, source_target_pairs={{0,32},{1,129},{2,34},{3,131},{4,36},{5,133},{6,38},{7,135},{8,40}... | collective-permute-start | bytes 2457608 | tf_op jit(solution)/shard_map/ppermute | solution.py:63
  48.9 19.1 %collective-permute-start.4 = (bf16[2,128,1280]{2,1,0:T(8,128)(2,1)S(1)}, bf16[2,128,1280]{2,1,0:T(8,128)(2,1)S(1)}, u32[]{:S(2)}, u32[]{:S(2)}) collective-permute-start(bf16[2,128,1280]{2,1,0:T(8,128)(2,1)S(1)} %shard_map.58.own), channel_id=1, source_target_pairs={{0,64},{1,17},{2,66},{3,19},{4,68},{5,21},{6,70},{7,23},{8,72},{9,... | collective-permute-start | bytes 1966088 | tf_op jit(solution)/shard_map/ppermute | solution.py:63
  50.2 17.9 %collective-permute-start.6 = (bf16[2,128,1280]{2,1,0:T(8,128)(2,1)S(1)}, bf16[2,128,1280]{2,1,0:T(8,128)(2,1)S(1)}, u32[]{:S(2)}, u32[]{:S(2)}) collective-permute-start(bf16[2,128,1280]{2,1,0:T(8,128)(2,1)S(1)} %shard_map.58.own), channel_id=1, source_target_pairs={{0,192},{1,49},{2,194},{3,51},{4,196},{5,53},{6,198},{7,55},{8,200... | collective-permute-start | bytes 1966088 | tf_op jit(solution)/shard_map/ppermute | solution.py:63
  68.1 11.4 %collective-permute-start.5 = (bf16[2,64,1280]{2,1,0:T(8,128)(2,1)S(1)}, bf16[2,64,1280]{2,1,0:T(8,128)(2,1)S(1)}, u32[]{:S(2)}, u32[]{:S(2)}) collective-permute-start(bf16[2,64,1280]{2,1,0:T(8,128)(2,1)S(1)} %slice.6), channel_id=1, source_target_pairs={{0,64},{1,17},{2,66},{3,19},{4,68},{5,21},{6,70},{7,23},{8,72},{9,... | collective-permute-start | bytes 983048 | tf_op jit(solution)/shard_map/ppermute | solution.py:63
  68.2 11.3 %collective-permute-start.7 = (bf16[2,64,1280]{2,1,0:T(8,128)(2,1)S(1)}, bf16[2,64,1280]{2,1,0:T(8,128)(2,1)S(1)}, u32[]{:S(2)}, u32[]{:S(2)}) collective-permute-start(bf16[2,64,1280]{2,1,0:T(8,128)(2,1)S(1)} %slice.8), channel_id=1, source_target_pairs={{0,192},{1,49},{2,194},{3,51},{4,196},{5,53},{6,198},{7,55},{8,200... | collective-permute-start | bytes 983048 | tf_op jit(solution)/shard_map/ppermute | solution.py:63
  76.1 17.1 %collective-permute-start.11 = (bf16[2,128,1280]{2,1,0:T(8,128)(2,1)S(1)}, bf16[2,128,1280]{2,1,0:T(8,128)(2,1)S(1)}, u32[]{:S(2)}, u32[]{:S(2)}) collective-permute-start(bf16[2,128,1280]{2,1,0:T(8,128)(2,1)S(1)} %get-tuple-element.54), channel_id=1, source_target_pairs={{0,192},{1,49},{2,194},{3,51},{4,196},{5,53},{6,198},{7,55},{8,200... | collective-permute-start | bytes 1966088 | tf_op jit(solution)/shard_map/ppermute | solution.py:63
  78.6 18.0 %collective-permute-start.12 = (bf16[2,128,1280]{2,1,0:T(8,128)(2,1)S(1)}, bf16[2,128,1280]{2,1,0:T(8,128)(2,1)S(1)}, u32[]{:S(2)}, u32[]{:S(2)}) collective-permute-start(bf16[2,128,1280]{2,1,0:T(8,128)(2,1)S(1)} %get-tuple-element.55), channel_id=1, source_target_pairs={{0,64},{1,17},{2,66},{3,19},{4,68},{5,21},{6,70},{7,23},{8,72},{9,... | collective-permute-start | bytes 1966088 | tf_op jit(solution)/shard_map/ppermute | solution.py:63
  82.9 13.9 %collective-permute-start.13 = (bf16[2,128,1280]{2,1,0:T(8,128)(2,1)S(1)}, bf16[2,128,1280]{2,1,0:T(8,128)(2,1)S(1)}, u32[]{:S(2)}, u32[]{:S(2)}) collective-permute-start(bf16[2,128,1280]{2,1,0:T(8,128)(2,1)S(1)} %get-tuple-element.60), channel_id=1, source_target_pairs={{0,128},{1,33},{2,130},{3,35},{4,132},{5,37},{6,134},{7,39},{8,136... | collective-permute-start | bytes 1966088 | tf_op jit(solution)/shard_map/ppermute | solution.py:63
  124.2 6.8 %collective-permute-start.14 = (bf16[128,1280]{1,0:T(8,128)(2,1)S(1)}, bf16[128,1280]{1,0:T(8,128)(2,1)S(1)}, u32[]{:S(2)}, u32[]{:S(2)}) collective-permute-start(bf16[128,1280]{1,0:T(8,128)(2,1)S(1)} %get-tuple-element.62), channel_id=1, source_target_pairs={{0,1},{1,0},{2,3},{3,2},{4,5},{5,4},{6,7},{7,6},{8,9},{9,8},{10,11... | collective-permute-start | bytes 983048 | tf_op jit(solution)/shard_map/ppermute | solution.py:59
